TPU v7x, 128 devices: a whole 4x4x4 slice. The times are simulated.
128 devices in a mesh: row: 16 (over y, x_hi, core), col: 8 (over z, x_lo).
Axes of the slice: x: 4 (x_hi: 2, x_lo: 2; x = x_hi * 2 + x_lo), y: 4, z: 4, core: 2. Of those that a mesh axis runs over, the one named last changes fastest.
Arguments:
- estimate: bfloat16 [2, 2048, 2048], P(None, 'row', 'col'), may hold values from -6 to 6
- dirty_image: bfloat16 [2, 2048, 2048], P(None, 'row', 'col'), may hold values from -6 to 6
- psf_spectra: float32 [3, 2048, 16, 128], P(None, ('row', 'col')), may hold values from -1 to 1
- w_first: bfloat16 [32, 4, 3, 3], replicated, may hold values from -1 to 1
- b_first: float32 [32], replicated, may hold values from -1 to 1
- w_second: bfloat16 [2, 32, 3, 3], replicated, may hold values from -0.375 to 0.375
- cotangent: bfloat16 [2, 2048, 2048], P(None, 'row', 'col'), may hold values from -36 to 36
Outputs:
- grad_image: float32 [2, 2048, 2048], P(None, 'row', 'col')
- grad_first: float32 [32, 4, 3, 3], replicated
- grad_first_bias: float32 [32], replicated
- grad_second: float32 [2, 32, 3, 3], replicated
- grad_second_bias: float32 [2], replicated
All inputs are finite; a program needn't handle non-finite values.
Results may differ from a plain program's by a relative error of at most 0.01.
Values may be sent and summed in bfloat16 or wider, within the bound.
No kernel may reach another device: no remote copies, remote signals or barrier semaphores. Data moves between devices by JAX's collectives and lax.ppermute only.
A program may use at most 192 MiB of HBM per device.

v0:
```python
import math

import jax
import jax.numpy as jnp
from jax import lax
from jax.sharding import PartitionSpec as P

IMAGE = 2048


def with_halo(cells, sides, width):
    for axis, dim in sides:
        count = lax.axis_size(axis)
        ends = count - 1
        head = lax.slice_in_dim(cells, 0, width, axis=dim)
        tail = lax.slice_in_dim(cells, cells.shape[dim] - width, cells.shape[dim], axis=dim)
        cells = jnp.concatenate(
            [
                lax.ppermute(tail, axis, [(i, (i + 1) % count) for i in range(ends)]),
                cells,
                lax.ppermute(head, axis, [((i + 1) % count, i) for i in range(ends)]),
            ],
            axis=dim,
        )
    return cells


def product(pattern, left_op, right_op):
    return jnp.einsum(
        pattern, left_op, right_op, precision=lax.Precision.HIGH, preferred_element_type=jnp.float32
    )


def complex_product(pattern, table_re, table_im, values_re, values_im):
    real_part = product(pattern, table_re, values_re) - product(pattern, table_im, values_im)
    imag_part = product(pattern, table_re, values_im) + product(pattern, table_im, values_re)
    return (real_part, imag_part)


def circle(row_index, col_index, period, direction):
    angle_index = row_index[:, None] * col_index[None, :] % period
    phase_value = angle_index.astype(jnp.float32) * (direction * 2.0 * math.pi / period)
    return (jnp.cos(phase_value), jnp.sin(phase_value))


def twiddle(values_re, values_im, short_len, long_len, period, direction):
    turn_re, turn_im = circle(
        jnp.arange(short_len, dtype=jnp.int32),
        jnp.arange(long_len, dtype=jnp.int32),
        period,
        direction,
    )
    return (values_re * turn_re - values_im * turn_im, values_re * turn_im + values_im * turn_re)


def forward_columns(rows_in, devices):
    channels, height, length = rows_in.shape
    short_len = length // devices
    blocks = rows_in.reshape(channels, height, short_len, devices)
    short_idx = jnp.arange(short_len, dtype=jnp.int32)
    long_idx = jnp.arange(devices, dtype=jnp.int32)
    first_re, first_im = circle(short_idx, short_idx, short_len, -1.0)
    section_re = product("kn,crnb->crkb", first_re, blocks)
    section_im = product("kn,crnb->crkb", first_im, blocks)
    section_re, section_im = twiddle(section_re, section_im, short_len, devices, length, -1.0)
    last_re, last_im = circle(long_idx, long_idx, devices, -1.0)
    return complex_product("jb,crkb->cjkr", last_re, last_im, section_re, section_im)


def forward_rows(values_re, values_im, devices):
    channels, width_loc, length = values_re.shape
    short_len = length // devices
    blocks_re = values_re.reshape(channels, width_loc, short_len, devices)
    blocks_im = values_im.reshape(channels, width_loc, short_len, devices)
    short_idx = jnp.arange(short_len, dtype=jnp.int32)
    long_idx = jnp.arange(devices, dtype=jnp.int32)
    first_re, first_im = circle(short_idx, short_idx, short_len, -1.0)
    section_re, section_im = complex_product(
        "kn,cqnb->cqkb", first_re, first_im, blocks_re, blocks_im
    )
    section_re, section_im = twiddle(section_re, section_im, short_len, devices, length, -1.0)
    last_re, last_im = circle(long_idx, long_idx, devices, -1.0)
    return complex_product("jb,cqkb->cqkj", last_re, last_im, section_re, section_im)


def inverse_rows(values_re, values_im):
    channels, width_loc, short_len, devices = values_re.shape
    length = short_len * devices
    short_idx = jnp.arange(short_len, dtype=jnp.int32)
    long_idx = jnp.arange(devices, dtype=jnp.int32)
    last_re, last_im = circle(long_idx, long_idx, devices, 1.0)
    section_re, section_im = complex_product(
        "nj,cqkj->cqkn", last_re, last_im, values_re, values_im
    )
    section_re, section_im = twiddle(section_re, section_im, short_len, devices, length, 1.0)
    first_re, first_im = circle(short_idx, short_idx, short_len, 1.0)
    out_re, out_im = complex_product("mk,cqkn->cqmn", first_re, first_im, section_re, section_im)
    return (
        out_re.reshape(channels, width_loc, length) / length,
        out_im.reshape(channels, width_loc, length) / length,
    )


def inverse_columns(values_re, values_im, slot_order):
    channels, devices, short_len, height = values_re.shape
    length = short_len * devices
    short_idx = jnp.arange(short_len, dtype=jnp.int32)
    long_idx = jnp.arange(devices, dtype=jnp.int32)
    table_re, table_im = circle(long_idx, slot_order, devices, 1.0)
    section_re, section_im = complex_product(
        "nj,cjkr->crkn", table_re, table_im, values_re, values_im
    )
    section_re, section_im = twiddle(section_re, section_im, short_len, devices, length, 1.0)
    first_re, first_im = circle(short_idx, short_idx, short_len, 1.0)
    real_part = product("mk,crkn->crmn", first_re, section_re) - product(
        "mk,crkn->crmn", first_im, section_im
    )
    return real_part.reshape(channels, height, length) / length


def blur(tile_data, spectra):
    row_count = lax.axis_size("row")
    col_count = lax.axis_size("col")
    devices = row_count * col_count
    full_rows = lax.all_to_all(tile_data, "col", split_axis=1, concat_axis=2, tiled=True)
    channels, height, length = full_rows.shape
    short_len = length // devices
    spec_re, spec_im = forward_columns(full_rows, devices)
    packed = jnp.stack([spec_re, spec_im]).astype(jnp.bfloat16)
    arrived = lax.all_to_all(packed, ("row", "col"), split_axis=2, concat_axis=4, tiled=True)
    slab_data = arrived.reshape(2, channels, short_len, length)
    full_re, full_im = forward_rows(slab_data[0], slab_data[1], devices)
    mixed_re = []
    mixed_im = []
    for target in range(channels):
        total_re = spectra[target] * full_re[0]
        total_im = spectra[target] * full_im[0]
        total_re = total_re + spectra[target + 1] * full_re[1]
        total_im = total_im + spectra[target + 1] * full_im[1]
        mixed_re.append(total_re)
        mixed_im.append(total_im)
    back_re, back_im = inverse_rows(jnp.stack(mixed_re), jnp.stack(mixed_im))
    packed_back = jnp.stack([back_re, back_im]).astype(jnp.bfloat16)[:, :, None]
    returned = lax.all_to_all(packed_back, ("row", "col"), split_axis=4, concat_axis=2, tiled=True)
    slot_order = jnp.arange(devices, dtype=jnp.int32)
    image_part = inverse_columns(returned[0], returned[1], slot_order).astype(jnp.bfloat16)
    return lax.all_to_all(image_part, "col", split_axis=2, concat_axis=1, tiled=True)


def activation_slope(preact):
    gate_value = jax.nn.sigmoid(preact)
    return gate_value * (1.0 + preact * (1.0 - gate_value))


def conv_valid(inputs, kernel):
    return lax.conv_general_dilated(
        inputs[None],
        kernel,
        (1, 1),
        "VALID",
        dimension_numbers=("NCHW", "OIHW", "NCHW"),
        preferred_element_type=jnp.float32,
    )[0]


def kernel_grad(inputs, cot_part):
    return lax.conv_general_dilated(
        inputs[:, None],
        cot_part[:, None],
        (1, 1),
        "VALID",
        dimension_numbers=("NCHW", "OIHW", "NCHW"),
        preferred_element_type=jnp.float32,
    )


def accumulate(totals, inputs_mid, cot_mid, preact_mid, grad_mid):
    hidden = jax.nn.silu(preact_mid).astype(jnp.bfloat16)
    return (
        totals[0] + kernel_grad(inputs_mid, grad_mid).transpose(1, 0, 2, 3),
        totals[1] + jnp.sum(grad_mid.astype(jnp.float32), axis=(1, 2)),
        totals[2] + jnp.flip(kernel_grad(cot_mid, hidden), (2, 3)),
    )


def network(features, cotangent, w_first, b_first, w_second):
    channels = features.shape[0]
    hidden_count = w_first.shape[0]
    term_count = cotangent.shape[0]
    height = features.shape[1]
    width_loc = features.shape[2]
    rim_width = 1
    padded = with_halo(
        jnp.concatenate([features, cotangent], 0), (("row", 1), ("col", 2)), rim_width
    )
    flip_first = jnp.flip(w_first, (2, 3)).transpose(1, 0, 2, 3)
    flip_second = jnp.flip(w_second, (2, 3)).transpose(1, 0, 2, 3)
    band_count = height // height
    start_totals = (
        jnp.zeros((hidden_count, channels, 3, 3), jnp.float32),
        jnp.zeros((hidden_count,), jnp.float32),
        jnp.zeros((term_count, hidden_count, 3, 3), jnp.float32),
    )
    start_grad = jnp.zeros((channels, height, width_loc), jnp.float32)

    def first_pass(band_index, state_pair):
        totals, grad_all = state_pair
        offset = band_index * height
        preact = conv_valid(padded[:channels], w_first) + b_first[:, None, None]
        grad_pre = (conv_valid(padded[channels:], flip_second) * activation_slope(preact)).astype(
            jnp.bfloat16
        )
        totals = accumulate(totals, padded[:channels], padded[channels:], preact, grad_pre)
        return (totals, lax.dynamic_update_slice_in_dim(grad_all, grad_pre, offset, 1))

    totals, grad_all = lax.fori_loop(
        0,
        band_count,
        first_pass,
        (start_totals, jnp.zeros((hidden_count, height, width_loc), jnp.bfloat16)),
    )
    grad_padded = with_halo(grad_all, (("row", 1), ("col", 2)), 1)

    def second_pass(band_index, result):
        offset = band_index * height
        return lax.dynamic_update_slice_in_dim(
            result, conv_valid(grad_padded, flip_first), offset, 1
        )

    feature_grad = lax.fori_loop(0, band_count, second_pass, start_grad)
    return (feature_grad, totals)


def shards(estimate, dirty_image, psf_spectra, w_first, b_first, w_second, cotangent):
    term_count = estimate.shape[0]
    model_blur = blur(estimate, psf_spectra)
    residual = (dirty_image.astype(jnp.float32) - model_blur.astype(jnp.float32)).astype(
        jnp.bfloat16
    )
    features = jnp.concatenate([estimate, residual], 0)
    feature_grad, totals = network(features, cotangent, w_first, b_first, w_second)
    residual_grad = feature_grad[term_count:].astype(jnp.bfloat16)
    blurred_grad = blur(residual_grad, psf_spectra)
    grad_image = (
        cotangent.astype(jnp.float32) + feature_grad[:term_count] - blurred_grad.astype(jnp.float32)
    )
    first_sum, bias_sum, second_sum = totals
    cot_sum = jnp.sum(cotangent.astype(jnp.float32), axis=(1, 2))
    summed = lax.psum((first_sum, bias_sum, second_sum, cot_sum), ("row", "col"))
    scaling = 1.0 / IMAGE
    return (
        grad_image,
        summed[0] * scaling,
        summed[1] * scaling,
        summed[2] * scaling,
        summed[3] * scaling,
    )


def solution(mesh):
    return jax.shard_map(
        shards,
        mesh=mesh,
        in_specs=(
            P(None, "row", "col"),
            P(None, "row", "col"),
            P(None, ("row", "col"), None, None),
            P(),
            P(),
            P(),
            P(None, "row", "col"),
        ),
        out_specs=(P(None, "row", "col"), P(), P(), P(), P()),
        check_vma=False,
    )
```

profile of v0, /device:TPU:0, one launch (start us, length us, event | category | flops | bytes accessed | tf_op | source)
XLA Modules:
  0.0 935.3 jit_solution(13126283702640362338)
XLA Ops:
  0.6 1.7 copy.305
  2.3 6.3 all-to-all-start
  8.7 6.6 all-to-all-done
  18.1 3.0 copy.307
  21.1 3.0 reshape.343
  24.1 8.4 all-to-all-start.1
  32.5 10.9 %all-to-all-done.1 = bf16[128,2,512]{2,1,0:T(2,128)(2,1)S(1)} async-done(((bf16[128,2,512]{2,1,0:T(2,128)(2,1)}), bf16[128,2,512]{2,1,0:T(2,128)(2,1)S(1)}, u32[]{:S(2)}, u32[]{:S(2)}) %all-to-all-start.1) | async-done | bytes 262176 | tf_op jit(solution)/shard_map/all_to_all | solution.py:130
  45.7 2.0 copy.309
  48.6 2.0 copy.308
  59.7 4.7 fusion.412
  64.3 2.5 reshape.345
  66.9 15.1 %all_to_all.108 = bf16[128,2,512]{2,1,0:T(2,128)(2,1)S(1)} all-to-all(bf16[128,2,512]{2,1,0:T(2,128)(2,1)S(1)} %reshape.345), channel_id=1, replica_groups=mesh['row'=16,'col'=8] {'row','col'}, dimensions={0} | all-to-all | bytes 524288 | tf_op jit(solution)/shard_map/all_to_all | solution.py:144
  83.4 3.2 copy.313
  90.9 9.1 all_to_all.109
  102.7 3.0 collective-permute-start
  108.1 4.6 collective-permute-start.2
  112.7 3.5 collective-permute-done.3
  116.2 1.7 collective-permute-done.2
  118.9 5.9 copy.324
  126.0 5.0 fusion.443
  131.0 17.0 %convolution_select_fusion = f32[128,8,33,32]{3,1,2,0:T(8,128)} fusion(bf16[32,4,3,3]{0,1,3,2:T(4,128)(2,1)S(1)} %copy-done, pred[8,33]{0,1:T(8,128)(4,1)S(1)} %copy-done.23, bf16[4,130,8,35]{2,0,3,1:T(4,128)(2,1)S(1)} %fusion.443), kind=kOutput, calls=%fused_computation.11 | convolution fusion | flops 78938112 | bytes 4619144 | tf_op jit(solution)/shard_map/while/body/eval_jaxpr/conv_general_dilated | solution.py:156
  148.0 14.6 %copy.325 = f32[128,8,33,32]{0,3,2,1:T(8,128)} copy(f32[128,8,33,32]{3,1,2,0:T(8,128)} %convolution_select_fusion) | data formatting | bytes 8650752 | tf_op jit(solution)/shard_map/while/body/eval_jaxpr/conv_general_dilated | solution.py:156
  163.2 4.4 copy.320
  168.8 24.9 %convolution_select_fusion.1 = f32[128,8,33,32]{3,1,2,0:T(8,128)} fusion(bf16[2,32,3,3]{1,0,3,2:T(2,128)(2,1)S(1)} %copy-done.22, pred[8,33]{0,1:T(8,128)(4,1)S(1)} %copy-done.23, bf16[2,130,1,7,2]{3,0,4,1,2:T(2,128)(2,1)S(1)} %slice.182, bf16[2,130,1,8,33]{3,0,4,1,2:T(2,128)(2,1)} %copy.320), kind=kOutput, calls=%fused_computation.12 | convolution fusion | flops 40446528 | bytes 4471352 | tf_op jit(solution)/shard_map/while/body/eval_jaxpr/conv_general_dilated | solution.py:156
  193.7 14.6 %copy.321 = f32[128,8,33,32]{0,3,2,1:T(8,128)} copy(f32[128,8,33,32]{3,1,2,0:T(8,128)} %convolution_select_fusion.1) | data formatting | bytes 8650752 | tf_op jit(solution)/shard_map/while/body/eval_jaxpr/conv_general_dilated | solution.py:156
  208.3 5.1 convert_reduce_fusion
  213.5 2.9 fusion.408
  216.4 3.2 copy.327
  220.9 3.3 copy.326
  224.2 3.0 collective-permute-start.4
  227.2 3.9 copy.329
  231.1 3.9 copy.328
  237.4 5.0 collective-permute-start.6
  243.9 2.8 maximum_bitcast_fusion
  246.7 3.3 pad.4
  250.0 11.8 %copy.331 = bf16[32,130,1,8,33]{0,3,4,1,2:T(8,128)(2,1)} copy(bf16[32,130,1,8,33]{1,0,4,3,2:T(8,128)(2,1)} %bitcast.387) | data formatting | bytes 4392960 | tf_op jit(solution)/shard_map/while/body/eval_jaxpr/conv_general_dilated | solution.py:156
  263.1 192.2 %fusion.16 = f32[128,8,33,4]{1,3,2,0:T(4,128)S(1)} fusion(bf16[32,4,3,3]{0,1,3,2:T(4,128)(2,1)S(1)} %copy-done, bf16[32,130,1,7,2]{0,3,4,1,2:T(8,128)(2,1)S(1)} %slice.188, bf16[32,130,1,8,33]{0,3,4,1,2:T(8,128)(2,1)} %copy.331, pred[8,33]{0,1:T(8,128)(4,1)S(1)} %copy-done.23), kind=kOutput, calls=%fused_computation.19 | convolution fusion | flops 84980736 | bytes 2856200 | tf_op jit(solution)/shard_map/while/body/eval_jaxpr/conv_general_dilated | solution.py:156
  455.3 3.4 copy-done.5
  458.7 2.2 slice.255
  460.9 1.8 copy.333
  463.6 8.9 all-to-all-start.4
  473.3 6.3 all-to-all-done.4
  482.4 3.0 copy.337
  485.3 3.0 reshape.349
  488.3 6.8 all-to-all-start.5
  495.1 5.6 multiply_convert_fusion
  501.9 31.3 %copy.350 = bf16[4,1,130,258]{0,1,3,2:T(2,128)(2,1)} copy(bf16[4,1,130,258]{3,2,0,1:T(8,128)(2,1)} %fusion.438) | data formatting | bytes 536640 | tf_op jit(solution)/shard_map/while/body/eval_jaxpr/broadcast_in_dim | solution.py:168
  533.2 25.6 %copy.351 = bf16[32,1,128,256]{0,1,3,2:T(2,128)(2,1)} copy(bf16[32,1,128,256]{2,0,3,1:T(8,128)(2,1)S(1)} %get-tuple-element.94) | data formatting | bytes 4194304 | tf_op jit(solution)/shard_map/while/body/eval_jaxpr/convert_element_type | solution.py:210
  561.0 2.0 copy.339
  564.0 2.0 copy.338
  575.0 5.1 fusion.411
  580.1 3.0 reshape.351
  583.1 10.4 %all-to-all-start.6 = ((bf16[128,2,512]{2,1,0:T(2,128)(2,1)}), bf16[128,2,512]{2,1,0:T(2,128)(2,1)}, u32[]{:S(2)}, u32[]{:S(2)}) async-start(bf16[128,2,512]{2,1,0:T(2,128)(2,1)} %reshape.351), calls=%async_computation.6 | async-start | bytes 524288 | tf_op jit(solution)/shard_map/all_to_all | solution.py:144
  593.5 92.1 %fusion.417 = f32[32,4,3,3]{0,1,3,2:T(4,128)S(1)} fusion(bf16[4,1,130,258]{0,1,3,2:T(2,128)(2,1)} %copy.350, bf16[32,1,128,256]{0,1,3,2:T(2,128)(2,1)} %copy.351), kind=kOutput, calls=%fused_computation.533 | convolution fusion | flops 75497472 | bytes 2370080 | tf_op jit(solution)/shard_map/while/body/eval_jaxpr/transpose | solution.py:180
  685.6 27.1 %copy.352 = bf16[2,1,130,258]{1,0,3,2:T(2,128)(2,1)} copy(bf16[2,1,130,258]{3,2,0,1:T(8,128)(2,1)S(1)} %bitcast.410) | data formatting | bytes 268320 | tf_op jit(solution)/shard_map/while/body/eval_jaxpr/broadcast_in_dim | solution.py:168
  712.7 25.6 %copy.353 = bf16[32,1,128,256]{0,1,3,2:T(2,128)(2,1)} copy(bf16[32,1,128,256]{2,0,3,1:T(8,128)(2,1)S(1)} %copy-done.4) | data formatting | bytes 4194304 | tf_op jit(solution)/shard_map/while/body/eval_jaxpr/convert_element_type | solution.py:178
  738.4 7.2 reshape.352
  745.6 3.4 copy.343
  752.2 1.7 reshape.353
  753.9 5.0 all-to-all-start.7
  758.9 91.3 %fusion.418 = f32[2,32,3,3]{1,0,3,2:T(2,128)S(1)} fusion(bf16[2,1,130,258]{1,0,3,2:T(2,128)(2,1)} %copy.352, bf16[32,1,128,256]{0,1,3,2:T(2,128)(2,1)} %copy.353), kind=kOutput, calls=%fused_computation.534 | convolution fusion | flops 37748736 | bytes 2233616 | tf_op jit(solution)/shard_map/while/body/eval_jaxpr/conv_general_dilated | solution.py:167
  850.3 7.0 slice.189
  857.2 5.4 copy.332
  865.6 67.3 %all-reduce = (f32[32,4,3,3]{0,1,3,2:T(4,128)S(1)}, f32[32]{0:T(128)S(1)}, f32[2,32,3,3]{1,0,3,2:T(2,128)S(1)}, f32[2]{0:T(128)S(1)}) all-reduce(f32[32,4,3,3]{0,1,3,2:T(4,128)S(1)} %fusion.417, f32[32]{0:T(128)S(1)} %copy-done.21, f32[2,32,3,3]{1,0,3,2:T(2,128)S(1)} %rev.9, ...), channel_id=1, replica_groups=mesh['row'=16,'col'=8] {'row','col'}, use_global_device_ids=true, to_apply=%region_0.1 | all-reduce | flops 1762 | bytes 14096 | tf_op jit(solution)/shard_map/psum | solution.py:249
  (178 shorter events, 61.8 us)
Async XLA Ops:
  0.6 130.3 %copy-start = (bf16[32,4,3,3]{0,1,3,2:T(4,128)(2,1)S(1)}, bf16[32,4,3,3]{0,1,3,2:T(4,128)(2,1)}, u32[]{:S(2)}) copy-start(bf16[32,4,3,3]{0,1,3,2:T(4,128)(2,1)} %param.10) | copy-start | bytes 6916
  2.3 13.0 %all-to-all-start = ((bf16[2,128,256]{2,0,1:T(2,128)(2,1)}), bf16[2,128,256]{2,0,1:T(2,128)(2,1)S(1)}, u32[]{:S(2)}, u32[]{:S(2)}) async-start(bf16[2,128,256]{2,0,1:T(2,128)(2,1)} %copy.305), calls=%async_computation | async-start | bytes 262144 | tf_op jit(solution)/shard_map/all_to_all | solution.py:125
  24.1 19.3 %all-to-all-start.1 = ((bf16[128,2,512]{2,1,0:T(2,128)(2,1)}), bf16[128,2,512]{2,1,0:T(2,128)(2,1)S(1)}, u32[]{:S(2)}, u32[]{:S(2)}) async-start(bf16[128,2,512]{2,1,0:T(2,128)(2,1)} %reshape.343), calls=%async_computation.1 | async-start | bytes 524288 | tf_op jit(solution)/shard_map/all_to_all | solution.py:130
  32.5 540.8 %copy-start.14 = (f32[16,128]{1,0:T(8,128)}, f32[16,128]{1,0:T(8,128)S(1)}, u32[]{:S(2)}) copy-start(f32[16,128]{1,0:T(8,128)S(1)} %get-tuple-element.125) | copy-start | bytes 24580
  32.5 540.8 %copy-start.16 = (f32[16,128]{1,0:T(8,128)}, f32[16,128]{1,0:T(8,128)S(1)}, u32[]{:S(2)}) copy-start(f32[16,128]{1,0:T(8,128)S(1)} %get-tuple-element.126) | copy-start | bytes 24580
  48.6 5.6 copy-start.12
  87.1 14.3 %copy-start.19 = (bf16[2,128,256]{2,1,0:T(8,128)(2,1)S(1)}, bf16[2,128,256]{2,1,0:T(8,128)(2,1)}, u32[]{:S(2)}) copy-start(bf16[2,128,256]{2,1,0:T(8,128)(2,1)} %param.8) | copy-start | bytes 393220
  87.6 13.8 %copy-start.6 = (bf16[2,128,256]{2,1,0:T(8,128)(2,1)S(1)}, bf16[2,128,256]{2,1,0:T(8,128)(2,1)}, u32[]{:S(2)}) copy-start(bf16[2,128,256]{2,1,0:T(8,128)(2,1)} %param.13) | copy-start | bytes 393220
  87.6 13.8 %copy-start.7 = (bf16[2,128,256]{2,1,0:T(8,128)(2,1)S(1)}, bf16[2,128,256]{2,1,0:T(8,128)(2,1)}, u32[]{:S(2)}) copy-start(bf16[2,128,256]{2,1,0:T(8,128)(2,1)} %param.7) | copy-start | bytes 393220
  101.4 4.3 collective-permute-start.1
  102.7 3.8 collective-permute-start
  106.8 9.4 %collective-permute-start.3 = (bf16[6,130,1]{2,1,0:T(8,128)(2,1)S(1)}, bf16[6,130,1]{2,1,0:T(8,128)(2,1)S(1)}, u32[]{:S(2)}, u32[]{:S(2)}) collective-permute-start(bf16[6,130,1]{2,1,0:T(8,128)(2,1)S(1)} %get-tuple-element.114), channel_id=1, source_target_pairs={{1,0},{2,1},{3,2},{4,3},{5,4},{6,5},{7,6},{9,8},{10,9},{11,10},{12... | collective-permute-start | bytes 4688 | tf_op jit(solution)/shard_map/ppermute | solution.py:21
  108.1 9.8 %collective-permute-start.2 = (bf16[6,130,1]{2,1,0:T(8,128)(2,1)S(1)}, bf16[6,130,1]{2,1,0:T(8,128)(2,1)S(1)}, u32[]{:S(2)}, u32[]{:S(2)}) collective-permute-start(bf16[6,130,1]{2,1,0:T(8,128)(2,1)S(1)} %get-tuple-element.113), channel_id=1, source_target_pairs={{0,1},{1,2},{2,3},{3,4},{4,5},{5,6},{6,7},{8,9},{9,10},{10,11},{11... | collective-permute-start | bytes 4688 | tf_op jit(solution)/shard_map/ppermute | solution.py:19
  117.9 44.6 %copy-start.10 = (bf16[6,130,1]{2,1,0:T(8,128)(2,1)}, bf16[6,130,1]{2,1,0:T(8,128)(2,1)S(1)}, u32[]{:S(2)}) copy-start(bf16[6,130,1]{2,1,0:T(8,128)(2,1)S(1)} %collective-permute-done.2) | copy-start | bytes 4684
  125.9 5.0 copy-start.23
  162.6 6.2 copy-start.22
  162.7 31.0 %copy-start.8 = (bf16[2,130,258]{2,1,0:T(8,128)(2,1)}, bf16[2,130,258]{2,1,0:T(8,128)(2,1)S(1)}, u32[]{:S(2)}) copy-start(bf16[2,130,258]{2,1,0:T(8,128)(2,1)S(1)} %pad_maximum_fusion.23) | copy-start | bytes 402484
  193.7 14.6 %copy-start.20 = (f32[32]{0:T(128)S(1)}, f32[32]{0:T(128)}, u32[]{:S(2)}) copy-start(f32[32]{0:T(128)} %param.11) | copy-start | bytes 388
  219.6 7.6 collective-permute-start.5
  224.2 7.0 collective-permute-start.4
  235.0 8.9 copy-start.2
  235.0 8.9 copy-start.3
  236.0 6.5 collective-permute-start.7
  237.4 6.5 collective-permute-start.6
  455.3 3.4 copy-start.5
  463.6 16.0 %all-to-all-start.4 = ((bf16[2,128,256]{2,0,1:T(2,128)(2,1)}), bf16[2,128,256]{2,0,1:T(2,128)(2,1)S(1)}, u32[]{:S(2)}, u32[]{:S(2)}) async-start(bf16[2,128,256]{2,0,1:T(2,128)(2,1)} %copy.334), calls=%async_computation.4 | async-start | bytes 262144 | tf_op jit(solution)/shard_map/all_to_all | solution.py:125
  488.3 70.5 %all-to-all-start.5 = ((bf16[128,2,512]{2,1,0:T(2,128)(2,1)}), bf16[128,2,512]{2,1,0:T(2,128)(2,1)S(1)}, u32[]{:S(2)}, u32[]{:S(2)}) async-start(bf16[128,2,512]{2,1,0:T(2,128)(2,1)} %reshape.349), calls=%async_computation.5 | async-start | bytes 524288 | tf_op jit(solution)/shard_map/all_to_all | solution.py:130
  495.1 5.7 copy-start.11
  564.0 5.6 copy-start.13
  583.1 155.3 %all-to-all-start.6 = ((bf16[128,2,512]{2,1,0:T(2,128)(2,1)}), bf16[128,2,512]{2,1,0:T(2,128)(2,1)}, u32[]{:S(2)}, u32[]{:S(2)}) async-start(bf16[128,2,512]{2,1,0:T(2,128)(2,1)} %reshape.351), calls=%async_computation.6 | async-start | bytes 524288 | tf_op jit(solution)/shard_map/all_to_all | solution.py:144
  593.5 92.1 %copy-start.9 = (bf16[2,130,258]{2,1,0:T(8,128)(2,1)S(1)}, bf16[2,130,258]{2,1,0:T(8,128)(2,1)}, u32[]{:S(2)}) copy-start(bf16[2,130,258]{2,1,0:T(8,128)(2,1)} %copy-done.8) | copy-start | bytes 402484
  685.6 27.2 %copy-start.4 = (bf16[32,1,128,256]{2,0,3,1:T(8,128)(2,1)S(1)}, bf16[32,1,128,256]{2,0,3,1:T(8,128)(2,1)}, u32[]{:S(2)}) copy-start(bf16[32,1,128,256]{2,0,3,1:T(8,128)(2,1)} %get-tuple-element.93) | copy-start | bytes 6291460
  738.4 12.0 %copy-start.15 = (f32[16,128]{1,0:T(8,128)S(1)}, f32[16,128]{1,0:T(8,128)}, u32[]{:S(2)}) copy-start(f32[16,128]{1,0:T(8,128)} %copy-done.14) | copy-start | bytes 24580
  738.4 12.1 %copy-start.17 = (f32[16,128]{1,0:T(8,128)S(1)}, f32[16,128]{1,0:T(8,128)}, u32[]{:S(2)}) copy-start(f32[16,128]{1,0:T(8,128)} %copy-done.16) | copy-start | bytes 24580
  753.9 108.7 %all-to-all-start.7 = ((bf16[8,2,4096]{2,1,0:T(2,128)(2,1)}), bf16[8,2,4096]{2,1,0:T(2,128)(2,1)S(1)}, u32[]{:S(2)}, u32[]{:S(2)}) async-start(bf16[8,2,4096]{2,1,0:T(2,128)(2,1)} %reshape.353), calls=%async_computation.7 | async-start | bytes 262144 | tf_op jit(solution)/shard_map/all_to_all | solution.py:147
  850.2 84.8 %copy-start.1 = (bf16[32,4,3,3]{0,1,3,2:T(4,128)(2,1)S(1)}, bf16[32,4,3,3]{0,1,3,2:T(4,128)(2,1)}, u32[]{:S(2)}) copy-start(bf16[32,4,3,3]{0,1,3,2:T(4,128)(2,1)} %param.10) | copy-start | bytes 6916
  857.2 7.0 copy-start.18
  857.2 8.3 copy-start.21
where the time goes:
time: 944 us; the launch traced here: 935 us
  matrix products  440 us (47%)
  local copies, waits for them, and re-layouts  269 us (28%)
  blocking collectives  91.4 us (10%)
  starting transfers between devices  66.7 us (7%)
  other arithmetic  34 us (4%)
  waiting for transfers between devices  31.3 us (3%)
    conv_general_dilated x3, matrix products, conv_valid(): lax.conv_general_dilated(inputs[None], kernel, (1, 1), 'VALID', dimension...  234 us
    transpose x1, matrix products, accumulate(): kernel_grad(inputs_mid, grad_mid).transpose(1, 0, 2, 3)  92.1 us
    conv_general_dilated x1, matrix products, kernel_grad(): lax.conv_general_dilated(inputs[:, None], cot_part[:, None], (1, 1), 'VAL...  91.3 us
    psum x1, blocking collectives, shards(): lax.psum((first_sum, bias_sum, second_sum, cot_sum), ('row', 'col'))  67.3 us
    conv_general_dilated x10, local copies, waits for them, and re-layouts, conv_valid(): lax.conv_general_dilated(inputs[None], kernel, (1, 1), 'VALID', dimension...  67.2 us
    broadcast_in_dim x2, local copies, waits for them, and re-layouts, kernel_grad(): inputs[:, None]  58.4 us
    unnamed x66, local copies, waits for them, and re-layouts  34.5 us
    convert_element_type x1, local copies, waits for them, and re-layouts, accumulate(): hidden = jax.nn.silu(preact_mid).astype(jnp.bfloat16)  25.6 us
  transfers between devices with their start and end apart: 14, of which 7 were waited for; matrix products, arithmetic and copies ran while one was open for 34% of the time, Pallas kernels for 0%

commit v1 on v0

v1 whole, which is shorter than its diff:
```python
import functools

import jax
import jax.numpy as jnp
import numpy as np
from jax import lax
from jax.experimental import pallas as pl
from jax.experimental.pallas import tpu as pltpu
from jax.sharding import PartitionSpec as P

IMAGE = 2048
DEVS = 128
STRIP = 16
REACH = 20
HOLD = 24
GRAD_ROWS = 18
HIDDEN = 32
RC = ("row", "col")
F32 = jnp.float32
BF16 = jnp.bfloat16
NT = (((1,), (1,)), ((), ()))
TN = (((0,), (0,)), ((), ()))


def turn(product, period):
    angle = 2.0 * np.pi * (product % period) / period
    return np.cos(angle), np.sin(angle)


def bf16_table(values):
    return np.asarray(values, np.float32).astype(jnp.bfloat16)


@functools.lru_cache(None)
def column_twiddle():
    cos, sin = turn(np.arange(8)[:, None] * np.arange(256)[None, :], 2048)
    return np.concatenate([cos, sin]).astype(np.float32)


@functools.lru_cache(None)
def column_forward_table(per):
    freq = 2 * np.arange(128)[:, None] + np.arange(2)[None, :]
    cos, sin = turn(freq[:, :, None] * np.arange(256), 256)
    table = np.zeros((128, 2, 2, 2, 2, 2, 256))
    for jhi in range(2):
        table[:, 0, :, jhi, jhi, 0] = cos
        table[:, 0, :, jhi, jhi, 1] = sin
        table[:, 1, :, jhi, jhi, 0] = -sin
        table[:, 1, :, jhi, jhi, 1] = cos
    full = np.zeros((128, per, 1024))
    full[:, :8] = table.reshape(128, 8, 1024)
    return bf16_table(full.reshape(128 * per, 1024))


@functools.lru_cache(None)
def column_inverse_table(per):
    freq = 2 * np.arange(128)[:, None] + np.arange(2)[None, :]
    cos, sin = turn(freq[:, :, None] * np.arange(256), 256)
    table = np.zeros((128, 2, 2, 2, 2, 2, 256))
    for jhi in range(2):
        table[:, 0, :, jhi, 0, jhi] = cos
        table[:, 1, :, jhi, 0, jhi] = -sin
        table[:, 0, :, jhi, 1, jhi] = sin
        table[:, 1, :, jhi, 1, jhi] = cos
    full = np.zeros((128, per, 1024))
    full[:, :8] = table.reshape(128, 8, 1024)
    return bf16_table(full.reshape(128 * per, 1024))


@functools.lru_cache(None)
def row_block_tables(per):
    cos, sin = turn(np.arange(16)[:, None] * np.arange(16), 16)
    ahead = np.zeros((2, 4, 8, 16, 16, 8, 2, 4))
    for kj in range(4):
        for c in range(8):
            ahead[0, kj, c, :, :, c, 0, kj] = cos
            ahead[0, kj, c, :, :, c, 1, kj] = sin
            ahead[1, kj, c, :, :, c, 0, kj] = -sin
            ahead[1, kj, c, :, :, c, 1, kj] = cos
    back = np.conj(ahead).transpose(4, 5, 6, 7, 0, 1, 2, 3).reshape(128, 8, 1024)
    full_ahead = np.zeros((1024, 128, per))
    full_ahead[:, :, :8] = ahead.reshape(1024, 128, 8)
    full_back = np.zeros((128, per, 1024))
    full_back[:, :8] = back
    return (
        bf16_table(full_ahead.reshape(1024, 128 * per)),
        bf16_table(full_back.reshape(128 * per, 1024) / IMAGE),
    )


@functools.lru_cache(None)
def row_forward_tables():
    pos = np.arange(128)
    cos, sin = turn(np.arange(16)[:, None] * pos, 2048)
    twiddle = np.concatenate([cos, sin]).astype(np.float32)
    cos, sin = turn(pos[:, None] * np.arange(128), 128)
    return twiddle, bf16_table(np.concatenate([cos, sin], 1))


@functools.lru_cache(None)
def row_inverse_tables(window, lead):
    pos = (16 * np.arange(8)[:, None] + np.arange(window)[None, :] - lead).reshape(-1)
    cos, sin = turn(np.arange(16)[:, None] * pos, 2048)
    twiddle = np.concatenate([cos, sin]).astype(np.float32)
    cos, sin = turn(np.arange(128)[:, None] * pos, 128)
    return twiddle, bf16_table(np.concatenate([cos, sin], 1))


@functools.lru_cache(None)
def sum_tables():
    spread = np.zeros((128, 10, 64))
    share = np.zeros((128, 10, 32))
    gather = np.zeros((16, 128, 10))
    collect = np.zeros((32, 128, 10))
    for d in range(128):
        spread[d, 8, d % 32] = 1.0
        spread[d, 9, 32 + d % 32] = 1.0
    share[:, 8, 0] = 1.0
    share[:, 9, 16] = 1.0
    gather[:, :, 8:] = 1.0
    for c in range(32):
        collect[c, c, 8:] = 1.0
    return (
        bf16_table(spread.reshape(1280, 64)),
        bf16_table(gather.reshape(16, 1280)),
        bf16_table(share.reshape(1280, 32)),
        bf16_table(collect.reshape(32, 1280)),
    )


@functools.lru_cache(None)
def weight_tables():
    first = np.zeros((3, 36, 256))
    second = np.zeros((2, 3, 9, 128))
    back = np.zeros((3, 36, 192))
    rows = np.full((8, 256), 99)
    for i in range(4):
        for q in range(3):
            at = 128 * (i // 2) + 20 * (3 * (i % 2) + q)
            rows[:, at : at + 20] = np.arange(20)
            for p in range(3):
                first[p, i * 9 + p * 3 + q, at : at + 20] = 1.0
                back[p, i * 9 + p * 3 + q, q * 64 + i * 16 : q * 64 + i * 16 + 16] = 1.0
    rows[:, 120] = -1
    for o in range(2):
        for q in range(3):
            at = 20 * (3 * o + q)
            for e in range(3):
                second[o, e, (2 - e) * 3 + 2 - q, at : at + 20] = 1.0
    fold = np.zeros((3, 384, 128), np.float32)
    for p in range(3):
        for i in range(4):
            for q in range(3):
                at = 128 * (i // 2) + 20 * (3 * (i % 2) + q)
                fold[p, at : at + 20, p * 12 + i * 3 + q] = 1.0
        for o in range(2):
            for q in range(3):
                at = 256 + 20 * (3 * o + q)
                fold[p, at : at + 20, 36 + p * 6 + o * 3 + q] = 1.0
    fold[0, 120, 54] = 1.0
    return (
        bf16_table(first),
        bf16_table(second),
        bf16_table(back),
        rows.astype(np.int32),
        fold,
    )


def columns_ahead(z, twiddle_ref):
    root = float(np.sqrt(0.5))
    s04, d04 = z[0] + z[4], z[0] - z[4]
    s26, d26 = z[2] + z[6], z[2] - z[6]
    s15, d15 = z[1] + z[5], z[1] - z[5]
    s37, d37 = z[3] + z[7], z[3] - z[7]
    low, high = root * (d15 - d37), root * (d15 + d37)
    real = [None] * 8
    imag = [None] * 8
    even, odd = s04 + s26, s15 + s37
    real[0], real[4] = even + odd, even - odd
    real[2], imag[2] = s04 - s26, s37 - s15
    real[1], imag[1] = d04 + low, -d26 - high
    real[3], imag[3] = d04 - low, d26 - high
    for j in (1, 2, 3):
        real[8 - j], imag[8 - j] = real[j], -imag[j]
    groups = []
    for jlo in range(4):
        pieces = []
        for jhi in range(2):
            j = 4 * jhi + jlo
            cos, sin = twiddle_ref[j : j + 1, :], twiddle_ref[8 + j : 9 + j, :]
            if imag[j] is None:
                pieces += [real[j] * cos, -real[j] * sin]
            else:
                pieces += [real[j] * cos + imag[j] * sin, imag[j] * cos - real[j] * sin]
        groups.append(jnp.concatenate(pieces, axis=1).astype(BF16))
    return jnp.concatenate(groups, axis=0)


def columns_back(rows_of, twiddle_ref):
    real = [None] * 8
    imag = [None] * 8
    for jlo in range(4):
        rows = rows_of(jlo)
        for jhi in range(2):
            j = 4 * jhi + jlo
            re = rows[:, jhi * 256 : jhi * 256 + 256]
            im = rows[:, 512 + jhi * 256 : 768 + jhi * 256]
            cos, sin = twiddle_ref[j : j + 1, :], twiddle_ref[8 + j : 9 + j, :]
            real[j] = re * cos - im * sin
            imag[j] = re * sin + im * cos
    fold_re = [real[0]] + [real[j] + real[8 - j] for j in (1, 2, 3)] + [real[4]]
    fold_im = [None] + [imag[j] - imag[8 - j] for j in (1, 2, 3)]
    scale = 1.0 / IMAGE
    root = float(np.sqrt(0.5)) * scale
    base_even = (fold_re[0] + fold_re[4]) * scale
    base_odd = (fold_re[0] - fold_re[4]) * scale
    re2, im2 = fold_re[2] * scale, fold_im[2] * scale
    sum_re, dif_re = fold_re[1] + fold_re[3], fold_re[1] - fold_re[3]
    sum_im, dif_im = fold_im[1] + fold_im[3], fold_im[1] - fold_im[3]
    cross = root * (dif_re - sum_im), root * (dif_re + sum_im)
    return [
        base_even + re2 + sum_re * scale,
        base_odd - im2 + cross[0],
        base_even - re2 - dif_im * scale,
        base_odd + im2 - cross[1],
        base_even + re2 - sum_re * scale,
        base_odd - im2 - cross[0],
        base_even - re2 + dif_im * scale,
        base_odd + im2 + cross[1],
    ]


def swap_blocks(arrays, size):
    arrays = list(arrays)
    count = 128 // size
    lane = lax.broadcasted_iota(jnp.int32, arrays[0].shape, 1)
    step = count // 2
    while step:
        low = (lane & (step * size)) == 0
        for i in range(count):
            if not i & step:
                one, two = arrays[i], arrays[i + step]
                arrays[i] = jnp.where(low, one, pltpu.roll(two, step * size, 1))
                arrays[i + step] = jnp.where(low, pltpu.roll(one, 128 - step * size, 1), two)
        step //= 2
    return arrays


def halves(values):
    high = values.astype(BF16)
    return high, (values - high.astype(F32)).astype(BF16)


def ahead_body(strip_ref, twiddle_ref, table_ref, out_ref):
    z = [strip_ref[c, 0:2].astype(F32).reshape(32, 256) for c in range(8)]
    values = columns_ahead(z, twiddle_ref)
    out_ref[...] = lax.dot_general(
        table_ref[...], values, NT, preferred_element_type=F32
    ).astype(BF16)


def middle_body(window, summing, *refs):
    in_ref, spectra_ref, ahead_ref, back_ref, row_ref, back_row_ref, tw_ref, back_tw_ref = refs[:8]
    out_ref = refs[-1]
    chunks = in_ref[...]
    first = jnp.dot(ahead_ref[...], chunks, preferred_element_type=F32).reshape(8, 8, 16, 128)
    per_m = swap_blocks([first[:, c].reshape(128, 128) for c in range(8)], 16)
    cos, sin = tw_ref[0:16, :], tw_ref[16:32, :]
    rows = []
    for m in range(8):
        real = per_m[m][:64].reshape(4, 16, 128)
        imag = per_m[m][64:].reshape(4, 16, 128)
        rows.append((real * cos + imag * sin).astype(BF16).reshape(64, 128))
        rows.append((imag * cos - real * sin).astype(BF16).reshape(64, 128))
    second = jnp.dot(jnp.concatenate(rows, 0), row_ref[...], preferred_element_type=F32)
    rows = []
    for jlo in range(4):
        full_re, full_im = [], []
        for plane in range(2):
            m = 2 * jlo + plane
            part = second[128 * m : 128 * m + 128]
            full_re.append(part[:64, :128] + part[64:, 128:])
            full_im.append(part[64:, :128] - part[:64, 128:])
        weights = [
            spectra_ref[t].reshape(4, 4, 16, 128)[:, jlo].reshape(64, 128) for t in range(3)
        ]
        for plane in range(2):
            for part in (full_re, full_im):
                mixed = weights[plane] * part[0] + weights[plane + 1] * part[1]
                rows.append(mixed.astype(BF16))
    third = jnp.dot(jnp.concatenate(rows, 0), back_row_ref[...], preferred_element_type=F32)
    half = 8 * window
    cos, sin = back_tw_ref[0:16, :], back_tw_ref[16:32, :]
    per_m = []
    for m in range(8):
        part = third[128 * m : 128 * m + 128]
        real = (part[:64, :half] - part[64:, half:]).reshape(4, 16, half)
        imag = (part[64:, :half] + part[:64, half:]).reshape(4, 16, half)
        per_m.append(
            jnp.concatenate(
                [
                    (real * cos - imag * sin).reshape(64, half),
                    (real * sin + imag * cos).reshape(64, half),
                ],
                0,
            )
        )
    count = 128 // window
    tiles = 8 // count
    per_c = [[None] * tiles for _ in range(8)]
    for m_hi in range(tiles):
        for c_hi in range(tiles):
            cols = slice(128 * c_hi, 128 * c_hi + 128)
            group = [per_m[m_hi * count + i][:, cols] for i in range(count)]
            for i, value in enumerate(swap_blocks(group, window)):
                per_c[c_hi * count + i][m_hi] = value
    blocks = [
        (v[0] if tiles == 1 else jnp.concatenate(v, 1)).astype(BF16).reshape(8, 1, 16, half)
        for v in per_c
    ]
    rows = jnp.concatenate(blocks, 1).reshape(1024, half)
    out = jnp.dot(back_ref[...], rows, preferred_element_type=F32)
    if summing:
        gather_ref, share_ref = refs[8:10]
        total = jnp.dot(gather_ref[...], chunks, preferred_element_type=F32)
        out = out + jnp.dot(
            share_ref[...], jnp.concatenate(halves(total), 0), preferred_element_type=F32
        )
    out_ref[...] = out.astype(BF16)


def shifted(value, q):
    if q == 1:
        return value
    lane = lax.broadcasted_iota(jnp.int32, value.shape, 1)
    if q == 0:
        return jnp.where(lane == 0, 0.0, pltpu.roll(value, 1, 1))
    return jnp.where(lane == IMAGE - 1, 0.0, pltpu.roll(value, IMAGE - 1, 1))


def banded(weights, first_row, lowest):
    rows = []
    for r in range(GRAD_ROWS):
        total = jnp.zeros(weights[0].shape, F32)
        for p in range(3):
            total = total + jnp.where(first_row == r + p + lowest, weights[p], 0.0)
        rows.append(total)
    return jnp.concatenate(rows, 0)


def prepare_body(
    strip_ref,
    above_ref,
    below_ref,
    w_first_ref,
    w_second_ref,
    bias_ref,
    first_table_ref,
    second_table_ref,
    back_table_ref,
    rows_ref,
    estimate_ref,
    cot_ref,
    dirty_ref,
    first_ref,
    second_ref,
    back_ref,
    tall_ref,
    stack_ref,
):
    row = lax.broadcasted_iota(jnp.int32, (128, IMAGE), 0)
    tall_ref[...] = jnp.zeros_like(tall_ref)
    for i in range(6):
        for c in range(8):
            cols = slice(256 * c, 256 * c + 256)
            tall_ref[0:2, cols] = above_ref[c, i].astype(F32)
            tall_ref[2:18, cols] = strip_ref[c, i].astype(F32)
            tall_ref[18:20, cols] = below_ref[c, i].astype(F32)
        value = tall_ref[...]
        if i in (2, 3):
            dirty_ref[i - 2] = value
        else:
            for q in range(3):
                at = 20 * (3 * (i % 2) + q)
                stack_ref[at : at + 20, :] = shifted(value, q)[0:20]
            if i == 1:
                out = jnp.where(row < 120, stack_ref[...], jnp.where(row < 123, 1.0, 0.0))
                estimate_ref[...] = out.astype(BF16)
            if i == 5:
                cot_ref[...] = jnp.where(row < 120, stack_ref[...], 0.0).astype(BF16)
    w_first = w_first_ref[...]
    rows = rows_ref[0:1, :]
    parts = [jnp.dot(w_first, first_table_ref[p], preferred_element_type=F32) for p in range(3)]
    lanes = lax.broadcasted_iota(jnp.int32, (HIDDEN, 256), 1)
    bias = bias_ref[...]
    high = bias.astype(BF16).astype(F32)
    middle = (bias - high).astype(BF16).astype(F32)
    low = bias - high - middle
    offset = jnp.where(
        lanes == 120, high, jnp.where(lanes == 121, middle, jnp.where(lanes == 122, low, 0.0))
    )
    first = banded(parts, rows, 0) + jnp.concatenate([offset] * GRAD_ROWS, 0)
    first_ref[...] = first.astype(BF16)
    parts = [
        jnp.dot(w_second_ref[0], second_table_ref[0, e], preferred_element_type=F32)
        + jnp.dot(w_second_ref[1], second_table_ref[1, e], preferred_element_type=F32)
        for e in range(3)
    ]
    second_ref[...] = banded(parts, rows[:, :128], 0).astype(BF16)
    parts = [jnp.dot(w_first, back_table_ref[p], preferred_element_type=F32) for p in range(3)]
    rows = lax.broadcasted_iota(jnp.int32, (1, 192), 1) & 15
    parts = [parts[2 - p] for p in range(3)]
    back = banded_back(parts, rows)
    back_ref[...] = back.T.astype(BF16)


def banded_back(parts, rows):
    blocks = []
    for r in range(GRAD_ROWS):
        total = jnp.zeros(parts[0].shape, F32)
        for k in range(3):
            total = total + jnp.where(rows == r - k, parts[k], 0.0)
        blocks.append(total)
    return jnp.concatenate(blocks, 0)


def network_body(
    place_ref,
    in_ref,
    strip_ref,
    dirty_ref,
    estimate_ref,
    cot_ref,
    first_ref,
    second_ref,
    back_ref,
    twiddle_ref,
    inverse_ref,
    forward_ref,
    spread_ref,
    rows_ref,
    fold_ref,
    base_ref,
    out_ref,
    stack_ref,
    features_ref,
    spread_grad_ref,
    acc_first_ref,
    acc_second_ref,
):
    place = place_ref[0]
    values = lax.dot_general(in_ref[...], inverse_ref[...], TN, preferred_element_type=F32)
    row = lax.broadcasted_iota(jnp.int32, (HOLD, IMAGE), 0)
    inside = ((row >= 2) | (place > 0)) & ((row < 18) | (place < DEVS - 1))
    for plane in range(2):
        blocks = columns_back(
            lambda jlo: values[64 * jlo + 32 * plane : 64 * jlo + 32 * plane + HOLD], twiddle_ref
        )
        blurred = jnp.concatenate(blocks, 1).astype(BF16).astype(F32)
        residual = dirty_ref[plane] - jnp.where(inside, blurred, 0.0)
        residual = residual.astype(BF16).astype(F32)
        for q in range(3):
            at = 20 * (3 * plane + q)
            stack_ref[at : at + 20, :] = shifted(residual, q)[0:20]
    stack_ref[120:128, :] = jnp.zeros((8, IMAGE), F32)
    features_ref[0:128, :] = estimate_ref[...]
    features_ref[128:256, :] = stack_ref[...].astype(BF16)
    acc_first_ref[...] = jnp.zeros_like(acc_first_ref)
    acc_second_ref[...] = jnp.zeros_like(acc_second_ref)
    top = jnp.where(place > 0, 1.0, 0.0)
    bottom = jnp.where(place < DEVS - 1, 1.0, 0.0)

    def block(step, carry):
        cols = pl.ds(pl.multiple_of(step * 256, 256), 256)
        features = features_ref[:, cols]
        cots = cot_ref[:, cols]
        preact = jnp.dot(first_ref[...], features, preferred_element_type=F32)
        back = jnp.dot(second_ref[...], cots, preferred_element_type=F32)
        gate = 0.5 * jnp.tanh(0.5 * preact) + 0.5
        hidden = preact * gate
        grad_pre = back * (gate + hidden * (1.0 - gate))
        grad_pre = jnp.concatenate(
            [grad_pre[0:32] * top, grad_pre[32:544], grad_pre[544:576] * bottom], 0
        ).astype(BF16)
        spread_grad_ref[:, cols] = jnp.dot(back_ref[...], grad_pre, preferred_element_type=F32)
        acc_first_ref[...] += lax.dot_general(grad_pre, features, NT, preferred_element_type=F32)
        acc_second_ref[...] += lax.dot_general(
            hidden.astype(BF16), cots, NT, preferred_element_type=F32
        )
        return carry

    lax.fori_loop(0, 8, block, 0)

    cot_sums = []
    z = [[None, None] for _ in range(8)]
    for i in range(4):
        rows = [spread_grad_ref[64 * q + 16 * i : 64 * q + 16 * i + 16, :] for q in range(3)]
        total = shifted(rows[0], 2) + rows[1] + shifted(rows[2], 0)
        for c in range(8):
            part = total[:, 256 * c : 256 * c + 256]
            if i < 2:
                base_ref[c, i] = part + strip_ref[c, 4 + i].astype(F32)
            else:
                z[c][i - 2] = part.astype(BF16).astype(F32)
    for i in range(2):
        total = strip_ref[0, 4 + i].astype(F32)
        for c in range(1, 8):
            total = total + strip_ref[c, 4 + i].astype(F32)
        cot_sums.append(total.sum(axis=0, keepdims=True).sum(axis=1, keepdims=True))

    rows = rows_ref[0:1, :]
    parts = [jnp.zeros((HIDDEN, 384), F32) for _ in range(3)]
    for r in range(1, 17):
        of_first = acc_first_ref[32 * r : 32 * r + 32, :]
        of_second = acc_second_ref[32 * r : 32 * r + 32, :]
        for p in range(3):
            keep = (rows == r + p) | (rows == -1)
            parts[p] = parts[p] + jnp.concatenate(
                [
                    jnp.where(keep, of_first, 0.0),
                    jnp.where(rows[:, :128] == r + p, of_second, 0.0),
                ],
                1,
            )
    sums = jnp.zeros((HIDDEN, 128), F32)
    for p in range(3):
        sums = sums + jnp.dot(
            parts[p], fold_ref[p], precision=lax.Precision.HIGHEST, preferred_element_type=F32
        )
    at = lax.broadcasted_iota(jnp.int32, (HIDDEN, 128), 1)
    of = lax.broadcasted_iota(jnp.int32, (HIDDEN, 128), 0)
    for i in range(2):
        sums = jnp.where((at == 55) & (of == i), cot_sums[i], sums)

    values = columns_ahead([jnp.concatenate(v, 0) for v in z], twiddle_ref)
    out = lax.dot_general(forward_ref[...], values, NT, preferred_element_type=F32)
    out = out + jnp.dot(
        spread_ref[...], jnp.concatenate(halves(sums), 0), preferred_element_type=F32
    )
    out_ref[...] = out.astype(BF16)


def finish_body(in_ref, base_ref, twiddle_ref, inverse_ref, collect_ref, out_ref, sums_ref):
    chunks = in_ref[...]
    sums_ref[...] = jnp.dot(collect_ref[...], chunks, preferred_element_type=F32) * (1.0 / IMAGE)
    values = lax.dot_general(chunks, inverse_ref[...], TN, preferred_element_type=F32)
    blocks = columns_back(lambda jlo: values[32 * jlo : 32 * jlo + 32], twiddle_ref)
    for c in range(8):
        blurred = blocks[c].astype(BF16).astype(F32).reshape(2, STRIP, 256)
        out_ref[c] = base_ref[c] - blurred


def call(body, outs, *args, scratch=(), scalars=0, vmem=56):
    whole = pl.BlockSpec(memory_space=pltpu.VMEM)
    return pl.pallas_call(
        body,
        out_shape=outs,
        in_specs=[pl.BlockSpec(memory_space=pltpu.SMEM)] * scalars
        + [whole] * (len(args) - scalars),
        out_specs=jax.tree.map(lambda _: whole, outs),
        scratch_shapes=list(scratch),
        compiler_params=pltpu.CompilerParams(vmem_limit_bytes=vmem * 1024 * 1024),
    )(*args)


def like(*shape, dtype=BF16):
    return jax.ShapeDtypeStruct(shape, dtype)


def exchange(chunks, per):
    width = chunks.shape[-1]
    rows = 8 if per == 8 else 2
    moved = lax.all_to_all(chunks.reshape(DEVS * per // rows, rows, width), RC, 0, 0, tiled=True)
    return moved.reshape(DEVS * per, width)


def middle(chunks, spectra, window, lead, per):
    ahead, back = row_block_tables(per)
    twiddle, row_table = row_forward_tables()
    back_twiddle, back_row = row_inverse_tables(window, lead)
    extra = sum_tables()[1:3] if per == 10 else ()
    return call(
        functools.partial(middle_body, window, per == 10),
        like(DEVS * per, 8 * window),
        chunks,
        spectra,
        ahead,
        back,
        row_table,
        back_row,
        twiddle,
        back_twiddle,
        *extra,
    )


def shards(estimate, dirty_image, psf_spectra, w_first, b_first, w_second, cotangent):
    cells = jnp.stack([v.reshape(2, 8, STRIP, 256) for v in (estimate, dirty_image, cotangent)])
    cells = cells.transpose(2, 0, 1, 3, 4).reshape(8, 6, STRIP, 256)
    strip = lax.all_to_all(cells, "col", 0, 0, tiled=True)
    spec = call(
        ahead_body, like(1024, 128), strip, column_twiddle(), column_forward_table(8)
    )
    spec = exchange(spec, 8)
    above = lax.ppermute(strip[:, :, -2:], RC, [(d, d + 1) for d in range(DEVS - 1)])
    below = lax.ppermute(strip[:, :, :2], RC, [(d + 1, d) for d in range(DEVS - 1)])
    first_table, second_table, back_table, row_of, fold = weight_tables()
    im_estimate, im_cot, dirty, first, second, back = call(
        prepare_body,
        (
            like(128, IMAGE),
            like(128, IMAGE),
            like(2, HOLD, IMAGE, dtype=F32),
            like(576, 256),
            like(576, 128),
            like(192, 576),
        ),
        strip,
        above,
        below,
        w_first.reshape(32, 36),
        w_second.reshape(2, 32, 9),
        b_first.reshape(32, 1),
        first_table,
        second_table,
        back_table,
        row_of,
        scratch=[pltpu.VMEM((HOLD, IMAGE), F32), pltpu.VMEM((128, IMAGE), F32)],
    )
    mixed = exchange(middle(spec, psf_spectra, 32, 2, 8), 8)
    place = (lax.axis_index("row") * 8 + lax.axis_index("col")).astype(jnp.int32).reshape(1)
    base, spec = call(
        network_body,
        (like(8, 2, STRIP, 256, dtype=F32), like(1280, 128)),
        place,
        mixed,
        strip,
        dirty,
        im_estimate,
        im_cot,
        first,
        second,
        back,
        column_twiddle(),
        column_inverse_table(8),
        column_forward_table(10),
        sum_tables()[0],
        row_of,
        fold,
        scratch=[
            pltpu.VMEM((128, IMAGE), F32),
            pltpu.VMEM((256, IMAGE), BF16),
            pltpu.VMEM((192, IMAGE), F32),
            pltpu.VMEM((576, 256), F32),
            pltpu.VMEM((576, 128), F32),
        ],
        scalars=1,
    )
    mixed = exchange(middle(exchange(spec, 10), psf_spectra, 16, 0, 10), 10)
    image, sums = call(
        finish_body,
        (like(8, 2, STRIP, 256, dtype=F32), like(32, 128, dtype=F32)),
        mixed,
        base,
        column_twiddle(),
        column_inverse_table(10),
        sum_tables()[3],
    )
    image = lax.all_to_all(image, "col", 0, 0, tiled=True)
    grad_image = image.transpose(1, 0, 2, 3).reshape(2, 128, 256)
    grad_first = sums[:, :36].reshape(32, 3, 4, 3).transpose(0, 2, 1, 3)
    grad_second = jnp.flip(sums[:, 36:54].reshape(32, 3, 2, 3), (1, 3)).transpose(2, 0, 1, 3)
    return grad_image, grad_first, sums[:, 54], grad_second, sums[:2, 55]


def solution(mesh):
    return jax.shard_map(
        shards,
        mesh=mesh,
        in_specs=(
            P(None, "row", "col"),
            P(None, "row", "col"),
            P(None, ("row", "col"), None, None),
            P(),
            P(),
            P(),
            P(None, "row", "col"),
        ),
        out_specs=(P(None, "row", "col"), P(), P(), P(), P()),
        check_vma=False,
    )
```

time: 944 us -> 143 us (0.15)
  matrix products: 440 us -> 0 us
  local copies, waits for them, and re-layouts: 269 us -> 11.7 us
  starting transfers between devices: 66.7 us -> 13.9 us
  Pallas kernels: 0 us -> 37.7 us
  other arithmetic: 34 us -> 1.08 us
  waiting for transfers between devices: 31.3 us -> 2.03 us
  blocking collectives: 91.4 us -> 75.5 us
    conv_general_dilated x4 -> x0, matrix products: 325 us -> none  [the longest x3 234 us: conv_valid(): lax.conv_general_dilated(inputs[None], kernel, (1, 1), 'VALID', dimension...]
    transpose x1 -> x0, matrix products: 92.1 us -> none  [accumulate(): kernel_grad(inputs_mid, grad_mid).transpose(1, 0, 2, 3)]
    psum x1 -> x0, blocking collectives: 67.3 us -> none  [shards(): lax.psum((first_sum, bias_sum, second_sum, cot_sum), ('row', 'col'))]
    conv_general_dilated x10 -> x0, local copies, waits for them, and re-layouts: 67.2 us -> none  [conv_valid(): lax.conv_general_dilated(inputs[None], kernel, (1, 1), 'VALID', dimension...]
    broadcast_in_dim x5 -> x0, local copies, waits for them, and re-layouts: 62.3 us -> none  [the longest x2 58.4 us: kernel_grad(): inputs[:, None]]
    convert_element_type x10 -> x0, local copies, waits for them, and re-layouts: 54.2 us -> none  [the longest x1 25.6 us: accumulate(): hidden = jax.nn.silu(preact_mid).astype(jnp.bfloat16)]
    all_to_all x2 -> x4, blocking collectives: 24.2 us -> 75.5 us  [the longest x3 60.5 us: exchange(): lax.all_to_all(chunks.reshape(DEVS * per // rows, rows, width), RC, 0, 0,...]
    all_to_all x6 -> x2, starting transfers between devices: 45.8 us -> 8.02 us  [the longest x1 4.61 us: exchange(): lax.all_to_all(chunks.reshape(DEVS * per // rows, rows, width), RC, 0, 0,...]
  transfers between devices with their start and end apart: 14 -> 4, of which waited for: 7 -> 2; matrix products, arithmetic and copies ran while one was open for 34% -> 6% of each run, Pallas kernels for 0% -> 2%
where the time goes in v1:
time: 143 us
  blocking collectives  75.5 us (53%)
  Pallas kernels  37.7 us (26%)
  starting transfers between devices  13.9 us (10%)
  local copies, waits for them, and re-layouts  11.7 us (8%)
  waiting for transfers between devices  2.03 us (1%)
    all_to_all x3, blocking collectives, exchange(): lax.all_to_all(chunks.reshape(DEVS * per // rows, rows, width), RC, 0, 0,...  60.5 us
    pallas_call x6, Pallas kernels, call(): pl.pallas_call(body, out_shape=outs, in_specs=[pl.BlockSpec(memory_space=...  37.7 us
    all_to_all x1, blocking collectives, shards(): strip = lax.all_to_all(cells, 'col', 0, 0, tiled=True)  15 us
    all_to_all x1, starting transfers between devices, exchange(): lax.all_to_all(chunks.reshape(DEVS * per // rows, rows, width), RC, 0, 0,...  4.61 us
    ppermute x1, starting transfers between devices, shards(): lax.ppermute(strip[:, :, -2:], RC, [(d, d + 1) for d in range(DEVS - 1)])  4.55 us
    all_to_all x1, starting transfers between devices, shards(): image = lax.all_to_all(image, 'col', 0, 0, tiled=True)  3.41 us
    unnamed x15, local copies, waits for them, and re-layouts  3.26 us
  transfers between devices with their start and end apart: 4, of which 2 were waited for; matrix products, arithmetic and copies ran while one was open for 6% of the time, Pallas kernels for 2%

profile of v1, /device:TPU:0, one launch (start us, length us, event | category | flops | bytes accessed | tf_op | source)
XLA Modules:
  0.0 142.6 jit_solution(9992944702095967913)
XLA Ops:
  0.6 1.1 pad_maximum_fusion
  1.8 15.0 %all_to_all.30.strip_ref = bf16[8,6,16,256]{3,2,1,0:T(8,128)(2,1)} all-to-all(bf16[8,6,16,256]{3,2,1,0:T(8,128)(2,1)S(1)} %bitcast.30), channel_id=1, replica_groups=mesh['row'=16,'col'=8] {'col'}, dimensions={0} | all-to-all | bytes 786432 | tf_op jit(solution)/shard_map/all_to_all | solution.py:601
  16.8 3.2 %shard_map.326 = bf16[1024,128]{1,0:T(8,128)(2,1)} custom-call(bf16[8,6,16,256]{3,2,1,0:T(8,128)(2,1)} %all_to_all.30.strip_ref, f32[16,256]{1,0:T(8,128)} %constant.55.clone.twiddle_ref, bf16[1024,1024]{1,0:T(8,128)(2,1)} %constant.56.clone.table_ref), custom_call_target="tpu_custom_call" | custom-call | tf_op jit(solution)/shard_map/pallas_call | solution.py:556
  20.0 19.0 %all_to_all.31 = bf16[128,8,128]{2,1,0:T(8,128)(2,1)} all-to-all(bf16[128,8,128]{2,1,0:T(8,128)(2,1)} %bitcast.36), channel_id=1, replica_groups=mesh['row'=16,'col'=8] {'row','col'}, dimensions={0} | all-to-all | bytes 524288 | tf_op jit(solution)/shard_map/all_to_all | solution.py:574
  38.9 0.0 copy-start.3
  38.9 0.0 copy-start.5
  38.9 0.0 copy-start.4
  38.9 7.0 %shard_map.327 = bf16[1024,256]{1,0:T(8,128)(2,1)} custom-call(bf16[1024,128]{1,0:T(8,128)(2,1)} %bitcast.34, f32[3,16,16,128]{3,2,1,0:T(8,128)} %refs_1_.3, bf16[1024,1024]{1,0:T(8,128)(2,1)} %constant.61.clone.refs_2_, bf16[1024,1024]{1,0:T(8,128)(2,1)} %constant.62.clone.refs_3_, bf16[128,256]{1,0:T(8,128)(2,1)} %constant.63.clone.refs_4_.refs_5_, ...), custom_call_target="tpu_custom_call" | custom-call | tf_op jit(solution)/shard_map/pallas_call | solution.py:556
  46.0 4.6 %all-to-all-start.2 = ((bf16[128,8,256]{2,1,0:T(8,128)(2,1)}), bf16[128,8,256]{2,1,0:T(8,128)(2,1)S(1)}, u32[]{:S(2)}, u32[]{:S(2)}) async-start(bf16[128,8,256]{2,1,0:T(8,128)(2,1)} %bitcast.29), calls=%async_computation.2 | async-start | bytes 1048576 | tf_op jit(solution)/shard_map/all_to_all | solution.py:574
  50.6 1.1 fusion
  51.7 1.3 collective-permute-start.1
  53.0 4.5 %collective-permute-start = (bf16[8,6,2,256]{3,2,1,0:T(2,128)(2,1)S(1)}, bf16[8,6,2,256]{3,2,1,0:T(2,128)(2,1)S(1)}, u32[]{:S(2)}, u32[]{:S(2)}) collective-permute-start(bf16[8,6,2,256]{3,2,1,0:T(2,128)(2,1)S(1)} %get-tuple-element.31), channel_id=1, source_target_pairs={{0,1},{1,2},{2,3},{3,4},{4,5},{5,6},{6,7},{7,8},{8,9},{9,10},{10,1... | collective-permute-start | bytes 147464 | tf_op jit(solution)/shard_map/ppermute | solution.py:606
  57.5 0.0 copy-done.3
  57.6 0.7 copy.48.w_first_ref
  58.3 0.0 copy-done.5
  58.3 0.7 copy.50.bias_ref
  59.0 0.0 copy-done.4
  59.0 0.7 copy.49.w_second_ref
  59.7 0.0 collective-permute-done.1.below_ref
  59.7 0.0 copy-start.1
  59.7 0.0 collective-permute-done.above_ref
  59.7 0.6 copy-done.1
  60.3 0.0 copy-start.2
  60.3 0.6 copy-done.2
  60.9 3.4 %shard_map.328 = (bf16[128,2048]{1,0:T(8,128)(2,1)}, bf16[128,2048]{1,0:T(8,128)(2,1)}, f32[2,24,2048]{2,1,0:T(8,128)}, bf16[576,256]{1,0:T(8,128)(2,1)}, bf16[5...) custom-call(bf16[8,6,16,256]{3,2,1,0:T(8,128)(2,1)} %all_to_all.30.strip_ref, bf16[8,6,2,256]{3,2,1,0:T(2,128)(2,1)} %copy-done.2, ...), custom_call_target="tpu_custom_call" | custom-call | tf_op jit(solution)/shard_map/pallas_call | solution.py:556
  64.3 0.5 all-to-all-done.2
  64.8 0.0 copy-start
  64.8 0.8 copy-done
  65.6 13.5 %shard_map.329 = (f32[8,2,16,256]{3,2,1,0:T(8,128)}, bf16[1280,128]{1,0:T(8,128)(2,1)}) custom-call(s32[1]{0:T(128)} %bitcast.place_ref, bf16[1024,256]{1,0:T(8,128)(2,1)} %bitcast.28, bf16[8,6,16,256]{3,2,1,0:T(8,128)(2,1)} %all_to_all.30.strip_ref, f32[2,24,2048]{2,1,0:T(8,128)} %get-tuple-element.15.dirty_ref, ...), custom_call_target="tpu_custom_call" | custom-call | tf_op jit(solution)/shard_map/pallas_call | solution.py:556
  79.1 24.4 %all_to_all.32 = bf16[640,2,128]{2,1,0:T(2,128)(2,1)} all-to-all(bf16[640,2,128]{2,1,0:T(2,128)(2,1)} %bitcast.37), channel_id=1, replica_groups=mesh['row'=16,'col'=8] {'row','col'}, dimensions={0} | all-to-all | bytes 655360 | tf_op jit(solution)/shard_map/all_to_all | solution.py:574
  103.5 7.3 %shard_map.330 = bf16[1280,128]{1,0:T(8,128)(2,1)} custom-call(bf16[1280,128]{1,0:T(8,128)(2,1)} %bitcast.32, f32[3,16,16,128]{3,2,1,0:T(8,128)} %refs_1_.3, bf16[1024,1280]{1,0:T(8,128)(2,1)} %constant.71.clone.refs_2_, bf16[1280,1024]{1,0:T(8,128)(2,1)} %constant.72.clone.refs_3_, bf16[128,256]{1,0:T(8,128)(2,1)} %constant.63.clone.refs_4_.refs_5_, ...), custom_call_target="tpu_custom_call" | custom-call | tf_op jit(solution)/shard_map/pallas_call | solution.py:556
  110.9 17.2 %all_to_all.33 = bf16[640,2,128]{2,1,0:T(2,128)(2,1)} all-to-all(bf16[640,2,128]{2,1,0:T(2,128)(2,1)} %bitcast.33), channel_id=1, replica_groups=mesh['row'=16,'col'=8] {'row','col'}, dimensions={0} | all-to-all | bytes 655360 | tf_op jit(solution)/shard_map/all_to_all | solution.py:574
  128.0 3.2 %shard_map.331 = (f32[8,2,16,256]{3,2,1,0:T(8,128)}, f32[32,128]{1,0:T(8,128)}) custom-call(bf16[1280,128]{1,0:T(8,128)(2,1)} %bitcast.31, f32[8,2,16,256]{3,2,1,0:T(8,128)} %get-tuple-element.22.base_ref, f32[16,256]{1,0:T(8,128)} %constant.55.clone.twiddle_ref, bf16[1280,1024]{1,0:T(8,128)(2,1)} %constant.75.clone.inverse_ref, ...), custom_call_target="tpu_custom_call" | custom-call | tf_op jit(solution)/shard_map/pallas_call | solution.py:556
  131.3 3.4 %all-to-all-start.5 = ((f32[8,2,16,256]{3,2,1,0:T(8,128)}), f32[8,2,16,256]{3,2,1,0:T(8,128)S(1)}, u32[]{:S(2)}, u32[]{:S(2)}) async-start(f32[8,2,16,256]{3,2,1,0:T(8,128)} %get-tuple-element.23), calls=%async_computation.5 | async-start | bytes 524288 | tf_op jit(solution)/shard_map/all_to_all | solution.py:670
  134.7 0.8 slice.22
  135.5 0.1 copy.53
  135.6 0.6 copy.55
  136.2 0.8 copy.52
  137.0 0.6 copy.54
  137.6 1.4 slice_reduce_fusion.1
  139.0 1.4 slice_reduce_fusion
  140.4 1.5 %all-to-all-done.5 = f32[8,2,16,256]{3,2,1,0:T(8,128)S(1)} async-done(((f32[8,2,16,256]{3,2,1,0:T(8,128)}), f32[8,2,16,256]{3,2,1,0:T(8,128)S(1)}, u32[]{:S(2)}, u32[]{:S(2)}) %all-to-all-start.5) | async-done | bytes 262176 | tf_op jit(solution)/shard_map/all_to_all | solution.py:670
  141.9 0.7 copy.51
  (6 shorter events, 0.1 us)
Async XLA Ops:
  38.9 18.6 %copy-start.3 = (bf16[32,4,3,3]{0,1,3,2:T(4,128)(2,1)S(1)}, bf16[32,4,3,3]{0,1,3,2:T(4,128)(2,1)}, u32[]{:S(2)}) copy-start(bf16[32,4,3,3]{0,1,3,2:T(4,128)(2,1)} %param.34) | copy-start | bytes 6916
  38.9 19.3 %copy-start.5 = (f32[32]{0:T(128)S(1)}, f32[32]{0:T(128)}, u32[]{:S(2)}) copy-start(f32[32]{0:T(128)} %param.35) | copy-start | bytes 388
  38.9 20.0 %copy-start.4 = (bf16[2,32,3,3]{1,0,3,2:T(2,128)(2,1)S(1)}, bf16[2,32,3,3]{1,0,3,2:T(2,128)(2,1)}, u32[]{:S(2)}) copy-start(bf16[2,32,3,3]{1,0,3,2:T(2,128)(2,1)} %param.36) | copy-start | bytes 3460
  46.0 18.9 %all-to-all-start.2 = ((bf16[128,8,256]{2,1,0:T(8,128)(2,1)}), bf16[128,8,256]{2,1,0:T(8,128)(2,1)S(1)}, u32[]{:S(2)}, u32[]{:S(2)}) async-start(bf16[128,8,256]{2,1,0:T(8,128)(2,1)} %bitcast.29), calls=%async_computation.2 | async-start | bytes 1048576 | tf_op jit(solution)/shard_map/all_to_all | solution.py:574
  51.7 8.0 %collective-permute-start.1 = (bf16[8,6,2,256]{3,2,1,0:T(2,128)(2,1)S(1)}, bf16[8,6,2,256]{3,2,1,0:T(2,128)(2,1)S(1)}, u32[]{:S(2)}, u32[]{:S(2)}) collective-permute-start(bf16[8,6,2,256]{3,2,1,0:T(2,128)(2,1)S(1)} %get-tuple-element.30), channel_id=1, source_target_pairs={{1,0},{2,1},{3,2},{4,3},{5,4},{6,5},{7,6},{8,7},{9,8},{10,9},{11,1... | collective-permute-start | bytes 147464 | tf_op jit(solution)/shard_map/ppermute | solution.py:607
  53.0 6.7 %collective-permute-start = (bf16[8,6,2,256]{3,2,1,0:T(2,128)(2,1)S(1)}, bf16[8,6,2,256]{3,2,1,0:T(2,128)(2,1)S(1)}, u32[]{:S(2)}, u32[]{:S(2)}) collective-permute-start(bf16[8,6,2,256]{3,2,1,0:T(2,128)(2,1)S(1)} %get-tuple-element.31), channel_id=1, source_target_pairs={{0,1},{1,2},{2,3},{3,4},{4,5},{5,6},{6,7},{7,8},{8,9},{9,10},{10,1... | collective-permute-start | bytes 147464 | tf_op jit(solution)/shard_map/ppermute | solution.py:606
  59.7 0.6 copy-start.1
  60.3 0.6 copy-start.2
  64.8 0.8 copy-start
  131.3 10.6 %all-to-all-start.5 = ((f32[8,2,16,256]{3,2,1,0:T(8,128)}), f32[8,2,16,256]{3,2,1,0:T(8,128)S(1)}, u32[]{:S(2)}, u32[]{:S(2)}) async-start(f32[8,2,16,256]{3,2,1,0:T(8,128)} %get-tuple-element.23), calls=%async_computation.5 | async-start | bytes 524288 | tf_op jit(solution)/shard_map/all_to_all | solution.py:670

commit v2 on v1

--- a/solution.py
+++ b/solution.py
@@ -38,54 +38,34 @@
 
 
 @functools.lru_cache(None)
-def column_forward_table(per):
+def column_tables():
     freq = 2 * np.arange(128)[:, None] + np.arange(2)[None, :]
     cos, sin = turn(freq[:, :, None] * np.arange(256), 256)
-    table = np.zeros((128, 2, 2, 2, 2, 2, 256))
-    for jhi in range(2):
-        table[:, 0, :, jhi, jhi, 0] = cos
-        table[:, 0, :, jhi, jhi, 1] = sin
-        table[:, 1, :, jhi, jhi, 0] = -sin
-        table[:, 1, :, jhi, jhi, 1] = cos
-    full = np.zeros((128, per, 1024))
-    full[:, :8] = table.reshape(128, 8, 1024)
-    return bf16_table(full.reshape(128 * per, 1024))
+    ahead = np.zeros((128, 2, 2, 2, 256))
+    ahead[:, 0, :, 0] = cos
+    ahead[:, 0, :, 1] = sin
+    ahead[:, 1, :, 0] = -sin
+    ahead[:, 1, :, 1] = cos
+    back = np.zeros((128, 2, 2, 2, 256))
+    back[:, 0, :, 0] = cos
+    back[:, 1, :, 0] = -sin
+    back[:, 0, :, 1] = sin
+    back[:, 1, :, 1] = cos
+    return bf16_table(ahead.reshape(512, 512)), bf16_table(back.reshape(512, 512))
 
 
 @functools.lru_cache(None)
-def column_inverse_table(per):
-    freq = 2 * np.arange(128)[:, None] + np.arange(2)[None, :]
-    cos, sin = turn(freq[:, :, None] * np.arange(256), 256)
-    table = np.zeros((128, 2, 2, 2, 2, 2, 256))
-    for jhi in range(2):
-        table[:, 0, :, jhi, 0, jhi] = cos
-        table[:, 1, :, jhi, 0, jhi] = -sin
-        table[:, 0, :, jhi, 1, jhi] = sin
-        table[:, 1, :, jhi, 1, jhi] = cos
-    full = np.zeros((128, per, 1024))
-    full[:, :8] = table.reshape(128, 8, 1024)
-    return bf16_table(full.reshape(128 * per, 1024))
-
-
-@functools.lru_cache(None)
-def row_block_tables(per):
+def row_block_tables():
     cos, sin = turn(np.arange(16)[:, None] * np.arange(16), 16)
-    ahead = np.zeros((2, 4, 8, 16, 16, 8, 2, 4))
-    for kj in range(4):
-        for c in range(8):
-            ahead[0, kj, c, :, :, c, 0, kj] = cos
-            ahead[0, kj, c, :, :, c, 1, kj] = sin
-            ahead[1, kj, c, :, :, c, 0, kj] = -sin
-            ahead[1, kj, c, :, :, c, 1, kj] = cos
-    back = np.conj(ahead).transpose(4, 5, 6, 7, 0, 1, 2, 3).reshape(128, 8, 1024)
-    full_ahead = np.zeros((1024, 128, per))
-    full_ahead[:, :, :8] = ahead.reshape(1024, 128, 8)
-    full_back = np.zeros((128, per, 1024))
-    full_back[:, :8] = back
-    return (
-        bf16_table(full_ahead.reshape(1024, 128 * per)),
-        bf16_table(full_back.reshape(128 * per, 1024) / IMAGE),
-    )
+    ahead = np.zeros((2, 2, 2, 16, 16, 2, 2, 2))
+    for kappa in range(2):
+        for jhi in range(2):
+            ahead[0, kappa, jhi, :, :, jhi, 0, kappa] = cos
+            ahead[0, kappa, jhi, :, :, jhi, 1, kappa] = sin
+            ahead[1, kappa, jhi, :, :, jhi, 0, kappa] = -sin
+            ahead[1, kappa, jhi, :, :, jhi, 1, kappa] = cos
+    ahead = ahead.reshape(128, 128)
+    return bf16_table(ahead), bf16_table(ahead.T / IMAGE)
 
 
 @functools.lru_cache(None)
@@ -163,11 +143,11 @@
         bf16_table(second),
         bf16_table(back),
         rows.astype(np.int32),
-        fold,
-    )
-
-
-def columns_ahead(z, twiddle_ref):
+        bf16_table(fold),
+    )
+
+
+def columns_ahead(z, twiddle_ref, table_ref):
     root = float(np.sqrt(0.5))
     s04, d04 = z[0] + z[4], z[0] - z[4]
     s26, d26 = z[2] + z[6], z[2] - z[6]
@@ -184,31 +164,54 @@
     for j in (1, 2, 3):
         real[8 - j], imag[8 - j] = real[j], -imag[j]
     groups = []
-    for jlo in range(4):
-        pieces = []
-        for jhi in range(2):
-            j = 4 * jhi + jlo
-            cos, sin = twiddle_ref[j : j + 1, :], twiddle_ref[8 + j : 9 + j, :]
-            if imag[j] is None:
-                pieces += [real[j] * cos, -real[j] * sin]
-            else:
-                pieces += [real[j] * cos + imag[j] * sin, imag[j] * cos - real[j] * sin]
+    for j in range(8):
+        cos, sin = twiddle_ref[j : j + 1, :], twiddle_ref[8 + j : 9 + j, :]
+        if imag[j] is None:
+            pieces = [real[j] * cos, -real[j] * sin]
+        else:
+            pieces = [real[j] * cos + imag[j] * sin, imag[j] * cos - real[j] * sin]
         groups.append(jnp.concatenate(pieces, axis=1).astype(BF16))
-    return jnp.concatenate(groups, axis=0)
+    values = lax.dot_general(
+        table_ref[...], jnp.concatenate(groups, axis=0), NT, preferred_element_type=F32
+    )
+    low, high = (values[:, at : at + 128].reshape(64, 8, 128) for at in (0, 128))
+    sub = lax.broadcasted_iota(jnp.int32, (64, 8, 128), 1)
+    return (
+        jnp.where(sub < 4, low, pltpu.roll(high, 4, 1)),
+        jnp.where(sub < 4, pltpu.roll(low, 4, 1), high),
+    )
+
+
+def regroup(even, odd):
+    sub = lax.broadcasted_iota(jnp.int32, even.shape, 1)
+    shape = (512, even.shape[2])
+    first = jnp.where(sub < 4, even, pltpu.roll(odd, 4, 1))
+    second = jnp.where(sub < 4, pltpu.roll(even, 4, 1), odd)
+    return jnp.concatenate([first.reshape(shape), second.reshape(shape)], 1).astype(BF16)
+
+
+def spaced(chunks):
+    gap = jnp.zeros((chunks[0].shape[0], 2, 128), F32)
+    pieces = []
+    for value in chunks:
+        pieces += [value, gap]
+    return jnp.concatenate(pieces, 1)
+
+
+def unspaced(rows):
+    rows = rows.astype(F32).reshape(32, 40, 128)
+    return [rows[:, 10 * j : 10 * j + 8] for j in range(4)]
 
 
 def columns_back(rows_of, twiddle_ref):
     real = [None] * 8
     imag = [None] * 8
-    for jlo in range(4):
-        rows = rows_of(jlo)
-        for jhi in range(2):
-            j = 4 * jhi + jlo
-            re = rows[:, jhi * 256 : jhi * 256 + 256]
-            im = rows[:, 512 + jhi * 256 : 768 + jhi * 256]
-            cos, sin = twiddle_ref[j : j + 1, :], twiddle_ref[8 + j : 9 + j, :]
-            real[j] = re * cos - im * sin
-            imag[j] = re * sin + im * cos
+    for j in range(8):
+        rows = rows_of(j)
+        re, im = rows[:, :256], rows[:, 256:]
+        cos, sin = twiddle_ref[j : j + 1, :], twiddle_ref[8 + j : 9 + j, :]
+        real[j] = re * cos - im * sin
+        imag[j] = re * sin + im * cos
     fold_re = [real[0]] + [real[j] + real[8 - j] for j in (1, 2, 3)] + [real[4]]
     fold_im = [None] + [imag[j] - imag[8 - j] for j in (1, 2, 3)]
     scale = 1.0 / IMAGE
@@ -254,18 +257,23 @@
 
 def ahead_body(strip_ref, twiddle_ref, table_ref, out_ref):
     z = [strip_ref[c, 0:2].astype(F32).reshape(32, 256) for c in range(8)]
-    values = columns_ahead(z, twiddle_ref)
-    out_ref[...] = lax.dot_general(
-        table_ref[...], values, NT, preferred_element_type=F32
-    ).astype(BF16)
+    even, odd = columns_ahead(z, twiddle_ref, table_ref)
+    out_ref[...] = jnp.stack([even, odd], 1).reshape(1024, 128).astype(BF16)
 
 
 def middle_body(window, summing, *refs):
     in_ref, spectra_ref, ahead_ref, back_ref, row_ref, back_row_ref, tw_ref, back_tw_ref = refs[:8]
     out_ref = refs[-1]
     chunks = in_ref[...]
-    first = jnp.dot(ahead_ref[...], chunks, preferred_element_type=F32).reshape(8, 8, 16, 128)
-    per_m = swap_blocks([first[:, c].reshape(128, 128) for c in range(8)], 16)
+    if summing:
+        fours = [part.reshape(16, 2, 8, 128) for part in unspaced(chunks)]
+        rows = [fours[c % 4][:, c // 4].reshape(128, 128) for c in range(8)]
+    else:
+        rows = chunks.astype(F32).reshape(16, 8, 8, 128)
+        rows = [rows[:, c].reshape(128, 128) for c in range(8)]
+    rows = jnp.concatenate(rows, 1).astype(BF16)
+    first = jnp.dot(ahead_ref[...], rows, preferred_element_type=F32)
+    per_m = swap_blocks([first[:, 128 * c : 128 * c + 128] for c in range(8)], 16)
     cos, sin = tw_ref[0:16, :], tw_ref[16:32, :]
     rows = []
     for m in range(8):
@@ -315,18 +323,18 @@
             group = [per_m[m_hi * count + i][:, cols] for i in range(count)]
             for i, value in enumerate(swap_blocks(group, window)):
                 per_c[c_hi * count + i][m_hi] = value
-    blocks = [
-        (v[0] if tiles == 1 else jnp.concatenate(v, 1)).astype(BF16).reshape(8, 1, 16, half)
-        for v in per_c
-    ]
-    rows = jnp.concatenate(blocks, 1).reshape(1024, half)
+    rows = jnp.concatenate([tile for v in per_c for tile in v], 1).astype(BF16)
     out = jnp.dot(back_ref[...], rows, preferred_element_type=F32)
+    out = [out[:, half * c : half * c + half].reshape(16, 8, half) for c in range(8)]
     if summing:
         gather_ref, share_ref = refs[8:10]
         total = jnp.dot(gather_ref[...], chunks, preferred_element_type=F32)
+        out = jnp.stack([spaced(out[:4]), spaced(out[4:])], 1).reshape(1280, 128)
         out = out + jnp.dot(
             share_ref[...], jnp.concatenate(halves(total), 0), preferred_element_type=F32
         )
+    else:
+        out = jnp.stack(out, 1).reshape(1024, half)
     out_ref[...] = out.astype(BF16)
 
 
@@ -450,12 +458,15 @@
     acc_second_ref,
 ):
     place = place_ref[0]
-    values = lax.dot_general(in_ref[...], inverse_ref[...], TN, preferred_element_type=F32)
+    chunks = in_ref[...].astype(F32).reshape(64, 2, 8, 256)
+    values = lax.dot_general(
+        regroup(chunks[:, 0], chunks[:, 1]), inverse_ref[...], TN, preferred_element_type=F32
+    )
     row = lax.broadcasted_iota(jnp.int32, (HOLD, IMAGE), 0)
     inside = ((row >= 2) | (place > 0)) & ((row < 18) | (place < DEVS - 1))
     for plane in range(2):
         blocks = columns_back(
-            lambda jlo: values[64 * jlo + 32 * plane : 64 * jlo + 32 * plane + HOLD], twiddle_ref
+            lambda j: values[64 * j + 32 * plane : 64 * j + 32 * plane + HOLD], twiddle_ref
         )
         blurred = jnp.concatenate(blocks, 1).astype(BF16).astype(F32)
         residual = dirty_ref[plane] - jnp.where(inside, blurred, 0.0)
@@ -526,15 +537,19 @@
     sums = jnp.zeros((HIDDEN, 128), F32)
     for p in range(3):
         sums = sums + jnp.dot(
-            parts[p], fold_ref[p], precision=lax.Precision.HIGHEST, preferred_element_type=F32
+            parts[p],
+            fold_ref[p].astype(F32),
+            precision=lax.Precision.HIGHEST,
+            preferred_element_type=F32,
         )
     at = lax.broadcasted_iota(jnp.int32, (HIDDEN, 128), 1)
     of = lax.broadcasted_iota(jnp.int32, (HIDDEN, 128), 0)
     for i in range(2):
         sums = jnp.where((at == 55) & (of == i), cot_sums[i], sums)
 
-    values = columns_ahead([jnp.concatenate(v, 0) for v in z], twiddle_ref)
-    out = lax.dot_general(forward_ref[...], values, NT, preferred_element_type=F32)
+    even, odd = columns_ahead([jnp.concatenate(v, 0) for v in z], twiddle_ref, forward_ref)
+    even, odd = even.reshape(32, 2, 8, 128), odd.reshape(32, 2, 8, 128)
+    out = spaced([even[:, 0], odd[:, 0], even[:, 1], odd[:, 1]]).reshape(1280, 128)
     out = out + jnp.dot(
         spread_ref[...], jnp.concatenate(halves(sums), 0), preferred_element_type=F32
     )
@@ -544,8 +559,13 @@
 def finish_body(in_ref, base_ref, twiddle_ref, inverse_ref, collect_ref, out_ref, sums_ref):
     chunks = in_ref[...]
     sums_ref[...] = jnp.dot(collect_ref[...], chunks, preferred_element_type=F32) * (1.0 / IMAGE)
-    values = lax.dot_general(chunks, inverse_ref[...], TN, preferred_element_type=F32)
-    blocks = columns_back(lambda jlo: values[32 * jlo : 32 * jlo + 32], twiddle_ref)
+    fours = unspaced(chunks)
+    even = jnp.stack([fours[0], fours[2]], 1).reshape(64, 8, 128)
+    odd = jnp.stack([fours[1], fours[3]], 1).reshape(64, 8, 128)
+    values = lax.dot_general(
+        regroup(even, odd), inverse_ref[...], TN, preferred_element_type=F32
+    )
+    blocks = columns_back(lambda j: values[32 * j : 32 * j + 32], twiddle_ref)
     for c in range(8):
         blurred = blocks[c].astype(BF16).astype(F32).reshape(2, STRIP, 256)
         out_ref[c] = base_ref[c] - blurred
@@ -576,7 +596,7 @@
 
 
 def middle(chunks, spectra, window, lead, per):
-    ahead, back = row_block_tables(per)
+    ahead, back = row_block_tables()
     twiddle, row_table = row_forward_tables()
     back_twiddle, back_row = row_inverse_tables(window, lead)
     extra = sum_tables()[1:3] if per == 10 else ()
@@ -600,7 +620,7 @@
     cells = cells.transpose(2, 0, 1, 3, 4).reshape(8, 6, STRIP, 256)
     strip = lax.all_to_all(cells, "col", 0, 0, tiled=True)
     spec = call(
-        ahead_body, like(1024, 128), strip, column_twiddle(), column_forward_table(8)
+        ahead_body, like(1024, 128), strip, column_twiddle(), column_tables()[0]
     )
     spec = exchange(spec, 8)
     above = lax.ppermute(strip[:, :, -2:], RC, [(d, d + 1) for d in range(DEVS - 1)])
@@ -643,8 +663,8 @@
         second,
         back,
         column_twiddle(),
-        column_inverse_table(8),
-        column_forward_table(10),
+        column_tables()[1],
+        column_tables()[0],
         sum_tables()[0],
         row_of,
         fold,
@@ -664,7 +684,7 @@
         mixed,
         base,
         column_twiddle(),
-        column_inverse_table(10),
+        column_tables()[1],
         sum_tables()[3],
     )
     image = lax.all_to_all(image, "col", 0, 0, tiled=True)

time: 143 us -> 134 us (0.937)
  Pallas kernels: 37.7 us -> 27.6 us
  waiting for transfers between devices: 2.03 us -> 4.3 us
  local copies, waits for them, and re-layouts: 11.7 us -> 9.56 us
    pallas_call x6, Pallas kernels: 37.7 us -> 27.6 us  [call(): pl.pallas_call(body, out_shape=outs, in_specs=[pl.BlockSpec(memory_space=...]
    all_to_all x1, waiting for transfers between devices: 1.48 us -> 4.29 us  [shards(): image = lax.all_to_all(image, 'col', 0, 0, tiled=True)]
    unnamed x15 -> x17, local copies, waits for them, and re-layouts: 3.26 us -> 3.92 us
  transfers between devices with their start and end apart: 4 -> 4, of which waited for: 2 -> 1; matrix products, arithmetic and copies ran while one was open for 6% -> 5% of each run, Pallas kernels for 2% -> 3%
where the time goes in v2:
time: 134 us; the launch traced here: 133 us
  blocking collectives  76.1 us (57%)
  Pallas kernels  27.6 us (21%)
  starting transfers between devices  14 us (10%)
  local copies, waits for them, and re-layouts  9.56 us (7%)
  waiting for transfers between devices  4.3 us (3%)
    all_to_all x3, blocking collectives, exchange(): lax.all_to_all(chunks.reshape(DEVS * per // rows, rows, width), RC, 0, 0,...  61.1 us
    pallas_call x6, Pallas kernels, call(): pl.pallas_call(body, out_shape=outs, in_specs=[pl.BlockSpec(memory_space=...  27.6 us
    all_to_all x1, blocking collectives, shards(): strip = lax.all_to_all(cells, 'col', 0, 0, tiled=True)  15 us
    all_to_all x1, starting transfers between devices, exchange(): lax.all_to_all(chunks.reshape(DEVS * per // rows, rows, width), RC, 0, 0,...  4.6 us
    ppermute x1, starting transfers between devices, shards(): lax.ppermute(strip[:, :, -2:], RC, [(d, d + 1) for d in range(DEVS - 1)])  4.55 us
    all_to_all x1, waiting for transfers between devices, shards(): image = lax.all_to_all(image, 'col', 0, 0, tiled=True)  4.29 us
    unnamed x17, local copies, waits for them, and re-layouts  3.92 us
    all_to_all x1, starting transfers between devices, shards(): image = lax.all_to_all(image, 'col', 0, 0, tiled=True)  3.54 us
  transfers between devices with their start and end apart: 4, of which 1 were waited for; matrix products, arithmetic and copies ran while one was open for 5% of the time, Pallas kernels for 3%

profile of v2, /device:TPU:0, one launch (start us, length us, event | category | flops | bytes accessed | tf_op | source)
XLA Modules:
  0.0 133.3 jit_solution(10176465298764821703)
XLA Ops:
  0.6 1.1 pad_maximum_fusion
  1.8 15.0 %all_to_all.30.strip_ref = bf16[8,6,16,256]{3,2,1,0:T(8,128)(2,1)} all-to-all(bf16[8,6,16,256]{3,2,1,0:T(8,128)(2,1)S(1)} %bitcast.30), channel_id=1, replica_groups=mesh['row'=16,'col'=8] {'col'}, dimensions={0} | all-to-all | bytes 786432 | tf_op jit(solution)/shard_map/all_to_all | solution.py:621
  16.8 2.2 %shard_map.290 = bf16[1024,128]{1,0:T(8,128)(2,1)} custom-call(bf16[8,6,16,256]{3,2,1,0:T(8,128)(2,1)} %all_to_all.30.strip_ref, f32[16,256]{1,0:T(8,128)} %constant.45.clone.twiddle_ref, bf16[512,512]{1,0:T(8,128)(2,1)} %constant.46.clone.table_ref.inverse_ref.forward_ref), custom_call_target="tpu_custom_call" | custom-call | tf_op jit(solution)/shard_map/pallas_call | solution.py:576
  19.0 19.0 %all_to_all.31 = bf16[128,8,128]{2,1,0:T(8,128)(2,1)} all-to-all(bf16[128,8,128]{2,1,0:T(8,128)(2,1)} %bitcast.36), channel_id=1, replica_groups=mesh['row'=16,'col'=8] {'row','col'}, dimensions={0} | all-to-all | bytes 524288 | tf_op jit(solution)/shard_map/all_to_all | solution.py:594
  38.0 4.0 %shard_map.291 = bf16[1024,256]{1,0:T(8,128)(2,1)} custom-call(bf16[1024,128]{1,0:T(8,128)(2,1)} %bitcast.35, f32[3,16,16,128]{3,2,1,0:T(8,128)} %refs_1_.3, bf16[128,128]{1,0:T(8,128)(2,1)} %constant.51.clone.refs_2_, bf16[128,128]{1,0:T(8,128)(2,1)} %constant.52.clone.refs_3_, bf16[128,256]{1,0:T(8,128)(2,1)} %constant.53.clone.refs_4_.refs_5_, ...), custom_call_target="tpu_custom_call" | custom-call | tf_op jit(solution)/shard_map/pallas_call | solution.py:576
  42.0 4.6 %all-to-all-start.2 = ((bf16[128,8,256]{2,1,0:T(8,128)(2,1)}), bf16[128,8,256]{2,1,0:T(8,128)(2,1)S(1)}, u32[]{:S(2)}, u32[]{:S(2)}) async-start(bf16[128,8,256]{2,1,0:T(8,128)(2,1)} %bitcast.29), calls=%async_computation.2 | async-start | bytes 1048576 | tf_op jit(solution)/shard_map/all_to_all | solution.py:594
  46.6 1.1 fusion
  47.7 0.0 copy-start.4
  47.8 1.3 collective-permute-start.1
  49.1 4.5 %collective-permute-start = (bf16[8,6,2,256]{3,2,1,0:T(2,128)(2,1)S(1)}, bf16[8,6,2,256]{3,2,1,0:T(2,128)(2,1)S(1)}, u32[]{:S(2)}, u32[]{:S(2)}) collective-permute-start(bf16[8,6,2,256]{3,2,1,0:T(2,128)(2,1)S(1)} %get-tuple-element.31), channel_id=1, source_target_pairs={{0,1},{1,2},{2,3},{3,4},{4,5},{5,6},{6,7},{7,8},{8,9},{9,10},{10,1... | collective-permute-start | bytes 147464 | tf_op jit(solution)/shard_map/ppermute | solution.py:626
  53.6 0.0 copy-done.4
  53.6 0.0 copy-start.5
  53.7 0.7 copy.44.w_first_ref
  54.4 0.0 copy-start.6
  54.4 0.7 copy-done.6
  55.0 0.7 copy.46.bias_ref
  55.7 0.0 copy-done.5
  55.7 0.7 copy.45.w_second_ref
  56.4 0.0 collective-permute-done.1.below_ref
  56.4 0.0 copy-start.2
  56.4 0.0 collective-permute-done.above_ref
  56.4 0.6 copy-done.2
  57.0 0.0 copy-start.3
  57.0 0.6 copy-done.3
  57.7 3.4 %shard_map.292 = (bf16[128,2048]{1,0:T(8,128)(2,1)}, bf16[128,2048]{1,0:T(8,128)(2,1)}, f32[2,24,2048]{2,1,0:T(8,128)}, bf16[576,256]{1,0:T(8,128)(2,1)}, bf16[5...) custom-call(bf16[8,6,16,256]{3,2,1,0:T(8,128)(2,1)} %all_to_all.30.strip_ref, bf16[8,6,2,256]{3,2,1,0:T(2,128)(2,1)} %copy-done.3, ...), custom_call_target="tpu_custom_call" | custom-call | tf_op jit(solution)/shard_map/pallas_call | solution.py:576
  61.1 0.0 all-to-all-done.2
  61.1 0.0 copy-start
  61.1 0.8 copy-done
  61.9 11.5 %shard_map.293 = (f32[8,2,16,256]{3,2,1,0:T(8,128)}, bf16[1280,128]{1,0:T(8,128)(2,1)}) custom-call(s32[1]{0:T(128)} %bitcast.place_ref, bf16[1024,256]{1,0:T(8,128)(2,1)} %bitcast.28, bf16[8,6,16,256]{3,2,1,0:T(8,128)(2,1)} %all_to_all.30.strip_ref, f32[2,24,2048]{2,1,0:T(8,128)} %get-tuple-element.15.dirty_ref, ...), custom_call_target="tpu_custom_call" | custom-call | tf_op jit(solution)/shard_map/pallas_call | solution.py:576
  73.4 24.9 %all_to_all.32 = bf16[640,2,128]{2,1,0:T(2,128)(2,1)} all-to-all(bf16[640,2,128]{2,1,0:T(2,128)(2,1)} %bitcast.37), channel_id=1, replica_groups=mesh['row'=16,'col'=8] {'row','col'}, dimensions={0} | all-to-all | bytes 655360 | tf_op jit(solution)/shard_map/all_to_all | solution.py:594
  98.3 4.0 %shard_map.294 = bf16[1280,128]{1,0:T(8,128)(2,1)} custom-call(bf16[1280,128]{1,0:T(8,128)(2,1)} %bitcast.32, f32[3,16,16,128]{3,2,1,0:T(8,128)} %refs_1_.3, bf16[128,128]{1,0:T(8,128)(2,1)} %constant.51.clone.refs_2_, bf16[128,128]{1,0:T(8,128)(2,1)} %constant.52.clone.refs_3_, bf16[128,256]{1,0:T(8,128)(2,1)} %constant.53.clone.refs_4_.refs_5_, ...), custom_call_target="tpu_custom_call" | custom-call | tf_op jit(solution)/shard_map/pallas_call | solution.py:576
  102.3 17.2 %all_to_all.33 = bf16[640,2,128]{2,1,0:T(2,128)(2,1)} all-to-all(bf16[640,2,128]{2,1,0:T(2,128)(2,1)} %bitcast.33), channel_id=1, replica_groups=mesh['row'=16,'col'=8] {'row','col'}, dimensions={0} | all-to-all | bytes 655360 | tf_op jit(solution)/shard_map/all_to_all | solution.py:594
  119.5 2.4 %shard_map.295 = (f32[8,2,16,256]{3,2,1,0:T(8,128)}, f32[32,128]{1,0:T(8,128)}) custom-call(bf16[1280,128]{1,0:T(8,128)(2,1)} %bitcast.31, f32[8,2,16,256]{3,2,1,0:T(8,128)} %get-tuple-element.22.base_ref, f32[16,256]{1,0:T(8,128)} %constant.45.clone.twiddle_ref, bf16[512,512]{1,0:T(8,128)(2,1)} %constant.46.clone.table_ref.inverse_ref.forward_ref, ...), custom_call_target="tpu_custom_call" | custom-call | tf_op jit(solution)/shard_map/pallas_call | solution.py:576
  121.9 0.0 copy-start.1
  121.9 3.5 %all-to-all-start.5 = ((f32[8,2,16,256]{3,2,1,0:T(8,128)}), f32[8,2,16,256]{3,2,1,0:T(8,128)S(1)}, u32[]{:S(2)}, u32[]{:S(2)}) async-start(f32[8,2,16,256]{3,2,1,0:T(8,128)} %get-tuple-element.23), calls=%async_computation.5 | async-start | bytes 524288 | tf_op jit(solution)/shard_map/all_to_all | solution.py:690
  125.4 0.0 copy-done.1
  125.4 0.1 slice.22
  125.5 0.1 copy.49
  125.6 0.6 copy.51
  126.2 0.1 copy.48
  126.3 0.6 copy.50
  126.9 0.7 slice_reduce_fusion.1
  127.6 0.7 slice_reduce_fusion
  128.3 4.3 %all-to-all-done.5 = f32[8,2,16,256]{3,2,1,0:T(8,128)S(1)} async-done(((f32[8,2,16,256]{3,2,1,0:T(8,128)}), f32[8,2,16,256]{3,2,1,0:T(8,128)S(1)}, u32[]{:S(2)}, u32[]{:S(2)}) %all-to-all-start.5) | async-done | bytes 262176 | tf_op jit(solution)/shard_map/all_to_all | solution.py:690
  132.6 0.7 copy.47
  (6 shorter events, 0.1 us)
Async XLA Ops:
  42.0 19.0 %all-to-all-start.2 = ((bf16[128,8,256]{2,1,0:T(8,128)(2,1)}), bf16[128,8,256]{2,1,0:T(8,128)(2,1)S(1)}, u32[]{:S(2)}, u32[]{:S(2)}) async-start(bf16[128,8,256]{2,1,0:T(8,128)(2,1)} %bitcast.29), calls=%async_computation.2 | async-start | bytes 1048576 | tf_op jit(solution)/shard_map/all_to_all | solution.py:594
  47.7 5.9 %copy-start.4 = (bf16[32,4,3,3]{0,1,3,2:T(4,128)(2,1)S(1)}, bf16[32,4,3,3]{0,1,3,2:T(4,128)(2,1)}, u32[]{:S(2)}) copy-start(bf16[32,4,3,3]{0,1,3,2:T(4,128)(2,1)} %param.30) | copy-start | bytes 6916
  47.8 8.7 %collective-permute-start.1 = (bf16[8,6,2,256]{3,2,1,0:T(2,128)(2,1)S(1)}, bf16[8,6,2,256]{3,2,1,0:T(2,128)(2,1)S(1)}, u32[]{:S(2)}, u32[]{:S(2)}) collective-permute-start(bf16[8,6,2,256]{3,2,1,0:T(2,128)(2,1)S(1)} %get-tuple-element.30), channel_id=1, source_target_pairs={{1,0},{2,1},{3,2},{4,3},{5,4},{6,5},{7,6},{8,7},{9,8},{10,9},{11,1... | collective-permute-start | bytes 147464 | tf_op jit(solution)/shard_map/ppermute | solution.py:627
  49.1 7.4 %collective-permute-start = (bf16[8,6,2,256]{3,2,1,0:T(2,128)(2,1)S(1)}, bf16[8,6,2,256]{3,2,1,0:T(2,128)(2,1)S(1)}, u32[]{:S(2)}, u32[]{:S(2)}) collective-permute-start(bf16[8,6,2,256]{3,2,1,0:T(2,128)(2,1)S(1)} %get-tuple-element.31), channel_id=1, source_target_pairs={{0,1},{1,2},{2,3},{3,4},{4,5},{5,6},{6,7},{7,8},{8,9},{9,10},{10,1... | collective-permute-start | bytes 147464 | tf_op jit(solution)/shard_map/ppermute | solution.py:626
  53.6 2.1 %copy-start.5 = (bf16[2,32,3,3]{1,0,3,2:T(2,128)(2,1)S(1)}, bf16[2,32,3,3]{1,0,3,2:T(2,128)(2,1)}, u32[]{:S(2)}) copy-start(bf16[2,32,3,3]{1,0,3,2:T(2,128)(2,1)} %param.32) | copy-start | bytes 3460
  54.4 0.7 copy-start.6
  56.4 0.6 copy-start.2
  57.0 0.6 copy-start.3
  61.1 0.8 copy-start
  121.9 3.6 %copy-start.1 = (f32[32,128]{1,0:T(8,128)S(1)}, f32[32,128]{1,0:T(8,128)}, u32[]{:S(2)}) copy-start(f32[32,128]{1,0:T(8,128)} %get-tuple-element.24) | copy-start | bytes 49156
  121.9 10.8 %all-to-all-start.5 = ((f32[8,2,16,256]{3,2,1,0:T(8,128)}), f32[8,2,16,256]{3,2,1,0:T(8,128)S(1)}, u32[]{:S(2)}, u32[]{:S(2)}) async-start(f32[8,2,16,256]{3,2,1,0:T(8,128)} %get-tuple-element.23), calls=%async_computation.5 | async-start | bytes 524288 | tf_op jit(solution)/shard_map/all_to_all | solution.py:690

commit v3 on v2

--- a/solution.py
+++ b/solution.py
@@ -10,6 +10,7 @@
 
 IMAGE = 2048
 DEVS = 128
+VM = 20
 STRIP = 16
 REACH = 20
 HOLD = 24
@@ -110,38 +111,33 @@
 
 @functools.lru_cache(None)
 def weight_tables():
-    first = np.zeros((3, 36, 256))
-    second = np.zeros((2, 3, 9, 128))
-    back = np.zeros((3, 36, 192))
+    first = np.zeros((4, 4, 256))
+    second = np.zeros((3, 2, 128))
+    back = np.zeros((3, 4, 192))
     rows = np.full((8, 256), 99)
-    for i in range(4):
-        for q in range(3):
+    fold = np.zeros((3, 384, 128), np.float32)
+    for q in range(3):
+        for i in range(4):
             at = 128 * (i // 2) + 20 * (3 * (i % 2) + q)
             rows[:, at : at + 20] = np.arange(20)
+            first[q, i, at : at + 20] = 1.0
+            back[q, i, q * 64 + i * 16 : q * 64 + i * 16 + 16] = 1.0
             for p in range(3):
-                first[p, i * 9 + p * 3 + q, at : at + 20] = 1.0
-                back[p, i * 9 + p * 3 + q, q * 64 + i * 16 : q * 64 + i * 16 + 16] = 1.0
+                fold[p, at : at + 20, (p * 3 + q) * 4 + i] = 1.0
+        for o in range(2):
+            at = 20 * (3 * o + q)
+            second[q, o, at : at + 20] = 1.0
+            for e in range(3):
+                to = 36 + ((2 - e) * 3 + 2 - q) * 2 + o
+                fold[e, 256 + at : 276 + at, to] = 1.0
     rows[:, 120] = -1
-    for o in range(2):
-        for q in range(3):
-            at = 20 * (3 * o + q)
-            for e in range(3):
-                second[o, e, (2 - e) * 3 + 2 - q, at : at + 20] = 1.0
-    fold = np.zeros((3, 384, 128), np.float32)
-    for p in range(3):
-        for i in range(4):
-            for q in range(3):
-                at = 128 * (i // 2) + 20 * (3 * (i % 2) + q)
-                fold[p, at : at + 20, p * 12 + i * 3 + q] = 1.0
-        for o in range(2):
-            for q in range(3):
-                at = 256 + 20 * (3 * o + q)
-                fold[p, at : at + 20, 36 + p * 6 + o * 3 + q] = 1.0
+    for i in range(3):
+        first[3, i, 120 + i] = 1.0
     fold[0, 120, 54] = 1.0
     return (
-        bf16_table(first),
-        bf16_table(second),
-        bf16_table(back),
+        first.astype(np.float32),
+        second.astype(np.float32),
+        back.astype(np.float32),
         rows.astype(np.int32),
         bf16_table(fold),
     )
@@ -347,17 +343,17 @@
     return jnp.where(lane == IMAGE - 1, 0.0, pltpu.roll(value, IMAGE - 1, 1))
 
 
-def banded(weights, first_row, lowest):
+def banded(weights, window_row):
     rows = []
     for r in range(GRAD_ROWS):
         total = jnp.zeros(weights[0].shape, F32)
         for p in range(3):
-            total = total + jnp.where(first_row == r + p + lowest, weights[p], 0.0)
+            total = total + jnp.where(window_row == r + p, weights[p], 0.0)
         rows.append(total)
     return jnp.concatenate(rows, 0)
 
 
-def prepare_body(
+def prepare(
     strip_ref,
     above_ref,
     below_ref,
@@ -368,12 +364,10 @@
     second_table_ref,
     back_table_ref,
     rows_ref,
-    estimate_ref,
+    features_ref,
     cot_ref,
     dirty_ref,
-    first_ref,
-    second_ref,
-    back_ref,
+    weights_ref,
     tall_ref,
     stack_ref,
 ):
@@ -394,33 +388,36 @@
                 stack_ref[at : at + 20, :] = shifted(value, q)[0:20]
             if i == 1:
                 out = jnp.where(row < 120, stack_ref[...], jnp.where(row < 123, 1.0, 0.0))
-                estimate_ref[...] = out.astype(BF16)
+                features_ref[0:128, :] = out.astype(BF16)
             if i == 5:
                 cot_ref[...] = jnp.where(row < 120, stack_ref[...], 0.0).astype(BF16)
-    w_first = w_first_ref[...]
     rows = rows_ref[0:1, :]
-    parts = [jnp.dot(w_first, first_table_ref[p], preferred_element_type=F32) for p in range(3)]
-    lanes = lax.broadcasted_iota(jnp.int32, (HIDDEN, 256), 1)
+
+    def spread(weights, table):
+        return lax.dot_general(weights, table, TN, preferred_element_type=F32)
+
+    def parts_of(source_ref, table_ref):
+        return [
+            sum(spread(source_ref[p, q].astype(F32), table_ref[q]) for q in range(3))
+            for p in range(3)
+        ]
+
     bias = bias_ref[...]
     high = bias.astype(BF16).astype(F32)
     middle = (bias - high).astype(BF16).astype(F32)
-    low = bias - high - middle
-    offset = jnp.where(
-        lanes == 120, high, jnp.where(lanes == 121, middle, jnp.where(lanes == 122, low, 0.0))
-    )
-    first = banded(parts, rows, 0) + jnp.concatenate([offset] * GRAD_ROWS, 0)
-    first_ref[...] = first.astype(BF16)
+    pieces = jnp.concatenate([high, middle, bias - high - middle, jnp.zeros_like(bias)], 0)
+    offset = spread(pieces, first_table_ref[3])
+    first = banded(parts_of(w_first_ref, first_table_ref), rows)
+    weights_ref[:, 0:256] = (first + jnp.concatenate([offset] * GRAD_ROWS, 0)).astype(BF16)
     parts = [
-        jnp.dot(w_second_ref[0], second_table_ref[0, e], preferred_element_type=F32)
-        + jnp.dot(w_second_ref[1], second_table_ref[1, e], preferred_element_type=F32)
+        sum(spread(w_second_ref[2 - e, 2 - q].astype(F32), second_table_ref[q]) for q in range(3))
         for e in range(3)
     ]
-    second_ref[...] = banded(parts, rows[:, :128], 0).astype(BF16)
-    parts = [jnp.dot(w_first, back_table_ref[p], preferred_element_type=F32) for p in range(3)]
+    weights_ref[:, 256:384] = banded(parts, rows[:, :128]).astype(BF16)
+    parts = parts_of(w_first_ref, back_table_ref)
     rows = lax.broadcasted_iota(jnp.int32, (1, 192), 1) & 15
     parts = [parts[2 - p] for p in range(3)]
-    back = banded_back(parts, rows)
-    back_ref[...] = back.T.astype(BF16)
+    weights_ref[:, 384:576] = banded_back(parts, rows).astype(BF16)
 
 
 def banded_back(parts, rows):
@@ -437,12 +434,14 @@
     place_ref,
     in_ref,
     strip_ref,
-    dirty_ref,
-    estimate_ref,
-    cot_ref,
-    first_ref,
-    second_ref,
-    back_ref,
+    above_ref,
+    below_ref,
+    w_first_ref,
+    w_second_ref,
+    bias_ref,
+    first_table_ref,
+    second_table_ref,
+    back_table_ref,
     twiddle_ref,
     inverse_ref,
     forward_ref,
@@ -456,7 +455,30 @@
     spread_grad_ref,
     acc_first_ref,
     acc_second_ref,
+    back_ref,
+    cot_ref,
+    dirty_ref,
+    weights_ref,
+    tall_ref,
 ):
+    prepare(
+        strip_ref,
+        above_ref,
+        below_ref,
+        w_first_ref,
+        w_second_ref,
+        bias_ref,
+        first_table_ref,
+        second_table_ref,
+        back_table_ref,
+        rows_ref,
+        features_ref,
+        cot_ref,
+        dirty_ref,
+        weights_ref,
+        tall_ref,
+        stack_ref,
+    )
     place = place_ref[0]
     chunks = in_ref[...].astype(F32).reshape(64, 2, 8, 256)
     values = lax.dot_general(
@@ -475,8 +497,8 @@
             at = 20 * (3 * plane + q)
             stack_ref[at : at + 20, :] = shifted(residual, q)[0:20]
     stack_ref[120:128, :] = jnp.zeros((8, IMAGE), F32)
-    features_ref[0:128, :] = estimate_ref[...]
     features_ref[128:256, :] = stack_ref[...].astype(BF16)
+    back_ref[...] = weights_ref[:, 384:576].astype(F32).T.astype(BF16)
     acc_first_ref[...] = jnp.zeros_like(acc_first_ref)
     acc_second_ref[...] = jnp.zeros_like(acc_second_ref)
     top = jnp.where(place > 0, 1.0, 0.0)
@@ -486,8 +508,8 @@
         cols = pl.ds(pl.multiple_of(step * 256, 256), 256)
         features = features_ref[:, cols]
         cots = cot_ref[:, cols]
-        preact = jnp.dot(first_ref[...], features, preferred_element_type=F32)
-        back = jnp.dot(second_ref[...], cots, preferred_element_type=F32)
+        preact = jnp.dot(weights_ref[:, 0:256], features, preferred_element_type=F32)
+        back = jnp.dot(weights_ref[:, 256:384], cots, preferred_element_type=F32)
         gate = 0.5 * jnp.tanh(0.5 * preact) + 0.5
         hidden = preact * gate
         grad_pre = back * (gate + hidden * (1.0 - gate))
@@ -556,9 +578,28 @@
     out_ref[...] = out.astype(BF16)
 
 
-def finish_body(in_ref, base_ref, twiddle_ref, inverse_ref, collect_ref, out_ref, sums_ref):
+def finish_body(
+    in_ref,
+    base_ref,
+    twiddle_ref,
+    inverse_ref,
+    collect_ref,
+    out_ref,
+    first_ref,
+    first_bias_ref,
+    second_ref,
+    second_bias_ref,
+):
     chunks = in_ref[...]
-    sums_ref[...] = jnp.dot(collect_ref[...], chunks, preferred_element_type=F32) * (1.0 / IMAGE)
+    sums = jnp.dot(collect_ref[...], chunks, preferred_element_type=F32) * (1.0 / IMAGE)
+    sums = sums.T
+    for p in range(3):
+        for q in range(3):
+            at = 3 * p + q
+            first_ref[p, q] = sums[4 * at : 4 * at + 4]
+            second_ref[p, q] = sums[36 + 2 * at : 38 + 2 * at]
+    first_bias_ref[...] = sums[54:55]
+    second_bias_ref[...] = sums[55:56, 0:2]
     fours = unspaced(chunks)
     even = jnp.stack([fours[0], fours[2]], 1).reshape(64, 8, 128)
     odd = jnp.stack([fours[1], fours[3]], 1).reshape(64, 8, 128)
@@ -571,17 +612,21 @@
         out_ref[c] = base_ref[c] - blurred
 
 
-def call(body, outs, *args, scratch=(), scalars=0, vmem=56):
+def call(body, outs, *args, scratch=(), scalars=0, after=(), cost=2):
     whole = pl.BlockSpec(memory_space=pltpu.VMEM)
     return pl.pallas_call(
         body,
         out_shape=outs,
         in_specs=[pl.BlockSpec(memory_space=pltpu.SMEM)] * scalars
-        + [whole] * (len(args) - scalars),
+        + [whole] * (len(args) - scalars)
+        + [pl.BlockSpec(memory_space=pl.ANY)] * len(after),
         out_specs=jax.tree.map(lambda _: whole, outs),
         scratch_shapes=list(scratch),
-        compiler_params=pltpu.CompilerParams(vmem_limit_bytes=vmem * 1024 * 1024),
-    )(*args)
+        compiler_params=pltpu.CompilerParams(vmem_limit_bytes=VM * 1024 * 1024),
+        cost_estimate=pl.CostEstimate(
+            flops=cost * 10**9, bytes_accessed=cost * 10**6, transcendentals=0
+        ),
+    )(*args, *after)
 
 
 def like(*shape, dtype=BF16):
@@ -595,7 +640,7 @@
     return moved.reshape(DEVS * per, width)
 
 
-def middle(chunks, spectra, window, lead, per):
+def middle(chunks, spectra, window, lead, per, after=()):
     ahead, back = row_block_tables()
     twiddle, row_table = row_forward_tables()
     back_twiddle, back_row = row_inverse_tables(window, lead)
@@ -612,6 +657,7 @@
         twiddle,
         back_twiddle,
         *extra,
+        after=after,
     )
 
 
@@ -626,29 +672,7 @@
     above = lax.ppermute(strip[:, :, -2:], RC, [(d, d + 1) for d in range(DEVS - 1)])
     below = lax.ppermute(strip[:, :, :2], RC, [(d + 1, d) for d in range(DEVS - 1)])
     first_table, second_table, back_table, row_of, fold = weight_tables()
-    im_estimate, im_cot, dirty, first, second, back = call(
-        prepare_body,
-        (
-            like(128, IMAGE),
-            like(128, IMAGE),
-            like(2, HOLD, IMAGE, dtype=F32),
-            like(576, 256),
-            like(576, 128),
-            like(192, 576),
-        ),
-        strip,
-        above,
-        below,
-        w_first.reshape(32, 36),
-        w_second.reshape(2, 32, 9),
-        b_first.reshape(32, 1),
-        first_table,
-        second_table,
-        back_table,
-        row_of,
-        scratch=[pltpu.VMEM((HOLD, IMAGE), F32), pltpu.VMEM((128, IMAGE), F32)],
-    )
-    mixed = exchange(middle(spec, psf_spectra, 32, 2, 8), 8)
+    mixed = exchange(middle(spec, psf_spectra, 32, 2, 8, ()), 8)
     place = (lax.axis_index("row") * 8 + lax.axis_index("col")).astype(jnp.int32).reshape(1)
     base, spec = call(
         network_body,
@@ -656,12 +680,14 @@
         place,
         mixed,
         strip,
-        dirty,
-        im_estimate,
-        im_cot,
-        first,
-        second,
-        back,
+        above,
+        below,
+        w_first.transpose(2, 3, 1, 0),
+        w_second.transpose(2, 3, 0, 1),
+        b_first.reshape(1, 32),
+        first_table,
+        second_table,
+        back_table,
         column_twiddle(),
         column_tables()[1],
         column_tables()[0],
@@ -674,13 +700,25 @@
             pltpu.VMEM((192, IMAGE), F32),
             pltpu.VMEM((576, 256), F32),
             pltpu.VMEM((576, 128), F32),
+            pltpu.VMEM((192, 576), BF16),
+            pltpu.VMEM((128, IMAGE), BF16),
+            pltpu.VMEM((2, HOLD, IMAGE), F32),
+            pltpu.VMEM((576, 576), BF16),
+            pltpu.VMEM((HOLD, IMAGE), F32),
         ],
         scalars=1,
+        cost=8,
     )
     mixed = exchange(middle(exchange(spec, 10), psf_spectra, 16, 0, 10), 10)
-    image, sums = call(
+    image, grad_first, first_bias, grad_second, second_bias = call(
         finish_body,
-        (like(8, 2, STRIP, 256, dtype=F32), like(32, 128, dtype=F32)),
+        (
+            like(8, 2, STRIP, 256, dtype=F32),
+            like(3, 3, 4, 32, dtype=F32),
+            like(1, 32, dtype=F32),
+            like(3, 3, 2, 32, dtype=F32),
+            like(1, 2, dtype=F32),
+        ),
         mixed,
         base,
         column_twiddle(),
@@ -689,9 +727,13 @@
     )
     image = lax.all_to_all(image, "col", 0, 0, tiled=True)
     grad_image = image.transpose(1, 0, 2, 3).reshape(2, 128, 256)
-    grad_first = sums[:, :36].reshape(32, 3, 4, 3).transpose(0, 2, 1, 3)
-    grad_second = jnp.flip(sums[:, 36:54].reshape(32, 3, 2, 3), (1, 3)).transpose(2, 0, 1, 3)
-    return grad_image, grad_first, sums[:, 54], grad_second, sums[:2, 55]
+    return (
+        grad_image,
+        grad_first.transpose(3, 2, 0, 1),
+        first_bias.reshape(32),
+        grad_second.transpose(2, 3, 0, 1),
+        second_bias.reshape(2),
+    )
 
 
 def solution(mesh):

time: 134 us -> 116 us (0.87)
  Pallas kernels: 27.6 us -> 15.7 us
  local copies, waits for them, and re-layouts: 9.56 us -> 1.56 us
  waiting for transfers between devices: 4.3 us -> 8.2 us
  starting transfers between devices: 14 us -> 10.6 us
  blocking collectives: 76.1 us -> 77.8 us
    pallas_call x6 -> x5, Pallas kernels: 27.6 us -> 15.7 us  [call(): pl.pallas_call(body, out_shape=outs, in_specs=[pl.BlockSpec(memory_space=...]
    all_to_all x0 -> x1, blocking collectives: none -> 9.68 us  [shards(): image = lax.all_to_all(image, 'col', 0, 0, tiled=True)]
    all_to_all x3, blocking collectives: 61.1 us -> 53.1 us  [exchange(): lax.all_to_all(chunks.reshape(DEVS * per // rows, rows, width), RC, 0, 0,...]
    all_to_all x1, waiting for transfers between devices: 0.01 us -> 6.39 us  [exchange(): lax.all_to_all(chunks.reshape(DEVS * per // rows, rows, width), RC, 0, 0,...]
    all_to_all x1 -> x0, waiting for transfers between devices: 4.29 us -> none  [shards(): image = lax.all_to_all(image, 'col', 0, 0, tiled=True)]
    all_to_all x1 -> x0, starting transfers between devices: 3.54 us -> none  [shards(): image = lax.all_to_all(image, 'col', 0, 0, tiled=True)]
    unnamed x17 -> x42, local copies, waits for them, and re-layouts: 3.92 us -> 0.72 us
    reshape x6 -> x0, local copies, waits for them, and re-layouts: 2.12 us -> none  [the longest x2 0.71 us: shards(): w_first.reshape(32, 36)]
  transfers between devices with their start and end apart: 4 -> 3, of which waited for: 1 -> 2; matrix products, arithmetic and copies ran while one was open for 5% -> 0% of each run, Pallas kernels for 3% -> 0%
where the time goes in v3:
time: 116 us
  blocking collectives  77.8 us (67%)
  Pallas kernels  15.7 us (14%)
  starting transfers between devices  10.6 us (9%)
  waiting for transfers between devices  8.2 us (7%)
  local copies, waits for them, and re-layouts  1.56 us (1%)
    all_to_all x3, blocking collectives, exchange(): lax.all_to_all(chunks.reshape(DEVS * per // rows, rows, width), RC, 0, 0,...  53.1 us
    pallas_call x5, Pallas kernels, call(): pl.pallas_call(body, out_shape=outs, in_specs=[pl.BlockSpec(memory_space=...  15.7 us
    all_to_all x1, blocking collectives, shards(): strip = lax.all_to_all(cells, 'col', 0, 0, tiled=True)  15 us
    all_to_all x1, blocking collectives, shards(): image = lax.all_to_all(image, 'col', 0, 0, tiled=True)  9.68 us
    all_to_all x1, waiting for transfers between devices, exchange(): lax.all_to_all(chunks.reshape(DEVS * per // rows, rows, width), RC, 0, 0,...  6.39 us
    all_to_all x1, starting transfers between devices, exchange(): lax.all_to_all(chunks.reshape(DEVS * per // rows, rows, width), RC, 0, 0,...  4.74 us
    ppermute x1, starting transfers between devices, shards(): lax.ppermute(strip[:, :, -2:], RC, [(d, d + 1) for d in range(DEVS - 1)])  4.55 us
  transfers between devices with their start and end apart: 3, of which 2 were waited for; matrix products, arithmetic and copies ran while one was open for 0% of the time, Pallas kernels for 0%

profile of v3, /device:TPU:0, one launch (start us, length us, event | category | flops | bytes accessed | tf_op | source)
XLA Modules:
  0.0 115.9 jit_solution(7360676627548605920)
XLA Ops:
  0.6 1.1 pad_maximum_fusion
  1.8 0.0 copy-start.4
  1.8 0.0 copy-start.15
  1.8 15.0 %all_to_all.30.strip_ref = bf16[8,6,16,256]{3,2,1,0:T(8,128)(2,1)S(1)} all-to-all(bf16[8,6,16,256]{3,2,1,0:T(8,128)(2,1)S(1)} %bitcast.34), channel_id=1, replica_groups=mesh['row'=16,'col'=8] {'col'}, dimensions={0} | all-to-all | bytes 786432 | tf_op jit(solution)/shard_map/all_to_all | solution.py:667
  16.8 0.0 copy-done.4
  16.8 0.0 copy-done.15
  16.8 0.0 copy-start.10
  16.8 0.0 copy-start.12
  16.8 0.0 copy-start.13
  16.9 0.0 copy-start.14
  16.9 0.0 copy-start.16
  16.9 0.4 shard_map.290
  17.2 0.0 copy-start
  17.3 0.0 copy-start.8
  17.3 18.7 %all_to_all.31 = bf16[128,8,128]{2,1,0:T(8,128)(2,1)S(1)} all-to-all(bf16[128,8,128]{2,1,0:T(8,128)(2,1)S(1)} %bitcast.30), channel_id=1, replica_groups=mesh['row'=16,'col'=8] {'row','col'}, dimensions={0} | all-to-all | bytes 524288 | tf_op jit(solution)/shard_map/all_to_all | solution.py:639
  35.9 0.0 copy-done.10
  35.9 0.0 copy-done.12
  35.9 0.0 copy-done.13
  35.9 0.0 copy-done.14
  36.0 0.0 copy-done.16
  36.0 0.0 copy-done
  36.0 0.0 copy-done.8
  36.0 2.9 %shard_map.291 = bf16[1024,256]{1,0:T(8,128)(2,1)} custom-call(bf16[1024,128]{1,0:T(8,128)(2,1)S(1)} %bitcast.29, f32[3,16,16,128]{3,2,1,0:T(8,128)S(1)} %copy-done, bf16[128,128]{1,0:T(8,128)(2,1)S(1)} %copy-done.13, bf16[128,128]{1,0:T(8,128)(2,1)S(1)} %copy-done.12, bf16[128,256]{1,0:T(8,128)(2,1)S(1)} %copy-done.10, bf16[128,512]{1,0:T(8,128)(2,1)S(1)} %copy-done.8, ...), custom_call_target="tpu_custom_call" | custom-call | flops 2000000000 | bytes 2000000 | tf_op jit(solution)/shard_map/pallas_call | solution.py:617
  38.9 0.0 copy-start.6
  38.9 0.0 copy-start.7
  38.9 4.7 %all-to-all-start.2 = ((bf16[128,8,256]{2,1,0:T(8,128)(2,1)}), bf16[128,8,256]{2,1,0:T(8,128)(2,1)S(1)}, u32[]{:S(2)}, u32[]{:S(2)}) async-start(bf16[128,8,256]{2,1,0:T(8,128)(2,1)} %bitcast.8), calls=%async_computation.2 | async-start | bytes 1048576 | tf_op jit(solution)/shard_map/all_to_all | solution.py:639
  43.6 0.0 copy-start.17
  43.7 0.0 copy-start.19
  43.7 0.0 copy-start.20
  43.7 0.1 fusion
  43.8 1.3 %collective-permute-start.1 = (bf16[8,6,2,256]{3,2,1,0:T(2,128)(2,1)S(1)}, bf16[8,6,2,256]{3,2,1,0:T(2,128)(2,1)S(1)}, u32[]{:S(2)}, u32[]{:S(2)}) collective-permute-start(bf16[8,6,2,256]{3,2,1,0:T(2,128)(2,1)S(1)} %get-tuple-element.19), channel_id=1, source_target_pairs={{1,0},{2,1},{3,2},{4,3},{5,4},{6,5},{7,6},{8,7},{9,8},{10,9},{11,1... | collective-permute-start | bytes 147464 | tf_op jit(solution)/shard_map/ppermute | solution.py:673
  45.1 0.0 copy-start.18
  45.1 4.5 %collective-permute-start = (bf16[8,6,2,256]{3,2,1,0:T(2,128)(2,1)S(1)}, bf16[8,6,2,256]{3,2,1,0:T(2,128)(2,1)S(1)}, u32[]{:S(2)}, u32[]{:S(2)}) collective-permute-start(bf16[8,6,2,256]{3,2,1,0:T(2,128)(2,1)S(1)} %get-tuple-element.20), channel_id=1, source_target_pairs={{0,1},{1,2},{2,3},{3,4},{4,5},{5,6},{6,7},{7,8},{8,9},{9,10},{10,1... | collective-permute-start | bytes 147464 | tf_op jit(solution)/shard_map/ppermute | solution.py:672
  49.6 0.0 copy-start.1
  49.7 0.0 copy-start.2
  49.7 1.8 %collective-permute-done.1.below_ref = bf16[8,6,2,256]{3,2,1,0:T(2,128)(2,1)S(1)} collective-permute-done((bf16[8,6,2,256]{3,2,1,0:T(2,128)(2,1)S(1)}, bf16[8,6,2,256]{3,2,1,0:T(2,128)(2,1)S(1)}, u32[]{:S(2)}, u32[]{:S(2)}) %collective-permute-start.1) | collective-permute-done | bytes 49184 | tf_op jit(solution)/shard_map/ppermute | solution.py:673
  51.5 0.0 collective-permute-done.above_ref
  51.5 6.4 %all-to-all-done.2 = bf16[128,8,256]{2,1,0:T(8,128)(2,1)S(1)} async-done(((bf16[128,8,256]{2,1,0:T(8,128)(2,1)}), bf16[128,8,256]{2,1,0:T(8,128)(2,1)S(1)}, u32[]{:S(2)}, u32[]{:S(2)}) %all-to-all-start.2) | async-done | bytes 524320 | tf_op jit(solution)/shard_map/all_to_all | solution.py:639
  57.9 0.0 copy-start.3
  57.9 0.0 copy-done.6
  57.9 0.0 copy-done.7
  57.9 0.0 copy-done.17
  57.9 0.0 copy-done.19
  57.9 0.0 copy-done.20
  57.9 0.0 copy-done.18
  57.9 0.0 copy-done.1
  57.9 0.0 copy-done.2
  57.9 0.6 copy-done.3
  58.5 9.5 %shard_map.292 = (f32[8,2,16,256]{3,2,1,0:T(8,128)S(1)}, bf16[1280,128]{1,0:T(8,128)(2,1)S(1)}) custom-call(s32[1]{0:T(128)} %bitcast.place_ref, bf16[1024,256]{1,0:T(8,128)(2,1)S(1)} %bitcast.24, bf16[8,6,16,256]{3,2,1,0:T(8,128)(2,1)S(1)} %all_to_all.30.strip_ref, bf16[8,6,2,256]{3,2,1,0:T(2,128)(2,1)S(1)} %collective-permute-done.above_ref, ...), custom_call_target="tpu_custom_call" | custom-call | flops 8000000000 | bytes 8000000 | tf_op jit(solution)/shard_map/pallas_call | solution.py:617
  68.0 0.0 copy-start.5
  68.0 0.0 copy-start.11
  68.0 18.7 %all_to_all.32 = bf16[640,2,128]{2,1,0:T(2,128)(2,1)S(1)} all-to-all(bf16[640,2,128]{2,1,0:T(2,128)(2,1)S(1)} %bitcast.25), channel_id=1, replica_groups=mesh['row'=16,'col'=8] {'row','col'}, dimensions={0} | all-to-all | bytes 655360 | tf_op jit(solution)/shard_map/all_to_all | solution.py:639
  86.7 0.0 copy-done.5
  86.7 0.0 copy-done.11
  86.7 1.9 %shard_map.293 = bf16[1280,128]{1,0:T(8,128)(2,1)S(1)} custom-call(bf16[1280,128]{1,0:T(8,128)(2,1)S(1)} %bitcast.27, f32[3,16,16,128]{3,2,1,0:T(8,128)S(1)} %copy-done, bf16[128,128]{1,0:T(8,128)(2,1)S(1)} %copy-done.13, bf16[128,128]{1,0:T(8,128)(2,1)S(1)} %copy-done.12, bf16[128,256]{1,0:T(8,128)(2,1)S(1)} %copy-done.10, bf16[128,256]{1,0:T(8,128)(2,1)S(1)} %copy-done.10, ...), custom_call_target="tpu_custom_call" | custom-call | flops 2000000000 | bytes 2000000 | tf_op jit(solution)/shard_map/pallas_call | solution.py:617
  88.6 0.0 copy-start.9
  88.7 15.8 %all_to_all.33 = bf16[640,2,128]{2,1,0:T(2,128)(2,1)S(1)} all-to-all(bf16[640,2,128]{2,1,0:T(2,128)(2,1)S(1)} %bitcast.28), channel_id=1, replica_groups=mesh['row'=16,'col'=8] {'row','col'}, dimensions={0} | all-to-all | bytes 655360 | tf_op jit(solution)/shard_map/all_to_all | solution.py:639
  104.4 0.0 copy-done.9
  104.4 1.1 shard_map.294
  105.5 9.7 %all_to_all.34 = f32[8,2,16,256]{3,2,1,0:T(8,128)S(1)} all-to-all(f32[8,2,16,256]{3,2,1,0:T(8,128)S(1)} %get-tuple-element.14), channel_id=1, replica_groups=mesh['row'=16,'col'=8] {'col'}, dimensions={0} | all-to-all | bytes 524288 | tf_op jit(solution)/shard_map/all_to_all | solution.py:728
  115.2 0.7 copy.38
  (1 shorter events, 0.0 us)
Async XLA Ops:
  1.8 15.1 %copy-start.4 = (bf16[512,512]{1,0:T(8,128)(2,1)S(1)}, bf16[512,512]{1,0:T(8,128)(2,1)}, u32[]{:S(2)}) copy-start(bf16[512,512]{1,0:T(8,128)(2,1)} %constant.46.clone.table_ref.inverse_ref.forward_ref) | copy-start | bytes 1572868
  1.8 15.1 %copy-start.15 = (f32[16,256]{1,0:T(8,128)S(1)}, f32[16,256]{1,0:T(8,128)}, u32[]{:S(2)}) copy-start(f32[16,256]{1,0:T(8,128)} %constant.45.clone.twiddle_ref) | copy-start | bytes 49156
  16.8 19.1 %copy-start.10 = (bf16[128,256]{1,0:T(8,128)(2,1)S(1)}, bf16[128,256]{1,0:T(8,128)(2,1)}, u32[]{:S(2)}) copy-start(bf16[128,256]{1,0:T(8,128)(2,1)} %constant.49.clone.refs_4_.refs_5_) | copy-start | bytes 196612
  16.8 19.1 %copy-start.12 = (bf16[128,128]{1,0:T(8,128)(2,1)S(1)}, bf16[128,128]{1,0:T(8,128)(2,1)}, u32[]{:S(2)}) copy-start(bf16[128,128]{1,0:T(8,128)(2,1)} %constant.48.clone.refs_3_) | copy-start | bytes 98308
  16.8 19.1 %copy-start.13 = (bf16[128,128]{1,0:T(8,128)(2,1)S(1)}, bf16[128,128]{1,0:T(8,128)(2,1)}, u32[]{:S(2)}) copy-start(bf16[128,128]{1,0:T(8,128)(2,1)} %constant.47.clone.refs_2_) | copy-start | bytes 98308
  16.9 19.1 %copy-start.14 = (f32[32,256]{1,0:T(8,128)S(1)}, f32[32,256]{1,0:T(8,128)}, u32[]{:S(2)}) copy-start(f32[32,256]{1,0:T(8,128)} %constant.52.clone.refs_7_) | copy-start | bytes 98308
  16.9 19.1 %copy-start.16 = (f32[32,128]{1,0:T(8,128)S(1)}, f32[32,128]{1,0:T(8,128)}, u32[]{:S(2)}) copy-start(f32[32,128]{1,0:T(8,128)} %constant.51.clone.refs_6_.refs_7_) | copy-start | bytes 49156
  17.2 18.7 %copy-start = (f32[3,16,16,128]{3,2,1,0:T(8,128)S(1)}, f32[3,16,16,128]{3,2,1,0:T(8,128)}, u32[]{:S(2)}) copy-start(f32[3,16,16,128]{3,2,1,0:T(8,128)} %refs_1_.3) | copy-start | bytes 1179652
  17.3 18.7 %copy-start.8 = (bf16[128,512]{1,0:T(8,128)(2,1)S(1)}, bf16[128,512]{1,0:T(8,128)(2,1)}, u32[]{:S(2)}) copy-start(bf16[128,512]{1,0:T(8,128)(2,1)} %constant.50.clone.refs_5_) | copy-start | bytes 393220
  38.9 19.0 %copy-start.6 = (bf16[1280,64]{1,0:T(8,128)(2,1)S(1)}, bf16[1280,64]{1,0:T(8,128)(2,1)}, u32[]{:S(2)}) copy-start(bf16[1280,64]{1,0:T(8,128)(2,1)} %constant.56.clone.spread_ref) | copy-start | bytes 491524
  38.9 19.0 %copy-start.7 = (bf16[3,384,128]{2,1,0:T(8,128)(2,1)S(1)}, bf16[3,384,128]{2,1,0:T(8,128)(2,1)}, u32[]{:S(2)}) copy-start(bf16[3,384,128]{2,1,0:T(8,128)(2,1)} %constant.58.clone.fold_ref) | copy-start | bytes 884740
  38.9 19.0 %all-to-all-start.2 = ((bf16[128,8,256]{2,1,0:T(8,128)(2,1)}), bf16[128,8,256]{2,1,0:T(8,128)(2,1)S(1)}, u32[]{:S(2)}, u32[]{:S(2)}) async-start(bf16[128,8,256]{2,1,0:T(8,128)(2,1)} %bitcast.8), calls=%async_computation.2 | async-start | bytes 1048576 | tf_op jit(solution)/shard_map/all_to_all | solution.py:639
  43.6 14.2 %copy-start.17 = (f32[4,4,256]{2,1,0:T(4,128)S(1)}, f32[4,4,256]{2,1,0:T(4,128)}, u32[]{:S(2)}) copy-start(f32[4,4,256]{2,1,0:T(4,128)} %constant.53.clone.first_table_ref) | copy-start | bytes 49156
  43.7 14.2 %copy-start.19 = (s32[8,256]{1,0:T(8,128)S(1)}, s32[8,256]{1,0:T(8,128)}, u32[]{:S(2)}) copy-start(s32[8,256]{1,0:T(8,128)} %constant.57.clone.rows_ref) | copy-start | bytes 24580
  43.7 14.2 %copy-start.20 = (f32[3,2,128]{2,1,0:T(2,128)S(1)}, f32[3,2,128]{2,1,0:T(2,128)}, u32[]{:S(2)}) copy-start(f32[3,2,128]{2,1,0:T(2,128)} %constant.54.clone.second_table_ref) | copy-start | bytes 9220
  43.8 7.7 %collective-permute-start.1 = (bf16[8,6,2,256]{3,2,1,0:T(2,128)(2,1)S(1)}, bf16[8,6,2,256]{3,2,1,0:T(2,128)(2,1)S(1)}, u32[]{:S(2)}, u32[]{:S(2)}) collective-permute-start(bf16[8,6,2,256]{3,2,1,0:T(2,128)(2,1)S(1)} %get-tuple-element.19), channel_id=1, source_target_pairs={{1,0},{2,1},{3,2},{4,3},{5,4},{6,5},{7,6},{8,7},{9,8},{10,9},{11,1... | collective-permute-start | bytes 147464 | tf_op jit(solution)/shard_map/ppermute | solution.py:673
  45.1 12.8 %copy-start.18 = (f32[3,4,192]{2,1,0:T(4,128)S(1)}, f32[3,4,192]{2,1,0:T(4,128)}, u32[]{:S(2)}) copy-start(f32[3,4,192]{2,1,0:T(4,128)} %constant.55.clone.back_table_ref) | copy-start | bytes 27652
  45.1 6.4 %collective-permute-start = (bf16[8,6,2,256]{3,2,1,0:T(2,128)(2,1)S(1)}, bf16[8,6,2,256]{3,2,1,0:T(2,128)(2,1)S(1)}, u32[]{:S(2)}, u32[]{:S(2)}) collective-permute-start(bf16[8,6,2,256]{3,2,1,0:T(2,128)(2,1)S(1)} %get-tuple-element.20), channel_id=1, source_target_pairs={{0,1},{1,2},{2,3},{3,4},{4,5},{5,6},{6,7},{7,8},{8,9},{9,10},{10,1... | collective-permute-start | bytes 147464 | tf_op jit(solution)/shard_map/ppermute | solution.py:672
  49.6 8.3 %copy-start.1 = (bf16[32,4,3,3]{0,1,3,2:T(4,128)(2,1)S(1)}, bf16[32,4,3,3]{0,1,3,2:T(4,128)(2,1)}, u32[]{:S(2)}) copy-start(bf16[32,4,3,3]{0,1,3,2:T(4,128)(2,1)} %param.30) | copy-start | bytes 6916
  49.7 8.3 %copy-start.2 = (bf16[2,32,3,3]{1,0,3,2:T(2,128)(2,1)S(1)}, bf16[2,32,3,3]{1,0,3,2:T(2,128)(2,1)}, u32[]{:S(2)}) copy-start(bf16[2,32,3,3]{1,0,3,2:T(2,128)(2,1)} %param.32) | copy-start | bytes 3460
  57.9 0.7 copy-start.3
  68.0 18.7 %copy-start.5 = (bf16[1280,32]{1,0:T(8,128)(2,1)S(1)}, bf16[1280,32]{1,0:T(8,128)(2,1)}, u32[]{:S(2)}) copy-start(bf16[1280,32]{1,0:T(8,128)(2,1)} %constant.60.clone.refs_9_) | copy-start | bytes 245764
  68.0 18.7 %copy-start.11 = (bf16[16,1280]{1,0:T(8,128)(2,1)S(1)}, bf16[16,1280]{1,0:T(8,128)(2,1)}, u32[]{:S(2)}) copy-start(bf16[16,1280]{1,0:T(8,128)(2,1)} %constant.59.clone.refs_8_) | copy-start | bytes 122884
  88.6 15.8 %copy-start.9 = (bf16[32,1280]{1,0:T(8,128)(2,1)S(1)}, bf16[32,1280]{1,0:T(8,128)(2,1)}, u32[]{:S(2)}) copy-start(bf16[32,1280]{1,0:T(8,128)(2,1)} %constant.61.clone.collect_ref) | copy-start | bytes 245764

commit v4 on v3

--- a/solution.py
+++ b/solution.py
@@ -408,12 +408,13 @@
     pieces = jnp.concatenate([high, middle, bias - high - middle, jnp.zeros_like(bias)], 0)
     offset = spread(pieces, first_table_ref[3])
     first = banded(parts_of(w_first_ref, first_table_ref), rows)
-    weights_ref[:, 0:256] = (first + jnp.concatenate([offset] * GRAD_ROWS, 0)).astype(BF16)
+    first = first + jnp.concatenate([offset] * GRAD_ROWS, 0)
+    weights_ref[:, 0:256] = (0.5 * first).astype(BF16)
     parts = [
         sum(spread(w_second_ref[2 - e, 2 - q].astype(F32), second_table_ref[q]) for q in range(3))
         for e in range(3)
     ]
-    weights_ref[:, 256:384] = banded(parts, rows[:, :128]).astype(BF16)
+    weights_ref[:, 256:384] = (0.5 * banded(parts, rows[:, :128])).astype(BF16)
     parts = parts_of(w_first_ref, back_table_ref)
     rows = lax.broadcasted_iota(jnp.int32, (1, 192), 1) & 15
     parts = [parts[2 - p] for p in range(3)]
@@ -505,14 +506,15 @@
     bottom = jnp.where(place < DEVS - 1, 1.0, 0.0)
 
     def block(step, carry):
-        cols = pl.ds(pl.multiple_of(step * 256, 256), 256)
+        cols = pl.ds(pl.multiple_of(step * 512, 512), 512)
         features = features_ref[:, cols]
         cots = cot_ref[:, cols]
         preact = jnp.dot(weights_ref[:, 0:256], features, preferred_element_type=F32)
         back = jnp.dot(weights_ref[:, 256:384], cots, preferred_element_type=F32)
-        gate = 0.5 * jnp.tanh(0.5 * preact) + 0.5
+        bend = jnp.tanh(preact)
+        gate = 1.0 + bend
         hidden = preact * gate
-        grad_pre = back * (gate + hidden * (1.0 - gate))
+        grad_pre = back * gate * (1.0 + preact * (1.0 - bend))
         grad_pre = jnp.concatenate(
             [grad_pre[0:32] * top, grad_pre[32:544], grad_pre[544:576] * bottom], 0
         ).astype(BF16)
@@ -523,7 +525,7 @@
         )
         return carry
 
-    lax.fori_loop(0, 8, block, 0)
+    lax.fori_loop(0, 4, block, 0, unroll=True)
 
     cot_sums = []
     z = [[None, None] for _ in range(8)]

time: 116 us -> 113 us (0.974)
  Pallas kernels: 15.7 us -> 12.6 us
    pallas_call x5, Pallas kernels: 15.7 us -> 12.6 us  [call(): pl.pallas_call(body, out_shape=outs, in_specs=[pl.BlockSpec(memory_space=...]
where the time goes in v4:
time: 113 us
  blocking collectives  77.8 us (69%)
  Pallas kernels  12.6 us (11%)
  starting transfers between devices  10.6 us (9%)
  waiting for transfers between devices  8.2 us (7%)
  local copies, waits for them, and re-layouts  1.56 us (1%)
    all_to_all x3, blocking collectives, exchange(): lax.all_to_all(chunks.reshape(DEVS * per // rows, rows, width), RC, 0, 0,...  53.1 us
    all_to_all x1, blocking collectives, shards(): strip = lax.all_to_all(cells, 'col', 0, 0, tiled=True)  15 us
    pallas_call x5, Pallas kernels, call(): pl.pallas_call(body, out_shape=outs, in_specs=[pl.BlockSpec(memory_space=...  12.6 us
    all_to_all x1, blocking collectives, shards(): image = lax.all_to_all(image, 'col', 0, 0, tiled=True)  9.68 us
    all_to_all x1, waiting for transfers between devices, exchange(): lax.all_to_all(chunks.reshape(DEVS * per // rows, rows, width), RC, 0, 0,...  6.39 us
    all_to_all x1, starting transfers between devices, exchange(): lax.all_to_all(chunks.reshape(DEVS * per // rows, rows, width), RC, 0, 0,...  4.74 us
    ppermute x1, starting transfers between devices, shards(): lax.ppermute(strip[:, :, -2:], RC, [(d, d + 1) for d in range(DEVS - 1)])  4.55 us
  transfers between devices with their start and end apart: 3, of which 2 were waited for; matrix products, arithmetic and copies ran while one was open for 0% of the time, Pallas kernels for 0%

profile of v4, /device:TPU:0, one launch (start us, length us, event | category | flops | bytes accessed | tf_op | source)
XLA Modules:
  0.0 112.8 jit_solution(10282015984753730660)
XLA Ops:
  0.6 1.1 pad_maximum_fusion
  1.8 0.0 copy-start.4
  1.8 0.0 copy-start.15
  1.8 15.0 %all_to_all.30.strip_ref = bf16[8,6,16,256]{3,2,1,0:T(8,128)(2,1)S(1)} all-to-all(bf16[8,6,16,256]{3,2,1,0:T(8,128)(2,1)S(1)} %bitcast.34), channel_id=1, replica_groups=mesh['row'=16,'col'=8] {'col'}, dimensions={0} | all-to-all | bytes 786432 | tf_op jit(solution)/shard_map/all_to_all | solution.py:669
  16.8 0.0 copy-done.4
  16.8 0.0 copy-done.15
  16.8 0.0 copy-start.10
  16.8 0.0 copy-start.12
  16.8 0.0 copy-start.13
  16.9 0.0 copy-start.14
  16.9 0.0 copy-start.16
  16.9 0.4 shard_map.290
  17.3 0.0 copy-start
  17.3 0.0 copy-start.8
  17.3 18.7 %all_to_all.31 = bf16[128,8,128]{2,1,0:T(8,128)(2,1)S(1)} all-to-all(bf16[128,8,128]{2,1,0:T(8,128)(2,1)S(1)} %bitcast.30), channel_id=1, replica_groups=mesh['row'=16,'col'=8] {'row','col'}, dimensions={0} | all-to-all | bytes 524288 | tf_op jit(solution)/shard_map/all_to_all | solution.py:641
  35.9 0.0 copy-done.10
  35.9 0.0 copy-done.12
  35.9 0.0 copy-done.13
  35.9 0.0 copy-done.14
  36.0 0.0 copy-done.16
  36.0 0.0 copy-done
  36.0 0.0 copy-done.8
  36.0 2.9 %shard_map.291 = bf16[1024,256]{1,0:T(8,128)(2,1)} custom-call(bf16[1024,128]{1,0:T(8,128)(2,1)S(1)} %bitcast.29, f32[3,16,16,128]{3,2,1,0:T(8,128)S(1)} %copy-done, bf16[128,128]{1,0:T(8,128)(2,1)S(1)} %copy-done.13, bf16[128,128]{1,0:T(8,128)(2,1)S(1)} %copy-done.12, bf16[128,256]{1,0:T(8,128)(2,1)S(1)} %copy-done.10, bf16[128,512]{1,0:T(8,128)(2,1)S(1)} %copy-done.8, ...), custom_call_target="tpu_custom_call" | custom-call | flops 2000000000 | bytes 2000000 | tf_op jit(solution)/shard_map/pallas_call | solution.py:619
  38.9 0.0 copy-start.6
  38.9 0.0 copy-start.7
  38.9 4.7 %all-to-all-start.2 = ((bf16[128,8,256]{2,1,0:T(8,128)(2,1)}), bf16[128,8,256]{2,1,0:T(8,128)(2,1)S(1)}, u32[]{:S(2)}, u32[]{:S(2)}) async-start(bf16[128,8,256]{2,1,0:T(8,128)(2,1)} %bitcast.8), calls=%async_computation.2 | async-start | bytes 1048576 | tf_op jit(solution)/shard_map/all_to_all | solution.py:641
  43.6 0.0 copy-start.17
  43.7 0.0 copy-start.19
  43.7 0.0 copy-start.20
  43.7 0.1 fusion
  43.8 1.3 %collective-permute-start.1 = (bf16[8,6,2,256]{3,2,1,0:T(2,128)(2,1)S(1)}, bf16[8,6,2,256]{3,2,1,0:T(2,128)(2,1)S(1)}, u32[]{:S(2)}, u32[]{:S(2)}) collective-permute-start(bf16[8,6,2,256]{3,2,1,0:T(2,128)(2,1)S(1)} %get-tuple-element.19), channel_id=1, source_target_pairs={{1,0},{2,1},{3,2},{4,3},{5,4},{6,5},{7,6},{8,7},{9,8},{10,9},{11,1... | collective-permute-start | bytes 147464 | tf_op jit(solution)/shard_map/ppermute | solution.py:675
  45.1 0.0 copy-start.18
  45.1 4.5 %collective-permute-start = (bf16[8,6,2,256]{3,2,1,0:T(2,128)(2,1)S(1)}, bf16[8,6,2,256]{3,2,1,0:T(2,128)(2,1)S(1)}, u32[]{:S(2)}, u32[]{:S(2)}) collective-permute-start(bf16[8,6,2,256]{3,2,1,0:T(2,128)(2,1)S(1)} %get-tuple-element.20), channel_id=1, source_target_pairs={{0,1},{1,2},{2,3},{3,4},{4,5},{5,6},{6,7},{7,8},{8,9},{9,10},{10,1... | collective-permute-start | bytes 147464 | tf_op jit(solution)/shard_map/ppermute | solution.py:674
  49.6 0.0 copy-start.1
  49.7 0.0 copy-start.2
  49.7 1.8 %collective-permute-done.1.below_ref = bf16[8,6,2,256]{3,2,1,0:T(2,128)(2,1)S(1)} collective-permute-done((bf16[8,6,2,256]{3,2,1,0:T(2,128)(2,1)S(1)}, bf16[8,6,2,256]{3,2,1,0:T(2,128)(2,1)S(1)}, u32[]{:S(2)}, u32[]{:S(2)}) %collective-permute-start.1) | collective-permute-done | bytes 49184 | tf_op jit(solution)/shard_map/ppermute | solution.py:675
  51.5 0.0 collective-permute-done.above_ref
  51.5 6.4 %all-to-all-done.2 = bf16[128,8,256]{2,1,0:T(8,128)(2,1)S(1)} async-done(((bf16[128,8,256]{2,1,0:T(8,128)(2,1)}), bf16[128,8,256]{2,1,0:T(8,128)(2,1)S(1)}, u32[]{:S(2)}, u32[]{:S(2)}) %all-to-all-start.2) | async-done | bytes 524320 | tf_op jit(solution)/shard_map/all_to_all | solution.py:641
  57.9 0.0 copy-start.3
  57.9 0.0 copy-done.6
  57.9 0.0 copy-done.7
  57.9 0.0 copy-done.17
  57.9 0.0 copy-done.19
  57.9 0.0 copy-done.20
  57.9 0.0 copy-done.18
  57.9 0.0 copy-done.1
  57.9 0.0 copy-done.2
  57.9 0.6 copy-done.3
  58.5 6.4 %shard_map.292 = (f32[8,2,16,256]{3,2,1,0:T(8,128)S(1)}, bf16[1280,128]{1,0:T(8,128)(2,1)S(1)}) custom-call(s32[1]{0:T(128)} %bitcast.place_ref, bf16[1024,256]{1,0:T(8,128)(2,1)S(1)} %bitcast.24, bf16[8,6,16,256]{3,2,1,0:T(8,128)(2,1)S(1)} %all_to_all.30.strip_ref, bf16[8,6,2,256]{3,2,1,0:T(2,128)(2,1)S(1)} %collective-permute-done.above_ref, ...), custom_call_target="tpu_custom_call" | custom-call | flops 8000000000 | bytes 8000000 | tf_op jit(solution)/shard_map/pallas_call | solution.py:619
  64.9 0.0 copy-start.5
  64.9 0.0 copy-start.11
  64.9 18.7 %all_to_all.32 = bf16[640,2,128]{2,1,0:T(2,128)(2,1)S(1)} all-to-all(bf16[640,2,128]{2,1,0:T(2,128)(2,1)S(1)} %bitcast.25), channel_id=1, replica_groups=mesh['row'=16,'col'=8] {'row','col'}, dimensions={0} | all-to-all | bytes 655360 | tf_op jit(solution)/shard_map/all_to_all | solution.py:641
  83.6 0.0 copy-done.5
  83.6 0.0 copy-done.11
  83.7 1.9 %shard_map.293 = bf16[1280,128]{1,0:T(8,128)(2,1)S(1)} custom-call(bf16[1280,128]{1,0:T(8,128)(2,1)S(1)} %bitcast.27, f32[3,16,16,128]{3,2,1,0:T(8,128)S(1)} %copy-done, bf16[128,128]{1,0:T(8,128)(2,1)S(1)} %copy-done.13, bf16[128,128]{1,0:T(8,128)(2,1)S(1)} %copy-done.12, bf16[128,256]{1,0:T(8,128)(2,1)S(1)} %copy-done.10, bf16[128,256]{1,0:T(8,128)(2,1)S(1)} %copy-done.10, ...), custom_call_target="tpu_custom_call" | custom-call | flops 2000000000 | bytes 2000000 | tf_op jit(solution)/shard_map/pallas_call | solution.py:619
  85.6 0.0 copy-start.9
  85.6 15.8 %all_to_all.33 = bf16[640,2,128]{2,1,0:T(2,128)(2,1)S(1)} all-to-all(bf16[640,2,128]{2,1,0:T(2,128)(2,1)S(1)} %bitcast.28), channel_id=1, replica_groups=mesh['row'=16,'col'=8] {'row','col'}, dimensions={0} | all-to-all | bytes 655360 | tf_op jit(solution)/shard_map/all_to_all | solution.py:641
  101.3 0.0 copy-done.9
  101.3 1.1 shard_map.294
  102.4 9.7 %all_to_all.34 = f32[8,2,16,256]{3,2,1,0:T(8,128)S(1)} all-to-all(f32[8,2,16,256]{3,2,1,0:T(8,128)S(1)} %get-tuple-element.14), channel_id=1, replica_groups=mesh['row'=16,'col'=8] {'col'}, dimensions={0} | all-to-all | bytes 524288 | tf_op jit(solution)/shard_map/all_to_all | solution.py:730
  112.1 0.7 copy.38
  (1 shorter events, 0.0 us)
Async XLA Ops:
  1.8 15.1 %copy-start.4 = (bf16[512,512]{1,0:T(8,128)(2,1)S(1)}, bf16[512,512]{1,0:T(8,128)(2,1)}, u32[]{:S(2)}) copy-start(bf16[512,512]{1,0:T(8,128)(2,1)} %constant.46.clone.table_ref.inverse_ref.forward_ref) | copy-start | bytes 1572868
  1.8 15.1 %copy-start.15 = (f32[16,256]{1,0:T(8,128)S(1)}, f32[16,256]{1,0:T(8,128)}, u32[]{:S(2)}) copy-start(f32[16,256]{1,0:T(8,128)} %constant.45.clone.twiddle_ref) | copy-start | bytes 49156
  16.8 19.1 %copy-start.10 = (bf16[128,256]{1,0:T(8,128)(2,1)S(1)}, bf16[128,256]{1,0:T(8,128)(2,1)}, u32[]{:S(2)}) copy-start(bf16[128,256]{1,0:T(8,128)(2,1)} %constant.49.clone.refs_4_.refs_5_) | copy-start | bytes 196612
  16.8 19.1 %copy-start.12 = (bf16[128,128]{1,0:T(8,128)(2,1)S(1)}, bf16[128,128]{1,0:T(8,128)(2,1)}, u32[]{:S(2)}) copy-start(bf16[128,128]{1,0:T(8,128)(2,1)} %constant.48.clone.refs_3_) | copy-start | bytes 98308
  16.8 19.1 %copy-start.13 = (bf16[128,128]{1,0:T(8,128)(2,1)S(1)}, bf16[128,128]{1,0:T(8,128)(2,1)}, u32[]{:S(2)}) copy-start(bf16[128,128]{1,0:T(8,128)(2,1)} %constant.47.clone.refs_2_) | copy-start | bytes 98308
  16.9 19.1 %copy-start.14 = (f32[32,256]{1,0:T(8,128)S(1)}, f32[32,256]{1,0:T(8,128)}, u32[]{:S(2)}) copy-start(f32[32,256]{1,0:T(8,128)} %constant.52.clone.refs_7_) | copy-start | bytes 98308
  16.9 19.1 %copy-start.16 = (f32[32,128]{1,0:T(8,128)S(1)}, f32[32,128]{1,0:T(8,128)}, u32[]{:S(2)}) copy-start(f32[32,128]{1,0:T(8,128)} %constant.51.clone.refs_6_.refs_7_) | copy-start | bytes 49156
  17.3 18.7 %copy-start = (f32[3,16,16,128]{3,2,1,0:T(8,128)S(1)}, f32[3,16,16,128]{3,2,1,0:T(8,128)}, u32[]{:S(2)}) copy-start(f32[3,16,16,128]{3,2,1,0:T(8,128)} %refs_1_.3) | copy-start | bytes 1179652
  17.3 18.7 %copy-start.8 = (bf16[128,512]{1,0:T(8,128)(2,1)S(1)}, bf16[128,512]{1,0:T(8,128)(2,1)}, u32[]{:S(2)}) copy-start(bf16[128,512]{1,0:T(8,128)(2,1)} %constant.50.clone.refs_5_) | copy-start | bytes 393220
  38.9 19.0 %copy-start.6 = (bf16[1280,64]{1,0:T(8,128)(2,1)S(1)}, bf16[1280,64]{1,0:T(8,128)(2,1)}, u32[]{:S(2)}) copy-start(bf16[1280,64]{1,0:T(8,128)(2,1)} %constant.56.clone.spread_ref) | copy-start | bytes 491524
  38.9 19.0 %copy-start.7 = (bf16[3,384,128]{2,1,0:T(8,128)(2,1)S(1)}, bf16[3,384,128]{2,1,0:T(8,128)(2,1)}, u32[]{:S(2)}) copy-start(bf16[3,384,128]{2,1,0:T(8,128)(2,1)} %constant.58.clone.fold_ref) | copy-start | bytes 884740
  38.9 19.0 %all-to-all-start.2 = ((bf16[128,8,256]{2,1,0:T(8,128)(2,1)}), bf16[128,8,256]{2,1,0:T(8,128)(2,1)S(1)}, u32[]{:S(2)}, u32[]{:S(2)}) async-start(bf16[128,8,256]{2,1,0:T(8,128)(2,1)} %bitcast.8), calls=%async_computation.2 | async-start | bytes 1048576 | tf_op jit(solution)/shard_map/all_to_all | solution.py:641
  43.6 14.2 %copy-start.17 = (f32[4,4,256]{2,1,0:T(4,128)S(1)}, f32[4,4,256]{2,1,0:T(4,128)}, u32[]{:S(2)}) copy-start(f32[4,4,256]{2,1,0:T(4,128)} %constant.53.clone.first_table_ref) | copy-start | bytes 49156
  43.7 14.2 %copy-start.19 = (s32[8,256]{1,0:T(8,128)S(1)}, s32[8,256]{1,0:T(8,128)}, u32[]{:S(2)}) copy-start(s32[8,256]{1,0:T(8,128)} %constant.57.clone.rows_ref) | copy-start | bytes 24580
  43.7 14.2 %copy-start.20 = (f32[3,2,128]{2,1,0:T(2,128)S(1)}, f32[3,2,128]{2,1,0:T(2,128)}, u32[]{:S(2)}) copy-start(f32[3,2,128]{2,1,0:T(2,128)} %constant.54.clone.second_table_ref) | copy-start | bytes 9220
  43.8 7.7 %collective-permute-start.1 = (bf16[8,6,2,256]{3,2,1,0:T(2,128)(2,1)S(1)}, bf16[8,6,2,256]{3,2,1,0:T(2,128)(2,1)S(1)}, u32[]{:S(2)}, u32[]{:S(2)}) collective-permute-start(bf16[8,6,2,256]{3,2,1,0:T(2,128)(2,1)S(1)} %get-tuple-element.19), channel_id=1, source_target_pairs={{1,0},{2,1},{3,2},{4,3},{5,4},{6,5},{7,6},{8,7},{9,8},{10,9},{11,1... | collective-permute-start | bytes 147464 | tf_op jit(solution)/shard_map/ppermute | solution.py:675
  45.1 12.8 %copy-start.18 = (f32[3,4,192]{2,1,0:T(4,128)S(1)}, f32[3,4,192]{2,1,0:T(4,128)}, u32[]{:S(2)}) copy-start(f32[3,4,192]{2,1,0:T(4,128)} %constant.55.clone.back_table_ref) | copy-start | bytes 27652
  45.1 6.4 %collective-permute-start = (bf16[8,6,2,256]{3,2,1,0:T(2,128)(2,1)S(1)}, bf16[8,6,2,256]{3,2,1,0:T(2,128)(2,1)S(1)}, u32[]{:S(2)}, u32[]{:S(2)}) collective-permute-start(bf16[8,6,2,256]{3,2,1,0:T(2,128)(2,1)S(1)} %get-tuple-element.20), channel_id=1, source_target_pairs={{0,1},{1,2},{2,3},{3,4},{4,5},{5,6},{6,7},{7,8},{8,9},{9,10},{10,1... | collective-permute-start | bytes 147464 | tf_op jit(solution)/shard_map/ppermute | solution.py:674
  49.6 8.3 %copy-start.1 = (bf16[32,4,3,3]{0,1,3,2:T(4,128)(2,1)S(1)}, bf16[32,4,3,3]{0,1,3,2:T(4,128)(2,1)}, u32[]{:S(2)}) copy-start(bf16[32,4,3,3]{0,1,3,2:T(4,128)(2,1)} %param.30) | copy-start | bytes 6916
  49.7 8.3 %copy-start.2 = (bf16[2,32,3,3]{1,0,3,2:T(2,128)(2,1)S(1)}, bf16[2,32,3,3]{1,0,3,2:T(2,128)(2,1)}, u32[]{:S(2)}) copy-start(bf16[2,32,3,3]{1,0,3,2:T(2,128)(2,1)} %param.32) | copy-start | bytes 3460
  57.9 0.7 copy-start.3
  64.9 18.7 %copy-start.5 = (bf16[1280,32]{1,0:T(8,128)(2,1)S(1)}, bf16[1280,32]{1,0:T(8,128)(2,1)}, u32[]{:S(2)}) copy-start(bf16[1280,32]{1,0:T(8,128)(2,1)} %constant.60.clone.refs_9_) | copy-start | bytes 245764
  64.9 18.7 %copy-start.11 = (bf16[16,1280]{1,0:T(8,128)(2,1)S(1)}, bf16[16,1280]{1,0:T(8,128)(2,1)}, u32[]{:S(2)}) copy-start(bf16[16,1280]{1,0:T(8,128)(2,1)} %constant.59.clone.refs_8_) | copy-start | bytes 122884
  85.6 15.8 %copy-start.9 = (bf16[32,1280]{1,0:T(8,128)(2,1)S(1)}, bf16[32,1280]{1,0:T(8,128)(2,1)}, u32[]{:S(2)}) copy-start(bf16[32,1280]{1,0:T(8,128)(2,1)} %constant.61.clone.collect_ref) | copy-start | bytes 245764

commit v5 on v4

--- a/solution.py
+++ b/solution.py
@@ -251,8 +251,22 @@
     return high, (values - high.astype(F32)).astype(BF16)
 
 
+def cells_body(estimate_ref, dirty_ref, cot_ref, out_ref):
+    sources = (estimate_ref, dirty_ref, cot_ref)
+    planes = [sources[i // 2][i % 2].astype(F32) for i in range(6)]
+    gap = jnp.zeros((2, 256), F32)
+    for c in range(8):
+        pieces = []
+        for i in range(6):
+            out_ref[c, 16 * i : 16 * i + 16] = sources[i // 2][i % 2, 16 * c : 16 * c + 16]
+            pieces.append(planes[i][16 * c - 2 : 16 * c] if c > 0 else gap)
+            pieces.append(planes[i][16 * c + 16 : 16 * c + 18] if c < 7 else gap)
+        pieces.append(jnp.zeros((8, 256), F32))
+        out_ref[c, 96:128] = jnp.concatenate(pieces, 0).astype(BF16)
+
+
 def ahead_body(strip_ref, twiddle_ref, table_ref, out_ref):
-    z = [strip_ref[c, 0:2].astype(F32).reshape(32, 256) for c in range(8)]
+    z = [strip_ref[c, 0:32].astype(F32) for c in range(8)]
     even, odd = columns_ahead(z, twiddle_ref, table_ref)
     out_ref[...] = jnp.stack([even, odd], 1).reshape(1024, 128).astype(BF16)
 
@@ -354,9 +368,9 @@
 
 
 def prepare(
+    place,
     strip_ref,
-    above_ref,
-    below_ref,
+    beyond_ref,
     w_first_ref,
     w_second_ref,
     bias_ref,
@@ -373,12 +387,16 @@
 ):
     row = lax.broadcasted_iota(jnp.int32, (128, IMAGE), 0)
     tall_ref[...] = jnp.zeros_like(tall_ref)
+    rims = [strip_ref[c, 96:128].astype(F32) for c in range(8)]
+    opens = (place & 7) == 0
+    closes = (place & 7) == 7
     for i in range(6):
         for c in range(8):
             cols = slice(256 * c, 256 * c + 256)
-            tall_ref[0:2, cols] = above_ref[c, i].astype(F32)
-            tall_ref[2:18, cols] = strip_ref[c, i].astype(F32)
-            tall_ref[18:20, cols] = below_ref[c, i].astype(F32)
+            beyond = beyond_ref[c, i].astype(F32)
+            tall_ref[0:2, cols] = jnp.where(opens, beyond, rims[c][4 * i : 4 * i + 2])
+            tall_ref[2:18, cols] = strip_ref[c, 16 * i : 16 * i + 16].astype(F32)
+            tall_ref[18:20, cols] = jnp.where(closes, beyond, rims[c][4 * i + 2 : 4 * i + 4])
         value = tall_ref[...]
         if i in (2, 3):
             dirty_ref[i - 2] = value
@@ -435,8 +453,7 @@
     place_ref,
     in_ref,
     strip_ref,
-    above_ref,
-    below_ref,
+    beyond_ref,
     w_first_ref,
     w_second_ref,
     bias_ref,
@@ -462,10 +479,11 @@
     weights_ref,
     tall_ref,
 ):
+    place = place_ref[0]
     prepare(
+        place,
         strip_ref,
-        above_ref,
-        below_ref,
+        beyond_ref,
         w_first_ref,
         w_second_ref,
         bias_ref,
@@ -480,7 +498,6 @@
         tall_ref,
         stack_ref,
     )
-    place = place_ref[0]
     chunks = in_ref[...].astype(F32).reshape(64, 2, 8, 256)
     values = lax.dot_general(
         regroup(chunks[:, 0], chunks[:, 1]), inverse_ref[...], TN, preferred_element_type=F32
@@ -519,9 +536,11 @@
             [grad_pre[0:32] * top, grad_pre[32:544], grad_pre[544:576] * bottom], 0
         ).astype(BF16)
         spread_grad_ref[:, cols] = jnp.dot(back_ref[...], grad_pre, preferred_element_type=F32)
-        acc_first_ref[...] += lax.dot_general(grad_pre, features, NT, preferred_element_type=F32)
+        acc_first_ref[...] += lax.dot_general(
+            grad_pre[32:544], features, NT, preferred_element_type=F32
+        )
         acc_second_ref[...] += lax.dot_general(
-            hidden.astype(BF16), cots, NT, preferred_element_type=F32
+            hidden[32:544].astype(BF16), cots, NT, preferred_element_type=F32
         )
         return carry
 
@@ -535,20 +554,20 @@
         for c in range(8):
             part = total[:, 256 * c : 256 * c + 256]
             if i < 2:
-                base_ref[c, i] = part + strip_ref[c, 4 + i].astype(F32)
+                base_ref[c, i] = part + strip_ref[c, 64 + 16 * i : 80 + 16 * i].astype(F32)
             else:
                 z[c][i - 2] = part.astype(BF16).astype(F32)
     for i in range(2):
-        total = strip_ref[0, 4 + i].astype(F32)
+        total = strip_ref[0, 64 + 16 * i : 80 + 16 * i].astype(F32)
         for c in range(1, 8):
-            total = total + strip_ref[c, 4 + i].astype(F32)
+            total = total + strip_ref[c, 64 + 16 * i : 80 + 16 * i].astype(F32)
         cot_sums.append(total.sum(axis=0, keepdims=True).sum(axis=1, keepdims=True))
 
     rows = rows_ref[0:1, :]
     parts = [jnp.zeros((HIDDEN, 384), F32) for _ in range(3)]
     for r in range(1, 17):
-        of_first = acc_first_ref[32 * r : 32 * r + 32, :]
-        of_second = acc_second_ref[32 * r : 32 * r + 32, :]
+        of_first = acc_first_ref[32 * r - 32 : 32 * r, :]
+        of_second = acc_second_ref[32 * r - 32 : 32 * r, :]
         for p in range(3):
             keep = (rows == r + p) | (rows == -1)
             parts[p] = parts[p] + jnp.concatenate(
@@ -614,7 +633,7 @@
         out_ref[c] = base_ref[c] - blurred
 
 
-def call(body, outs, *args, scratch=(), scalars=0, after=(), cost=2):
+def call(body, outs, *args, scratch=(), scalars=0, after=(), cost=2, vmem=VM):
     whole = pl.BlockSpec(memory_space=pltpu.VMEM)
     return pl.pallas_call(
         body,
@@ -624,7 +643,7 @@
         + [pl.BlockSpec(memory_space=pl.ANY)] * len(after),
         out_specs=jax.tree.map(lambda _: whole, outs),
         scratch_shapes=list(scratch),
-        compiler_params=pltpu.CompilerParams(vmem_limit_bytes=VM * 1024 * 1024),
+        compiler_params=pltpu.CompilerParams(vmem_limit_bytes=vmem * 1024 * 1024),
         cost_estimate=pl.CostEstimate(
             flops=cost * 10**9, bytes_accessed=cost * 10**6, transcendentals=0
         ),
@@ -664,15 +683,18 @@
 
 
 def shards(estimate, dirty_image, psf_spectra, w_first, b_first, w_second, cotangent):
-    cells = jnp.stack([v.reshape(2, 8, STRIP, 256) for v in (estimate, dirty_image, cotangent)])
-    cells = cells.transpose(2, 0, 1, 3, 4).reshape(8, 6, STRIP, 256)
+    cells = call(
+        cells_body, like(8, 128, 256), estimate, dirty_image, cotangent, vmem=60
+    )
     strip = lax.all_to_all(cells, "col", 0, 0, tiled=True)
     spec = call(
         ahead_body, like(1024, 128), strip, column_twiddle(), column_tables()[0]
     )
     spec = exchange(spec, 8)
-    above = lax.ppermute(strip[:, :, -2:], RC, [(d, d + 1) for d in range(DEVS - 1)])
-    below = lax.ppermute(strip[:, :, :2], RC, [(d + 1, d) for d in range(DEVS - 1)])
+    rows = strip[:, :96].reshape(8, 6, STRIP, 256)
+    edge = jnp.where(lax.axis_index("col") == 7, rows[:, :, -2:], rows[:, :, :2])
+    seams = [(8 * r + 7, 8 * r + 8) for r in range(15)]
+    beyond = lax.ppermute(edge, RC, seams + [(b, a) for a, b in seams])
     first_table, second_table, back_table, row_of, fold = weight_tables()
     mixed = exchange(middle(spec, psf_spectra, 32, 2, 8, ()), 8)
     place = (lax.axis_index("row") * 8 + lax.axis_index("col")).astype(jnp.int32).reshape(1)
@@ -682,8 +704,7 @@
         place,
         mixed,
         strip,
-        above,
-        below,
+        beyond,
         w_first.transpose(2, 3, 1, 0),
         w_second.transpose(2, 3, 0, 1),
         b_first.reshape(1, 32),
@@ -700,8 +721,8 @@
             pltpu.VMEM((128, IMAGE), F32),
             pltpu.VMEM((256, IMAGE), BF16),
             pltpu.VMEM((192, IMAGE), F32),
-            pltpu.VMEM((576, 256), F32),
-            pltpu.VMEM((576, 128), F32),
+            pltpu.VMEM((512, 256), F32),
+            pltpu.VMEM((512, 128), F32),
             pltpu.VMEM((192, 576), BF16),
             pltpu.VMEM((128, IMAGE), BF16),
             pltpu.VMEM((2, HOLD, IMAGE), F32),

time: 113 us -> 113 us (level)
  starting transfers between devices: 10.6 us -> 5.41 us
  waiting for transfers between devices: 8.2 us -> 12.7 us
  Pallas kernels: 12.6 us -> 14.4 us
    all_to_all x1, waiting for transfers between devices: 6.39 us -> 12.7 us  [exchange(): lax.all_to_all(chunks.reshape(DEVS * per // rows, rows, width), RC, 0, 0,...]
    ppermute x2 -> x1, starting transfers between devices: 5.84 us -> 0.8 us  [shards(): beyond = lax.ppermute(edge, RC, seams + [(b, a) for a, b in seams])]
    all_to_all x3, blocking collectives: 53.1 us -> 51.2 us  [exchange(): lax.all_to_all(chunks.reshape(DEVS * per // rows, rows, width), RC, 0, 0,...]
    ppermute x2 -> x1, waiting for transfers between devices: 1.81 us -> 0.01 us  [shards(): beyond = lax.ppermute(edge, RC, seams + [(b, a) for a, b in seams])]
    pallas_call x5 -> x6, Pallas kernels: 12.6 us -> 14.4 us  [call(): pl.pallas_call(body, out_shape=outs, in_specs=[pl.BlockSpec(memory_space=...]
    all_to_all x1, blocking collectives: 15 us -> 16.6 us  [shards(): strip = lax.all_to_all(cells, 'col', 0, 0, tiled=True)]
  transfers between devices with their start and end apart: 3 -> 2, of which waited for: 2 -> 1; matrix products, arithmetic and copies ran while one was open for 0% -> 0% of each run, Pallas kernels for 0% -> 0%
where the time goes in v5:
time: 113 us
  blocking collectives  77.5 us (69%)
  Pallas kernels  14.4 us (13%)
  waiting for transfers between devices  12.7 us (11%)
  starting transfers between devices  5.41 us (5%)
  local copies, waits for them, and re-layouts  1.49 us (1%)
    all_to_all x3, blocking collectives, exchange(): lax.all_to_all(chunks.reshape(DEVS * per // rows, rows, width), RC, 0, 0,...  51.2 us
    all_to_all x1, blocking collectives, shards(): strip = lax.all_to_all(cells, 'col', 0, 0, tiled=True)  16.6 us
    pallas_call x6, Pallas kernels, call(): pl.pallas_call(body, out_shape=outs, in_specs=[pl.BlockSpec(memory_space=...  14.4 us
    all_to_all x1, waiting for transfers between devices, exchange(): lax.all_to_all(chunks.reshape(DEVS * per // rows, rows, width), RC, 0, 0,...  12.7 us
    all_to_all x1, blocking collectives, shards(): image = lax.all_to_all(image, 'col', 0, 0, tiled=True)  9.68 us
    all_to_all x1, starting transfers between devices, exchange(): lax.all_to_all(chunks.reshape(DEVS * per // rows, rows, width), RC, 0, 0,...  4.61 us
  transfers between devices with their start and end apart: 2, of which 1 were waited for; matrix products, arithmetic and copies ran while one was open for 0% of the time, Pallas kernels for 0%

profile of v5, /device:TPU:0, one launch (start us, length us, event | category | flops | bytes accessed | tf_op | source)
XLA Modules:
  0.0 112.5 jit_solution(10415891227472961367)
XLA Ops:
  0.6 1.9 %shard_map.290 = bf16[8,128,256]{2,1,0:T(8,128)(2,1)} custom-call(bf16[2,128,256]{2,1,0:T(8,128)(2,1)} %estimate_ref.1, bf16[2,128,256]{2,1,0:T(8,128)(2,1)} %dirty_ref.1, bf16[2,128,256]{2,1,0:T(8,128)(2,1)} %cot_ref.1), custom_call_target="tpu_custom_call" | custom-call | flops 2000000000 | bytes 2000000 | tf_op jit(solution)/shard_map/pallas_call | solution.py:638
  2.5 0.0 copy-start.4
  2.6 0.0 copy-start.15
  2.6 16.6 %all_to_all.30.strip_ref = bf16[8,128,256]{2,1,0:T(8,128)(2,1)S(1)} all-to-all(bf16[8,128,256]{2,1,0:T(8,128)(2,1)} %shard_map.290), channel_id=1, replica_groups=mesh['row'=16,'col'=8] {'col'}, dimensions={0} | all-to-all | bytes 1048576 | tf_op jit(solution)/shard_map/all_to_all | solution.py:689
  19.1 0.0 copy-done.4
  19.1 0.0 copy-done.15
  19.1 0.0 copy-start.10
  19.1 0.0 copy-start.12
  19.1 0.0 copy-start.13
  19.2 0.0 copy-start.14
  19.2 0.0 copy-start.16
  19.2 0.4 shard_map.291
  19.6 0.0 copy-start
  19.6 0.0 copy-start.8
  19.6 18.6 %all_to_all.31 = bf16[128,8,128]{2,1,0:T(8,128)(2,1)S(1)} all-to-all(bf16[128,8,128]{2,1,0:T(8,128)(2,1)S(1)} %bitcast.25), channel_id=1, replica_groups=mesh['row'=16,'col'=8] {'row','col'}, dimensions={0} | all-to-all | bytes 524288 | tf_op jit(solution)/shard_map/all_to_all | solution.py:660
  38.2 0.0 copy-done.10
  38.2 0.0 copy-done.12
  38.2 0.0 copy-done.13
  38.2 0.0 copy-done.14
  38.2 0.0 copy-done.16
  38.2 0.0 copy-done
  38.2 0.0 copy-done.8
  38.2 2.9 %shard_map.292 = bf16[1024,256]{1,0:T(8,128)(2,1)} custom-call(bf16[1024,128]{1,0:T(8,128)(2,1)S(1)} %bitcast.24, f32[3,16,16,128]{3,2,1,0:T(8,128)S(1)} %copy-done, bf16[128,128]{1,0:T(8,128)(2,1)S(1)} %copy-done.13, bf16[128,128]{1,0:T(8,128)(2,1)S(1)} %copy-done.12, bf16[128,256]{1,0:T(8,128)(2,1)S(1)} %copy-done.10, bf16[128,512]{1,0:T(8,128)(2,1)S(1)} %copy-done.8, ...), custom_call_target="tpu_custom_call" | custom-call | flops 2000000000 | bytes 2000000 | tf_op jit(solution)/shard_map/pallas_call | solution.py:638
  41.1 4.6 %all-to-all-start.2 = ((bf16[128,8,256]{2,1,0:T(8,128)(2,1)}), bf16[128,8,256]{2,1,0:T(8,128)(2,1)S(1)}, u32[]{:S(2)}, u32[]{:S(2)}) async-start(bf16[128,8,256]{2,1,0:T(8,128)(2,1)} %bitcast.3), calls=%async_computation.2 | async-start | bytes 1048576 | tf_op jit(solution)/shard_map/all_to_all | solution.py:660
  45.8 0.0 copy-start.6
  45.8 0.0 copy-start.7
  45.8 0.0 copy-start.17
  45.8 0.0 copy-start.18
  45.8 0.0 copy-start.19
  45.9 0.1 broadcast_select_fusion
  45.9 0.0 copy-start.1
  46.0 0.8 collective-permute-start
  46.8 0.0 copy-start.2
  46.8 0.0 collective-permute-done.beyond_ref
  46.8 12.7 %all-to-all-done.2 = bf16[128,8,256]{2,1,0:T(8,128)(2,1)S(1)} async-done(((bf16[128,8,256]{2,1,0:T(8,128)(2,1)}), bf16[128,8,256]{2,1,0:T(8,128)(2,1)S(1)}, u32[]{:S(2)}, u32[]{:S(2)}) %all-to-all-start.2) | async-done | bytes 524320 | tf_op jit(solution)/shard_map/all_to_all | solution.py:660
  59.5 0.0 copy-start.20
  59.5 0.0 copy-start.3
  59.5 0.0 copy-done.6
  59.5 0.0 copy-done.7
  59.5 0.0 copy-done.17
  59.6 0.0 copy-done.18
  59.6 0.0 copy-done.19
  59.6 0.0 copy-done.1
  59.6 0.0 copy-done.2
  59.6 0.6 copy-done.20
  60.2 0.0 copy-done.3
  60.2 6.3 %shard_map.293 = (f32[8,2,16,256]{3,2,1,0:T(8,128)S(1)}, bf16[1280,128]{1,0:T(8,128)(2,1)S(1)}) custom-call(s32[1]{0:T(128)} %bitcast.place_ref, bf16[1024,256]{1,0:T(8,128)(2,1)S(1)} %bitcast.19, bf16[8,128,256]{2,1,0:T(8,128)(2,1)S(1)} %all_to_all.30.strip_ref, bf16[8,6,2,256]{3,2,1,0:T(2,128)(2,1)S(1)} %collective-permute-done.beyond_ref, ...), custom_call_target="tpu_custom_call" | custom-call | flops 8000000000 | bytes 8000000 | tf_op jit(solution)/shard_map/pallas_call | solution.py:638
  66.5 0.0 copy-start.5
  66.5 0.0 copy-start.11
  66.5 16.9 %all_to_all.32 = bf16[640,2,128]{2,1,0:T(2,128)(2,1)S(1)} all-to-all(bf16[640,2,128]{2,1,0:T(2,128)(2,1)S(1)} %bitcast.20), channel_id=1, replica_groups=mesh['row'=16,'col'=8] {'row','col'}, dimensions={0} | all-to-all | bytes 655360 | tf_op jit(solution)/shard_map/all_to_all | solution.py:660
  83.4 0.0 copy-done.5
  83.4 0.0 copy-done.11
  83.4 1.9 %shard_map.294 = bf16[1280,128]{1,0:T(8,128)(2,1)S(1)} custom-call(bf16[1280,128]{1,0:T(8,128)(2,1)S(1)} %bitcast.22, f32[3,16,16,128]{3,2,1,0:T(8,128)S(1)} %copy-done, bf16[128,128]{1,0:T(8,128)(2,1)S(1)} %copy-done.13, bf16[128,128]{1,0:T(8,128)(2,1)S(1)} %copy-done.12, bf16[128,256]{1,0:T(8,128)(2,1)S(1)} %copy-done.10, bf16[128,256]{1,0:T(8,128)(2,1)S(1)} %copy-done.10, ...), custom_call_target="tpu_custom_call" | custom-call | flops 2000000000 | bytes 2000000 | tf_op jit(solution)/shard_map/pallas_call | solution.py:638
  85.3 0.0 copy-start.9
  85.3 15.8 %all_to_all.33 = bf16[640,2,128]{2,1,0:T(2,128)(2,1)S(1)} all-to-all(bf16[640,2,128]{2,1,0:T(2,128)(2,1)S(1)} %bitcast.23), channel_id=1, replica_groups=mesh['row'=16,'col'=8] {'row','col'}, dimensions={0} | all-to-all | bytes 655360 | tf_op jit(solution)/shard_map/all_to_all | solution.py:660
  101.1 0.0 copy-done.9
  101.1 1.0 shard_map.295
  102.1 9.7 %all_to_all.34 = f32[8,2,16,256]{3,2,1,0:T(8,128)S(1)} all-to-all(f32[8,2,16,256]{3,2,1,0:T(8,128)S(1)} %get-tuple-element.14), channel_id=1, replica_groups=mesh['row'=16,'col'=8] {'col'}, dimensions={0} | all-to-all | bytes 524288 | tf_op jit(solution)/shard_map/all_to_all | solution.py:751
  111.8 0.7 copy.32
  (1 shorter events, 0.0 us)
Async XLA Ops:
  2.5 16.6 %copy-start.4 = (bf16[512,512]{1,0:T(8,128)(2,1)S(1)}, bf16[512,512]{1,0:T(8,128)(2,1)}, u32[]{:S(2)}) copy-start(bf16[512,512]{1,0:T(8,128)(2,1)} %constant.48.clone.table_ref.inverse_ref.forward_ref) | copy-start | bytes 1572868
  2.6 16.6 %copy-start.15 = (f32[16,256]{1,0:T(8,128)S(1)}, f32[16,256]{1,0:T(8,128)}, u32[]{:S(2)}) copy-start(f32[16,256]{1,0:T(8,128)} %constant.47.clone.twiddle_ref) | copy-start | bytes 49156
  19.1 19.0 %copy-start.10 = (bf16[128,256]{1,0:T(8,128)(2,1)S(1)}, bf16[128,256]{1,0:T(8,128)(2,1)}, u32[]{:S(2)}) copy-start(bf16[128,256]{1,0:T(8,128)(2,1)} %constant.51.clone.refs_4_.refs_5_) | copy-start | bytes 196612
  19.1 19.0 %copy-start.12 = (bf16[128,128]{1,0:T(8,128)(2,1)S(1)}, bf16[128,128]{1,0:T(8,128)(2,1)}, u32[]{:S(2)}) copy-start(bf16[128,128]{1,0:T(8,128)(2,1)} %constant.50.clone.refs_3_) | copy-start | bytes 98308
  19.1 19.0 %copy-start.13 = (bf16[128,128]{1,0:T(8,128)(2,1)S(1)}, bf16[128,128]{1,0:T(8,128)(2,1)}, u32[]{:S(2)}) copy-start(bf16[128,128]{1,0:T(8,128)(2,1)} %constant.49.clone.refs_2_) | copy-start | bytes 98308
  19.2 19.0 %copy-start.14 = (f32[32,256]{1,0:T(8,128)S(1)}, f32[32,256]{1,0:T(8,128)}, u32[]{:S(2)}) copy-start(f32[32,256]{1,0:T(8,128)} %constant.54.clone.refs_7_) | copy-start | bytes 98308
  19.2 19.0 %copy-start.16 = (f32[32,128]{1,0:T(8,128)S(1)}, f32[32,128]{1,0:T(8,128)}, u32[]{:S(2)}) copy-start(f32[32,128]{1,0:T(8,128)} %constant.53.clone.refs_6_.refs_7_) | copy-start | bytes 49156
  19.6 18.6 %copy-start = (f32[3,16,16,128]{3,2,1,0:T(8,128)S(1)}, f32[3,16,16,128]{3,2,1,0:T(8,128)}, u32[]{:S(2)}) copy-start(f32[3,16,16,128]{3,2,1,0:T(8,128)} %refs_1_.3) | copy-start | bytes 1179652
  19.6 18.6 %copy-start.8 = (bf16[128,512]{1,0:T(8,128)(2,1)S(1)}, bf16[128,512]{1,0:T(8,128)(2,1)}, u32[]{:S(2)}) copy-start(bf16[128,512]{1,0:T(8,128)(2,1)} %constant.52.clone.refs_5_) | copy-start | bytes 393220
  41.1 18.4 %all-to-all-start.2 = ((bf16[128,8,256]{2,1,0:T(8,128)(2,1)}), bf16[128,8,256]{2,1,0:T(8,128)(2,1)S(1)}, u32[]{:S(2)}, u32[]{:S(2)}) async-start(bf16[128,8,256]{2,1,0:T(8,128)(2,1)} %bitcast.3), calls=%async_computation.2 | async-start | bytes 1048576 | tf_op jit(solution)/shard_map/all_to_all | solution.py:660
  45.8 13.8 %copy-start.6 = (bf16[1280,64]{1,0:T(8,128)(2,1)S(1)}, bf16[1280,64]{1,0:T(8,128)(2,1)}, u32[]{:S(2)}) copy-start(bf16[1280,64]{1,0:T(8,128)(2,1)} %constant.58.clone.spread_ref) | copy-start | bytes 491524
  45.8 13.8 %copy-start.7 = (bf16[3,384,128]{2,1,0:T(8,128)(2,1)S(1)}, bf16[3,384,128]{2,1,0:T(8,128)(2,1)}, u32[]{:S(2)}) copy-start(bf16[3,384,128]{2,1,0:T(8,128)(2,1)} %constant.60.clone.fold_ref) | copy-start | bytes 884740
  45.8 13.7 %copy-start.17 = (f32[4,4,256]{2,1,0:T(4,128)S(1)}, f32[4,4,256]{2,1,0:T(4,128)}, u32[]{:S(2)}) copy-start(f32[4,4,256]{2,1,0:T(4,128)} %constant.55.clone.first_table_ref) | copy-start | bytes 49156
  45.8 13.7 %copy-start.18 = (f32[3,4,192]{2,1,0:T(4,128)S(1)}, f32[3,4,192]{2,1,0:T(4,128)}, u32[]{:S(2)}) copy-start(f32[3,4,192]{2,1,0:T(4,128)} %constant.57.clone.back_table_ref) | copy-start | bytes 27652
  45.8 13.7 %copy-start.19 = (s32[8,256]{1,0:T(8,128)S(1)}, s32[8,256]{1,0:T(8,128)}, u32[]{:S(2)}) copy-start(s32[8,256]{1,0:T(8,128)} %constant.59.clone.rows_ref) | copy-start | bytes 24580
  45.9 13.6 %copy-start.1 = (bf16[32,4,3,3]{0,1,3,2:T(4,128)(2,1)S(1)}, bf16[32,4,3,3]{0,1,3,2:T(4,128)(2,1)}, u32[]{:S(2)}) copy-start(bf16[32,4,3,3]{0,1,3,2:T(4,128)(2,1)} %param.30) | copy-start | bytes 6916
  46.0 0.8 collective-permute-start
  46.8 12.8 %copy-start.2 = (bf16[2,32,3,3]{1,0,3,2:T(2,128)(2,1)S(1)}, bf16[2,32,3,3]{1,0,3,2:T(2,128)(2,1)}, u32[]{:S(2)}) copy-start(bf16[2,32,3,3]{1,0,3,2:T(2,128)(2,1)} %param.32) | copy-start | bytes 3460
  59.5 0.7 copy-start.20
  59.5 0.7 copy-start.3
  66.5 16.9 %copy-start.5 = (bf16[1280,32]{1,0:T(8,128)(2,1)S(1)}, bf16[1280,32]{1,0:T(8,128)(2,1)}, u32[]{:S(2)}) copy-start(bf16[1280,32]{1,0:T(8,128)(2,1)} %constant.62.clone.refs_9_) | copy-start | bytes 245764
  66.5 16.9 %copy-start.11 = (bf16[16,1280]{1,0:T(8,128)(2,1)S(1)}, bf16[16,1280]{1,0:T(8,128)(2,1)}, u32[]{:S(2)}) copy-start(bf16[16,1280]{1,0:T(8,128)(2,1)} %constant.61.clone.refs_8_) | copy-start | bytes 122884
  85.3 15.8 %copy-start.9 = (bf16[32,1280]{1,0:T(8,128)(2,1)S(1)}, bf16[32,1280]{1,0:T(8,128)(2,1)}, u32[]{:S(2)}) copy-start(bf16[32,1280]{1,0:T(8,128)(2,1)} %constant.63.clone.collect_ref) | copy-start | bytes 245764

commit v6 on v5

--- a/solution.py
+++ b/solution.py
@@ -10,7 +10,7 @@
 
 IMAGE = 2048
 DEVS = 128
-VM = 20
+VM = 28
 STRIP = 16
 REACH = 20
 HOLD = 24
@@ -134,10 +134,12 @@
     for i in range(3):
         first[3, i, 120 + i] = 1.0
     fold[0, 120, 54] = 1.0
+    band = np.zeros((4, 4, 640), np.float32)
+    band[:, :, 0:256] = first
+    band[:3, :2, 256:384] = second
+    band[:3, :, 384:576] = back
     return (
-        first.astype(np.float32),
-        second.astype(np.float32),
-        back.astype(np.float32),
+        band,
         rows.astype(np.int32),
         bf16_table(fold),
     )
@@ -374,9 +376,7 @@
     w_first_ref,
     w_second_ref,
     bias_ref,
-    first_table_ref,
-    second_table_ref,
-    back_table_ref,
+    band_ref,
     rows_ref,
     features_ref,
     cot_ref,
@@ -414,9 +414,9 @@
     def spread(weights, table):
         return lax.dot_general(weights, table, TN, preferred_element_type=F32)
 
-    def parts_of(source_ref, table_ref):
+    def parts_of(source_ref, lanes):
         return [
-            sum(spread(source_ref[p, q].astype(F32), table_ref[q]) for q in range(3))
+            sum(spread(source_ref[p, q].astype(F32), band_ref[q][:, lanes]) for q in range(3))
             for p in range(3)
         ]
 
@@ -424,16 +424,19 @@
     high = bias.astype(BF16).astype(F32)
     middle = (bias - high).astype(BF16).astype(F32)
     pieces = jnp.concatenate([high, middle, bias - high - middle, jnp.zeros_like(bias)], 0)
-    offset = spread(pieces, first_table_ref[3])
-    first = banded(parts_of(w_first_ref, first_table_ref), rows)
+    offset = spread(pieces, band_ref[3][:, 0:256])
+    first = banded(parts_of(w_first_ref, slice(0, 256)), rows)
     first = first + jnp.concatenate([offset] * GRAD_ROWS, 0)
     weights_ref[:, 0:256] = (0.5 * first).astype(BF16)
     parts = [
-        sum(spread(w_second_ref[2 - e, 2 - q].astype(F32), second_table_ref[q]) for q in range(3))
+        sum(
+            spread(w_second_ref[2 - e, 2 - q].astype(F32), band_ref[q][0:2, 256:384])
+            for q in range(3)
+        )
         for e in range(3)
     ]
     weights_ref[:, 256:384] = (0.5 * banded(parts, rows[:, :128])).astype(BF16)
-    parts = parts_of(w_first_ref, back_table_ref)
+    parts = parts_of(w_first_ref, slice(384, 576))
     rows = lax.broadcasted_iota(jnp.int32, (1, 192), 1) & 15
     parts = [parts[2 - p] for p in range(3)]
     weights_ref[:, 384:576] = banded_back(parts, rows).astype(BF16)
@@ -457,9 +460,7 @@
     w_first_ref,
     w_second_ref,
     bias_ref,
-    first_table_ref,
-    second_table_ref,
-    back_table_ref,
+    band_ref,
     twiddle_ref,
     inverse_ref,
     forward_ref,
@@ -487,9 +488,7 @@
         w_first_ref,
         w_second_ref,
         bias_ref,
-        first_table_ref,
-        second_table_ref,
-        back_table_ref,
+        band_ref,
         rows_ref,
         features_ref,
         cot_ref,
@@ -523,7 +522,7 @@
     bottom = jnp.where(place < DEVS - 1, 1.0, 0.0)
 
     def block(step, carry):
-        cols = pl.ds(pl.multiple_of(step * 512, 512), 512)
+        cols = pl.ds(pl.multiple_of(step * 1024, 1024), 1024)
         features = features_ref[:, cols]
         cots = cot_ref[:, cols]
         preact = jnp.dot(weights_ref[:, 0:256], features, preferred_element_type=F32)
@@ -544,7 +543,7 @@
         )
         return carry
 
-    lax.fori_loop(0, 4, block, 0, unroll=True)
+    lax.fori_loop(0, 2, block, 0, unroll=True)
 
     cot_sums = []
     z = [[None, None] for _ in range(8)]
@@ -695,7 +694,7 @@
     edge = jnp.where(lax.axis_index("col") == 7, rows[:, :, -2:], rows[:, :, :2])
     seams = [(8 * r + 7, 8 * r + 8) for r in range(15)]
     beyond = lax.ppermute(edge, RC, seams + [(b, a) for a, b in seams])
-    first_table, second_table, back_table, row_of, fold = weight_tables()
+    band, row_of, fold = weight_tables()
     mixed = exchange(middle(spec, psf_spectra, 32, 2, 8, ()), 8)
     place = (lax.axis_index("row") * 8 + lax.axis_index("col")).astype(jnp.int32).reshape(1)
     base, spec = call(
@@ -708,9 +707,7 @@
         w_first.transpose(2, 3, 1, 0),
         w_second.transpose(2, 3, 0, 1),
         b_first.reshape(1, 32),
-        first_table,
-        second_table,
-        back_table,
+        band,
         column_twiddle(),
         column_tables()[1],
         column_tables()[0],

time: 113 us -> 113 us (level)
  no operation moved by 1% of the time
where the time goes in v6:
time: 113 us; the launch traced here: 112 us
  blocking collectives  77.5 us (69%)
  Pallas kernels  14.3 us (13%)
  waiting for transfers between devices  12.8 us (11%)
  starting transfers between devices  5.4 us (5%)
  local copies, waits for them, and re-layouts  1.47 us (1%)
    all_to_all x3, blocking collectives, exchange(): lax.all_to_all(chunks.reshape(DEVS * per // rows, rows, width), RC, 0, 0,...  51.2 us
    all_to_all x1, blocking collectives, shards(): strip = lax.all_to_all(cells, 'col', 0, 0, tiled=True)  16.6 us
    pallas_call x6, Pallas kernels, call(): pl.pallas_call(body, out_shape=outs, in_specs=[pl.BlockSpec(memory_space=...  14.3 us
    all_to_all x1, waiting for transfers between devices, exchange(): lax.all_to_all(chunks.reshape(DEVS * per // rows, rows, width), RC, 0, 0,...  12.8 us
    all_to_all x1, blocking collectives, shards(): image = lax.all_to_all(image, 'col', 0, 0, tiled=True)  9.68 us
    all_to_all x1, starting transfers between devices, exchange(): lax.all_to_all(chunks.reshape(DEVS * per // rows, rows, width), RC, 0, 0,...  4.61 us
  transfers between devices with their start and end apart: 2, of which 1 were waited for; matrix products, arithmetic and copies ran while one was open for 0% of the time, Pallas kernels for 0%

profile of v6, /device:TPU:0, one launch (start us, length us, event | category | flops | bytes accessed | tf_op | source)
XLA Modules:
  0.0 112.4 jit_solution(2452247003766251188)
XLA Ops:
  0.6 1.9 %shard_map.272 = bf16[8,128,256]{2,1,0:T(8,128)(2,1)} custom-call(bf16[2,128,256]{2,1,0:T(8,128)(2,1)} %estimate_ref.1, bf16[2,128,256]{2,1,0:T(8,128)(2,1)} %dirty_ref.1, bf16[2,128,256]{2,1,0:T(8,128)(2,1)} %cot_ref.1), custom_call_target="tpu_custom_call" | custom-call | flops 2000000000 | bytes 2000000 | tf_op jit(solution)/shard_map/pallas_call | solution.py:637
  2.5 0.0 copy-start.4
  2.6 0.0 copy-start.16
  2.6 16.6 %all_to_all.30.strip_ref = bf16[8,128,256]{2,1,0:T(8,128)(2,1)S(1)} all-to-all(bf16[8,128,256]{2,1,0:T(8,128)(2,1)} %shard_map.272), channel_id=1, replica_groups=mesh['row'=16,'col'=8] {'col'}, dimensions={0} | all-to-all | bytes 1048576 | tf_op jit(solution)/shard_map/all_to_all | solution.py:688
  19.1 0.0 copy-done.4
  19.1 0.0 copy-done.16
  19.1 0.0 copy-start.10
  19.1 0.0 copy-start.13
  19.1 0.0 copy-start.14
  19.2 0.0 copy-start.15
  19.2 0.0 copy-start.17
  19.2 0.4 shard_map.273
  19.5 0.0 copy-start
  19.6 0.0 copy-start.8
  19.6 18.6 %all_to_all.31 = bf16[128,8,128]{2,1,0:T(8,128)(2,1)S(1)} all-to-all(bf16[128,8,128]{2,1,0:T(8,128)(2,1)S(1)} %bitcast.25), channel_id=1, replica_groups=mesh['row'=16,'col'=8] {'row','col'}, dimensions={0} | all-to-all | bytes 524288 | tf_op jit(solution)/shard_map/all_to_all | solution.py:659
  38.2 0.0 copy-done.10
  38.2 0.0 copy-done.13
  38.2 0.0 copy-done.14
  38.2 0.0 copy-done.15
  38.2 0.0 copy-done.17
  38.2 0.0 copy-done
  38.2 0.0 copy-done.8
  38.2 2.9 %shard_map.274 = bf16[1024,256]{1,0:T(8,128)(2,1)} custom-call(bf16[1024,128]{1,0:T(8,128)(2,1)S(1)} %bitcast.24, f32[3,16,16,128]{3,2,1,0:T(8,128)S(1)} %copy-done, bf16[128,128]{1,0:T(8,128)(2,1)S(1)} %copy-done.14, bf16[128,128]{1,0:T(8,128)(2,1)S(1)} %copy-done.13, bf16[128,256]{1,0:T(8,128)(2,1)S(1)} %copy-done.10, bf16[128,512]{1,0:T(8,128)(2,1)S(1)} %copy-done.8, ...), custom_call_target="tpu_custom_call" | custom-call | flops 2000000000 | bytes 2000000 | tf_op jit(solution)/shard_map/pallas_call | solution.py:637
  41.1 4.6 %all-to-all-start.2 = ((bf16[128,8,256]{2,1,0:T(8,128)(2,1)}), bf16[128,8,256]{2,1,0:T(8,128)(2,1)S(1)}, u32[]{:S(2)}, u32[]{:S(2)}) async-start(bf16[128,8,256]{2,1,0:T(8,128)(2,1)} %bitcast.3), calls=%async_computation.2 | async-start | bytes 1048576 | tf_op jit(solution)/shard_map/all_to_all | solution.py:659
  45.7 0.0 copy-start.6
  45.8 0.0 copy-start.7
  45.8 0.0 copy-start.12
  45.8 0.0 copy-start.18
  45.8 0.1 broadcast_select_fusion
  45.9 0.0 copy-start.1
  45.9 0.8 collective-permute-start
  46.7 0.0 copy-start.2
  46.8 0.0 collective-permute-done.beyond_ref
  46.8 12.8 %all-to-all-done.2 = bf16[128,8,256]{2,1,0:T(8,128)(2,1)S(1)} async-done(((bf16[128,8,256]{2,1,0:T(8,128)(2,1)}), bf16[128,8,256]{2,1,0:T(8,128)(2,1)S(1)}, u32[]{:S(2)}, u32[]{:S(2)}) %all-to-all-start.2) | async-done | bytes 524320 | tf_op jit(solution)/shard_map/all_to_all | solution.py:659
  59.5 0.0 copy-start.3
  59.5 0.0 copy-done.6
  59.5 0.0 copy-done.7
  59.5 0.0 copy-done.12
  59.5 0.0 copy-done.18
  59.5 0.0 copy-done.1
  59.6 0.0 copy-done.2
  59.6 0.6 copy-done.3
  60.2 6.2 %shard_map.275 = (f32[8,2,16,256]{3,2,1,0:T(8,128)S(1)}, bf16[1280,128]{1,0:T(8,128)(2,1)S(1)}) custom-call(s32[1]{0:T(128)} %bitcast.place_ref, bf16[1024,256]{1,0:T(8,128)(2,1)S(1)} %bitcast.19, bf16[8,128,256]{2,1,0:T(8,128)(2,1)S(1)} %all_to_all.30.strip_ref, bf16[8,6,2,256]{3,2,1,0:T(2,128)(2,1)S(1)} %collective-permute-done.beyond_ref, ...), custom_call_target="tpu_custom_call" | custom-call | flops 8000000000 | bytes 8000000 | tf_op jit(solution)/shard_map/pallas_call | solution.py:637
  66.4 0.0 copy-start.5
  66.4 0.0 copy-start.11
  66.4 16.9 %all_to_all.32 = bf16[640,2,128]{2,1,0:T(2,128)(2,1)S(1)} all-to-all(bf16[640,2,128]{2,1,0:T(2,128)(2,1)S(1)} %bitcast.21), channel_id=1, replica_groups=mesh['row'=16,'col'=8] {'row','col'}, dimensions={0} | all-to-all | bytes 655360 | tf_op jit(solution)/shard_map/all_to_all | solution.py:659
  83.2 0.0 copy-done.5
  83.2 0.0 copy-done.11
  83.2 1.9 %shard_map.276 = bf16[1280,128]{1,0:T(8,128)(2,1)S(1)} custom-call(bf16[1280,128]{1,0:T(8,128)(2,1)S(1)} %bitcast.22, f32[3,16,16,128]{3,2,1,0:T(8,128)S(1)} %copy-done, bf16[128,128]{1,0:T(8,128)(2,1)S(1)} %copy-done.14, bf16[128,128]{1,0:T(8,128)(2,1)S(1)} %copy-done.13, bf16[128,256]{1,0:T(8,128)(2,1)S(1)} %copy-done.10, bf16[128,256]{1,0:T(8,128)(2,1)S(1)} %copy-done.10, ...), custom_call_target="tpu_custom_call" | custom-call | flops 2000000000 | bytes 2000000 | tf_op jit(solution)/shard_map/pallas_call | solution.py:637
  85.2 0.0 copy-start.9
  85.2 15.8 %all_to_all.33 = bf16[640,2,128]{2,1,0:T(2,128)(2,1)S(1)} all-to-all(bf16[640,2,128]{2,1,0:T(2,128)(2,1)S(1)} %bitcast.23), channel_id=1, replica_groups=mesh['row'=16,'col'=8] {'row','col'}, dimensions={0} | all-to-all | bytes 655360 | tf_op jit(solution)/shard_map/all_to_all | solution.py:659
  100.9 0.0 copy-done.9
  100.9 1.0 shard_map.277
  102.0 9.7 %all_to_all.34 = f32[8,2,16,256]{3,2,1,0:T(8,128)S(1)} all-to-all(f32[8,2,16,256]{3,2,1,0:T(8,128)S(1)} %get-tuple-element.14), channel_id=1, replica_groups=mesh['row'=16,'col'=8] {'col'}, dimensions={0} | all-to-all | bytes 524288 | tf_op jit(solution)/shard_map/all_to_all | solution.py:748
  111.7 0.7 copy.30
  (1 shorter events, 0.0 us)
Async XLA Ops:
  2.5 16.6 %copy-start.4 = (bf16[512,512]{1,0:T(8,128)(2,1)S(1)}, bf16[512,512]{1,0:T(8,128)(2,1)}, u32[]{:S(2)}) copy-start(bf16[512,512]{1,0:T(8,128)(2,1)} %constant.44.clone.table_ref.inverse_ref.forward_ref) | copy-start | bytes 1572868
  2.6 16.6 %copy-start.16 = (f32[16,256]{1,0:T(8,128)S(1)}, f32[16,256]{1,0:T(8,128)}, u32[]{:S(2)}) copy-start(f32[16,256]{1,0:T(8,128)} %constant.43.clone.twiddle_ref) | copy-start | bytes 49156
  19.1 19.0 %copy-start.10 = (bf16[128,256]{1,0:T(8,128)(2,1)S(1)}, bf16[128,256]{1,0:T(8,128)(2,1)}, u32[]{:S(2)}) copy-start(bf16[128,256]{1,0:T(8,128)(2,1)} %constant.47.clone.refs_4_.refs_5_) | copy-start | bytes 196612
  19.1 19.0 %copy-start.13 = (bf16[128,128]{1,0:T(8,128)(2,1)S(1)}, bf16[128,128]{1,0:T(8,128)(2,1)}, u32[]{:S(2)}) copy-start(bf16[128,128]{1,0:T(8,128)(2,1)} %constant.46.clone.refs_3_) | copy-start | bytes 98308
  19.1 19.0 %copy-start.14 = (bf16[128,128]{1,0:T(8,128)(2,1)S(1)}, bf16[128,128]{1,0:T(8,128)(2,1)}, u32[]{:S(2)}) copy-start(bf16[128,128]{1,0:T(8,128)(2,1)} %constant.45.clone.refs_2_) | copy-start | bytes 98308
  19.2 19.0 %copy-start.15 = (f32[32,256]{1,0:T(8,128)S(1)}, f32[32,256]{1,0:T(8,128)}, u32[]{:S(2)}) copy-start(f32[32,256]{1,0:T(8,128)} %constant.50.clone.refs_7_) | copy-start | bytes 98308
  19.2 19.0 %copy-start.17 = (f32[32,128]{1,0:T(8,128)S(1)}, f32[32,128]{1,0:T(8,128)}, u32[]{:S(2)}) copy-start(f32[32,128]{1,0:T(8,128)} %constant.49.clone.refs_6_.refs_7_) | copy-start | bytes 49156
  19.5 18.7 %copy-start = (f32[3,16,16,128]{3,2,1,0:T(8,128)S(1)}, f32[3,16,16,128]{3,2,1,0:T(8,128)}, u32[]{:S(2)}) copy-start(f32[3,16,16,128]{3,2,1,0:T(8,128)} %refs_1_.3) | copy-start | bytes 1179652
  19.6 18.7 %copy-start.8 = (bf16[128,512]{1,0:T(8,128)(2,1)S(1)}, bf16[128,512]{1,0:T(8,128)(2,1)}, u32[]{:S(2)}) copy-start(bf16[128,512]{1,0:T(8,128)(2,1)} %constant.48.clone.refs_5_) | copy-start | bytes 393220
  41.1 18.4 %all-to-all-start.2 = ((bf16[128,8,256]{2,1,0:T(8,128)(2,1)}), bf16[128,8,256]{2,1,0:T(8,128)(2,1)S(1)}, u32[]{:S(2)}, u32[]{:S(2)}) async-start(bf16[128,8,256]{2,1,0:T(8,128)(2,1)} %bitcast.3), calls=%async_computation.2 | async-start | bytes 1048576 | tf_op jit(solution)/shard_map/all_to_all | solution.py:659
  45.7 13.8 %copy-start.6 = (bf16[1280,64]{1,0:T(8,128)(2,1)S(1)}, bf16[1280,64]{1,0:T(8,128)(2,1)}, u32[]{:S(2)}) copy-start(bf16[1280,64]{1,0:T(8,128)(2,1)} %constant.52.clone.spread_ref) | copy-start | bytes 491524
  45.8 13.8 %copy-start.7 = (bf16[3,384,128]{2,1,0:T(8,128)(2,1)S(1)}, bf16[3,384,128]{2,1,0:T(8,128)(2,1)}, u32[]{:S(2)}) copy-start(bf16[3,384,128]{2,1,0:T(8,128)(2,1)} %constant.54.clone.fold_ref) | copy-start | bytes 884740
  45.8 13.7 %copy-start.12 = (f32[4,4,640]{2,1,0:T(4,128)S(1)}, f32[4,4,640]{2,1,0:T(4,128)}, u32[]{:S(2)}) copy-start(f32[4,4,640]{2,1,0:T(4,128)} %constant.51.clone.band_ref) | copy-start | bytes 122884
  45.8 13.7 %copy-start.18 = (s32[8,256]{1,0:T(8,128)S(1)}, s32[8,256]{1,0:T(8,128)}, u32[]{:S(2)}) copy-start(s32[8,256]{1,0:T(8,128)} %constant.53.clone.rows_ref) | copy-start | bytes 24580
  45.9 13.6 %copy-start.1 = (bf16[32,4,3,3]{0,1,3,2:T(4,128)(2,1)S(1)}, bf16[32,4,3,3]{0,1,3,2:T(4,128)(2,1)}, u32[]{:S(2)}) copy-start(bf16[32,4,3,3]{0,1,3,2:T(4,128)(2,1)} %param.28) | copy-start | bytes 6916
  45.9 0.8 collective-permute-start
  46.7 12.8 %copy-start.2 = (bf16[2,32,3,3]{1,0,3,2:T(2,128)(2,1)S(1)}, bf16[2,32,3,3]{1,0,3,2:T(2,128)(2,1)}, u32[]{:S(2)}) copy-start(bf16[2,32,3,3]{1,0,3,2:T(2,128)(2,1)} %param.30) | copy-start | bytes 3460
  59.5 0.7 copy-start.3
  66.4 16.9 %copy-start.5 = (bf16[1280,32]{1,0:T(8,128)(2,1)S(1)}, bf16[1280,32]{1,0:T(8,128)(2,1)}, u32[]{:S(2)}) copy-start(bf16[1280,32]{1,0:T(8,128)(2,1)} %constant.56.clone.refs_9_) | copy-start | bytes 245764
  66.4 16.9 %copy-start.11 = (bf16[16,1280]{1,0:T(8,128)(2,1)S(1)}, bf16[16,1280]{1,0:T(8,128)(2,1)}, u32[]{:S(2)}) copy-start(bf16[16,1280]{1,0:T(8,128)(2,1)} %constant.55.clone.refs_8_) | copy-start | bytes 122884
  85.2 15.8 %copy-start.9 = (bf16[32,1280]{1,0:T(8,128)(2,1)S(1)}, bf16[32,1280]{1,0:T(8,128)(2,1)}, u32[]{:S(2)}) copy-start(bf16[32,1280]{1,0:T(8,128)(2,1)} %constant.57.clone.collect_ref) | copy-start | bytes 245764

commit v7 on v6

--- a/solution.py
+++ b/solution.py
@@ -660,11 +660,11 @@
     return moved.reshape(DEVS * per, width)
 
 
-def middle(chunks, spectra, window, lead, per, after=()):
+def middle(chunks, spectra, window, lead, per, early=()):
     ahead, back = row_block_tables()
     twiddle, row_table = row_forward_tables()
     back_twiddle, back_row = row_inverse_tables(window, lead)
-    extra = sum_tables()[1:3] if per == 10 else ()
+    extra = sum_tables()[1:3] if per == 10 else early
     return call(
         functools.partial(middle_body, window, per == 10),
         like(DEVS * per, 8 * window),
@@ -677,7 +677,6 @@
         twiddle,
         back_twiddle,
         *extra,
-        after=after,
     )
 
 
@@ -690,12 +689,13 @@
         ahead_body, like(1024, 128), strip, column_twiddle(), column_tables()[0]
     )
     spec = exchange(spec, 8)
+    bias = b_first.reshape(1, 32)
     rows = strip[:, :96].reshape(8, 6, STRIP, 256)
     edge = jnp.where(lax.axis_index("col") == 7, rows[:, :, -2:], rows[:, :, :2])
     seams = [(8 * r + 7, 8 * r + 8) for r in range(15)]
     beyond = lax.ppermute(edge, RC, seams + [(b, a) for a, b in seams])
     band, row_of, fold = weight_tables()
-    mixed = exchange(middle(spec, psf_spectra, 32, 2, 8, ()), 8)
+    mixed = exchange(middle(spec, psf_spectra, 32, 2, 8, (bias,)), 8)
     place = (lax.axis_index("row") * 8 + lax.axis_index("col")).astype(jnp.int32).reshape(1)
     base, spec = call(
         network_body,
@@ -706,7 +706,7 @@
         beyond,
         w_first.transpose(2, 3, 1, 0),
         w_second.transpose(2, 3, 0, 1),
-        b_first.reshape(1, 32),
+        bias,
         band,
         column_twiddle(),
         column_tables()[1],

time: 113 us -> 113 us (level)
  no operation moved by 1% of the time
where the time goes in v7:
time: 113 us; the launch traced here: 112 us
  blocking collectives  77.5 us (69%)
  Pallas kernels  14.3 us (13%)
  waiting for transfers between devices  12.8 us (11%)
  starting transfers between devices  5.4 us (5%)
  local copies, waits for them, and re-layouts  1.46 us (1%)
    all_to_all x3, blocking collectives, exchange(): lax.all_to_all(chunks.reshape(DEVS * per // rows, rows, width), RC, 0, 0,...  51.2 us
    all_to_all x1, blocking collectives, shards(): strip = lax.all_to_all(cells, 'col', 0, 0, tiled=True)  16.6 us
    pallas_call x6, Pallas kernels, call(): pl.pallas_call(body, out_shape=outs, in_specs=[pl.BlockSpec(memory_space=...  14.3 us
    all_to_all x1, waiting for transfers between devices, exchange(): lax.all_to_all(chunks.reshape(DEVS * per // rows, rows, width), RC, 0, 0,...  12.8 us
    all_to_all x1, blocking collectives, shards(): image = lax.all_to_all(image, 'col', 0, 0, tiled=True)  9.68 us
    all_to_all x1, starting transfers between devices, exchange(): lax.all_to_all(chunks.reshape(DEVS * per // rows, rows, width), RC, 0, 0,...  4.61 us
  transfers between devices with their start and end apart: 2, of which 1 were waited for; matrix products, arithmetic and copies ran while one was open for 0% of the time, Pallas kernels for 0%

profile of v7, /device:TPU:0, one launch (start us, length us, event | category | flops | bytes accessed | tf_op | source)
XLA Modules:
  0.0 112.4 jit_solution(5681725518010472830)
XLA Ops:
  0.6 1.9 %shard_map.272 = bf16[8,128,256]{2,1,0:T(8,128)(2,1)} custom-call(bf16[2,128,256]{2,1,0:T(8,128)(2,1)} %estimate_ref.1, bf16[2,128,256]{2,1,0:T(8,128)(2,1)} %dirty_ref.1, bf16[2,128,256]{2,1,0:T(8,128)(2,1)} %cot_ref.1), custom_call_target="tpu_custom_call" | custom-call | flops 2000000000 | bytes 2000000 | tf_op jit(solution)/shard_map/pallas_call | solution.py:637
  2.5 0.0 copy-start.4
  2.6 0.0 copy-start.16
  2.6 16.6 %all_to_all.30.strip_ref = bf16[8,128,256]{2,1,0:T(8,128)(2,1)S(1)} all-to-all(bf16[8,128,256]{2,1,0:T(8,128)(2,1)} %shard_map.272), channel_id=1, replica_groups=mesh['row'=16,'col'=8] {'col'}, dimensions={0} | all-to-all | bytes 1048576 | tf_op jit(solution)/shard_map/all_to_all | solution.py:687
  19.1 0.0 copy-done.4
  19.1 0.0 copy-done.16
  19.1 0.0 copy-start.10
  19.1 0.0 copy-start.13
  19.1 0.0 copy-start.14
  19.2 0.0 copy-start.15
  19.2 0.0 copy-start.17
  19.2 0.4 shard_map.273
  19.5 0.0 copy-start
  19.6 0.0 copy-start.8
  19.6 18.6 %all_to_all.31 = bf16[128,8,128]{2,1,0:T(8,128)(2,1)S(1)} all-to-all(bf16[128,8,128]{2,1,0:T(8,128)(2,1)S(1)} %bitcast.25), channel_id=1, replica_groups=mesh['row'=16,'col'=8] {'row','col'}, dimensions={0} | all-to-all | bytes 524288 | tf_op jit(solution)/shard_map/all_to_all | solution.py:659
  38.2 0.0 copy-start.3
  38.2 0.0 copy-done.10
  38.2 0.0 copy-done.13
  38.2 0.0 copy-done.14
  38.2 0.0 copy-done.15
  38.2 0.0 copy-done.17
  38.2 0.0 copy-done
  38.2 0.0 copy-done.8
  38.2 0.6 copy-done.3
  38.8 2.9 %shard_map.274 = bf16[1024,256]{1,0:T(8,128)(2,1)} custom-call(bf16[1024,128]{1,0:T(8,128)(2,1)S(1)} %bitcast.24, f32[3,16,16,128]{3,2,1,0:T(8,128)S(1)} %copy-done, bf16[128,128]{1,0:T(8,128)(2,1)S(1)} %copy-done.14, bf16[128,128]{1,0:T(8,128)(2,1)S(1)} %copy-done.13, bf16[128,256]{1,0:T(8,128)(2,1)S(1)} %copy-done.10, bf16[128,512]{1,0:T(8,128)(2,1)S(1)} %copy-done.8, ...), custom_call_target="tpu_custom_call" | custom-call | flops 2000000000 | bytes 2000000 | tf_op jit(solution)/shard_map/pallas_call | solution.py:637
  41.7 4.6 %all-to-all-start.2 = ((bf16[128,8,256]{2,1,0:T(8,128)(2,1)}), bf16[128,8,256]{2,1,0:T(8,128)(2,1)S(1)}, u32[]{:S(2)}, u32[]{:S(2)}) async-start(bf16[128,8,256]{2,1,0:T(8,128)(2,1)} %bitcast.4), calls=%async_computation.2 | async-start | bytes 1048576 | tf_op jit(solution)/shard_map/all_to_all | solution.py:659
  46.3 0.0 copy-start.6
  46.4 0.0 copy-start.7
  46.4 0.0 copy-start.12
  46.4 0.0 copy-start.18
  46.4 0.1 broadcast_select_fusion
  46.5 0.0 copy-start.1
  46.5 0.8 collective-permute-start
  47.3 0.0 copy-start.2
  47.4 0.0 collective-permute-done.beyond_ref
  47.4 12.8 %all-to-all-done.2 = bf16[128,8,256]{2,1,0:T(8,128)(2,1)S(1)} async-done(((bf16[128,8,256]{2,1,0:T(8,128)(2,1)}), bf16[128,8,256]{2,1,0:T(8,128)(2,1)S(1)}, u32[]{:S(2)}, u32[]{:S(2)}) %all-to-all-start.2) | async-done | bytes 524320 | tf_op jit(solution)/shard_map/all_to_all | solution.py:659
  60.1 0.0 copy-done.6
  60.1 0.0 copy-done.7
  60.1 0.0 copy-done.12
  60.1 0.0 copy-done.18
  60.1 0.0 copy-done.1
  60.2 0.0 copy-done.2
  60.2 6.2 %shard_map.275 = (f32[8,2,16,256]{3,2,1,0:T(8,128)S(1)}, bf16[1280,128]{1,0:T(8,128)(2,1)S(1)}) custom-call(s32[1]{0:T(128)} %bitcast.place_ref, bf16[1024,256]{1,0:T(8,128)(2,1)S(1)} %bitcast.19, bf16[8,128,256]{2,1,0:T(8,128)(2,1)S(1)} %all_to_all.30.strip_ref, bf16[8,6,2,256]{3,2,1,0:T(2,128)(2,1)S(1)} %collective-permute-done.beyond_ref, ...), custom_call_target="tpu_custom_call" | custom-call | flops 8000000000 | bytes 8000000 | tf_op jit(solution)/shard_map/pallas_call | solution.py:637
  66.4 0.0 copy-start.5
  66.4 0.0 copy-start.11
  66.4 16.9 %all_to_all.32 = bf16[640,2,128]{2,1,0:T(2,128)(2,1)S(1)} all-to-all(bf16[640,2,128]{2,1,0:T(2,128)(2,1)S(1)} %bitcast.21), channel_id=1, replica_groups=mesh['row'=16,'col'=8] {'row','col'}, dimensions={0} | all-to-all | bytes 655360 | tf_op jit(solution)/shard_map/all_to_all | solution.py:659
  83.2 0.0 copy-done.5
  83.2 0.0 copy-done.11
  83.2 1.9 %shard_map.276 = bf16[1280,128]{1,0:T(8,128)(2,1)S(1)} custom-call(bf16[1280,128]{1,0:T(8,128)(2,1)S(1)} %bitcast.22, f32[3,16,16,128]{3,2,1,0:T(8,128)S(1)} %copy-done, bf16[128,128]{1,0:T(8,128)(2,1)S(1)} %copy-done.14, bf16[128,128]{1,0:T(8,128)(2,1)S(1)} %copy-done.13, bf16[128,256]{1,0:T(8,128)(2,1)S(1)} %copy-done.10, bf16[128,256]{1,0:T(8,128)(2,1)S(1)} %copy-done.10, ...), custom_call_target="tpu_custom_call" | custom-call | flops 2000000000 | bytes 2000000 | tf_op jit(solution)/shard_map/pallas_call | solution.py:637
  85.2 0.0 copy-start.9
  85.2 15.8 %all_to_all.33 = bf16[640,2,128]{2,1,0:T(2,128)(2,1)S(1)} all-to-all(bf16[640,2,128]{2,1,0:T(2,128)(2,1)S(1)} %bitcast.23), channel_id=1, replica_groups=mesh['row'=16,'col'=8] {'row','col'}, dimensions={0} | all-to-all | bytes 655360 | tf_op jit(solution)/shard_map/all_to_all | solution.py:659
  100.9 0.0 copy-done.9
  100.9 1.0 shard_map.277
  102.0 9.7 %all_to_all.34 = f32[8,2,16,256]{3,2,1,0:T(8,128)S(1)} all-to-all(f32[8,2,16,256]{3,2,1,0:T(8,128)S(1)} %get-tuple-element.14), channel_id=1, replica_groups=mesh['row'=16,'col'=8] {'col'}, dimensions={0} | all-to-all | bytes 524288 | tf_op jit(solution)/shard_map/all_to_all | solution.py:748
  111.7 0.7 copy.30
  (1 shorter events, 0.0 us)
Async XLA Ops:
  2.5 16.6 %copy-start.4 = (bf16[512,512]{1,0:T(8,128)(2,1)S(1)}, bf16[512,512]{1,0:T(8,128)(2,1)}, u32[]{:S(2)}) copy-start(bf16[512,512]{1,0:T(8,128)(2,1)} %constant.44.clone.table_ref.inverse_ref.forward_ref) | copy-start | bytes 1572868
  2.6 16.6 %copy-start.16 = (f32[16,256]{1,0:T(8,128)S(1)}, f32[16,256]{1,0:T(8,128)}, u32[]{:S(2)}) copy-start(f32[16,256]{1,0:T(8,128)} %constant.43.clone.twiddle_ref) | copy-start | bytes 49156
  19.1 19.0 %copy-start.10 = (bf16[128,256]{1,0:T(8,128)(2,1)S(1)}, bf16[128,256]{1,0:T(8,128)(2,1)}, u32[]{:S(2)}) copy-start(bf16[128,256]{1,0:T(8,128)(2,1)} %constant.47.clone.refs_4_.refs_5_) | copy-start | bytes 196612
  19.1 19.0 %copy-start.13 = (bf16[128,128]{1,0:T(8,128)(2,1)S(1)}, bf16[128,128]{1,0:T(8,128)(2,1)}, u32[]{:S(2)}) copy-start(bf16[128,128]{1,0:T(8,128)(2,1)} %constant.46.clone.refs_3_) | copy-start | bytes 98308
  19.1 19.0 %copy-start.14 = (bf16[128,128]{1,0:T(8,128)(2,1)S(1)}, bf16[128,128]{1,0:T(8,128)(2,1)}, u32[]{:S(2)}) copy-start(bf16[128,128]{1,0:T(8,128)(2,1)} %constant.45.clone.refs_2_) | copy-start | bytes 98308
  19.2 19.0 %copy-start.15 = (f32[32,256]{1,0:T(8,128)S(1)}, f32[32,256]{1,0:T(8,128)}, u32[]{:S(2)}) copy-start(f32[32,256]{1,0:T(8,128)} %constant.50.clone.refs_7_) | copy-start | bytes 98308
  19.2 19.0 %copy-start.17 = (f32[32,128]{1,0:T(8,128)S(1)}, f32[32,128]{1,0:T(8,128)}, u32[]{:S(2)}) copy-start(f32[32,128]{1,0:T(8,128)} %constant.49.clone.refs_6_.refs_7_) | copy-start | bytes 49156
  19.5 18.7 %copy-start = (f32[3,16,16,128]{3,2,1,0:T(8,128)S(1)}, f32[3,16,16,128]{3,2,1,0:T(8,128)}, u32[]{:S(2)}) copy-start(f32[3,16,16,128]{3,2,1,0:T(8,128)} %refs_1_.3) | copy-start | bytes 1179652
  19.6 18.7 %copy-start.8 = (bf16[128,512]{1,0:T(8,128)(2,1)S(1)}, bf16[128,512]{1,0:T(8,128)(2,1)}, u32[]{:S(2)}) copy-start(bf16[128,512]{1,0:T(8,128)(2,1)} %constant.48.clone.refs_5_) | copy-start | bytes 393220
  38.2 0.7 copy-start.3
  41.7 18.4 %all-to-all-start.2 = ((bf16[128,8,256]{2,1,0:T(8,128)(2,1)}), bf16[128,8,256]{2,1,0:T(8,128)(2,1)S(1)}, u32[]{:S(2)}, u32[]{:S(2)}) async-start(bf16[128,8,256]{2,1,0:T(8,128)(2,1)} %bitcast.4), calls=%async_computation.2 | async-start | bytes 1048576 | tf_op jit(solution)/shard_map/all_to_all | solution.py:659
  46.3 13.8 %copy-start.6 = (bf16[1280,64]{1,0:T(8,128)(2,1)S(1)}, bf16[1280,64]{1,0:T(8,128)(2,1)}, u32[]{:S(2)}) copy-start(bf16[1280,64]{1,0:T(8,128)(2,1)} %constant.52.clone.spread_ref) | copy-start | bytes 491524
  46.4 13.8 %copy-start.7 = (bf16[3,384,128]{2,1,0:T(8,128)(2,1)S(1)}, bf16[3,384,128]{2,1,0:T(8,128)(2,1)}, u32[]{:S(2)}) copy-start(bf16[3,384,128]{2,1,0:T(8,128)(2,1)} %constant.54.clone.fold_ref) | copy-start | bytes 884740
  46.4 13.7 %copy-start.12 = (f32[4,4,640]{2,1,0:T(4,128)S(1)}, f32[4,4,640]{2,1,0:T(4,128)}, u32[]{:S(2)}) copy-start(f32[4,4,640]{2,1,0:T(4,128)} %constant.51.clone.band_ref) | copy-start | bytes 122884
  46.4 13.7 %copy-start.18 = (s32[8,256]{1,0:T(8,128)S(1)}, s32[8,256]{1,0:T(8,128)}, u32[]{:S(2)}) copy-start(s32[8,256]{1,0:T(8,128)} %constant.53.clone.rows_ref) | copy-start | bytes 24580
  46.5 13.6 %copy-start.1 = (bf16[32,4,3,3]{0,1,3,2:T(4,128)(2,1)S(1)}, bf16[32,4,3,3]{0,1,3,2:T(4,128)(2,1)}, u32[]{:S(2)}) copy-start(bf16[32,4,3,3]{0,1,3,2:T(4,128)(2,1)} %param.28) | copy-start | bytes 6916
  46.5 0.8 collective-permute-start
  47.3 12.8 %copy-start.2 = (bf16[2,32,3,3]{1,0,3,2:T(2,128)(2,1)S(1)}, bf16[2,32,3,3]{1,0,3,2:T(2,128)(2,1)}, u32[]{:S(2)}) copy-start(bf16[2,32,3,3]{1,0,3,2:T(2,128)(2,1)} %param.30) | copy-start | bytes 3460
  66.4 16.9 %copy-start.5 = (bf16[1280,32]{1,0:T(8,128)(2,1)S(1)}, bf16[1280,32]{1,0:T(8,128)(2,1)}, u32[]{:S(2)}) copy-start(bf16[1280,32]{1,0:T(8,128)(2,1)} %constant.56.clone.refs_9_) | copy-start | bytes 245764
  66.4 16.9 %copy-start.11 = (bf16[16,1280]{1,0:T(8,128)(2,1)S(1)}, bf16[16,1280]{1,0:T(8,128)(2,1)}, u32[]{:S(2)}) copy-start(bf16[16,1280]{1,0:T(8,128)(2,1)} %constant.55.clone.refs_8_) | copy-start | bytes 122884
  85.2 15.8 %copy-start.9 = (bf16[32,1280]{1,0:T(8,128)(2,1)S(1)}, bf16[32,1280]{1,0:T(8,128)(2,1)}, u32[]{:S(2)}) copy-start(bf16[32,1280]{1,0:T(8,128)(2,1)} %constant.57.clone.collect_ref) | copy-start | bytes 245764
